TPU v7x, 512 devices: a whole 4x4x16 slice. The times are simulated.
512 devices in a mesh: tm: 64 (over z_lo, y, core), dp: 8 (over x, z_hi).
Axes of the slice: x: 4, y: 4, z: 16 (z_hi: 2, z_lo: 8; z = z_hi * 8 + z_lo), core: 2. Of those that a mesh axis runs over, the one named last changes fastest.
Arguments:
- latent: bfloat16 [8, 128, 4, 8, 384], P('dp', 'tm'), may hold values from -6 to 6
- frame_pos: int32 [8, 128], P('dp', 'tm'), may hold values from 0 to 127, as said below
- w_short: bfloat16 [384, 192], replicated, may hold values from -0.3125 to 0.3125
- gain: float32 [192], replicated, may hold values from 0.1 to 1.9
- w_conv: bfloat16 [3, 3, 3, 192, 192], replicated, may hold values from -0.078125 to 0.078125
- cotangent: bfloat16 [8, 128, 8, 16, 192], P('dp', 'tm'), may hold values from -16 to 16
Outputs:
- decoded: bfloat16 [8, 128, 8, 16, 192], P('dp', 'tm')
- grad_latent: bfloat16 [8, 128, 4, 8, 384], P('dp', 'tm')
- grad_conv: float32 [192, 5184], P('dp')
- grad_short: float32 [384, 192], replicated
- grad_gain: float32 [192], replicated
Inputs may be any that keep to these rules, and one draw needn't show every extreme that they name: frame_pos is 0 at the first frame of a clip and rises by one per frame within a clip; the first frame of every group starts a clip.
All inputs are finite; a program needn't handle non-finite values.
Results may differ from a plain program's by a relative error of at most 0.015.
Values may be sent and summed in bfloat16 or wider, within the bound.
No kernel may reach another device: no remote copies, remote signals or barrier semaphores. Data moves between devices by JAX's collectives and lax.ppermute only.
A program may use at most 64 MiB of HBM per device.

v0:
```python
import jax
import jax.numpy as jnp
from jax import lax
from jax.sharding import PartitionSpec as P

EPS = 1e-06


def shifted(x, axis, by):
    devices = lax.axis_size(axis)
    pairs = [(i, i + by) for i in range(devices) if 0 <= i + by < devices]
    return lax.ppermute(x, axis, pairs)


def enlarge(value):
    return jnp.repeat(jnp.repeat(value, 2, axis=1), 2, axis=2)


def pool_sum(value):
    frames, rows, cols, width = value.shape
    return value.reshape(frames, rows // 2, 2, cols // 2, 2, width).sum(axis=(2, 4))


def plane_conv(inputs, kernel):
    return lax.conv_general_dilated(
        inputs,
        kernel,
        (1, 1),
        ((1, 1), (1, 1)),
        dimension_numbers=("NHWC", "HWIO", "NHWC"),
        preferred_element_type=jnp.float32,
    )


def adjoint_conv(grad, kernel):
    return plane_conv(grad, jnp.transpose(kernel[::-1, ::-1], (0, 1, 3, 2)))


def patches_of(frames):
    rows, cols = (frames.shape[1], frames.shape[2])
    padded = jnp.pad(frames, ((0, 0), (1, 1), (1, 1), (0, 0)))
    return jnp.concatenate(
        [padded[:, a : a + rows, b : b + cols, :] for a in range(3) for b in range(3)], axis=-1
    )


def on_device(latent, frame_pos, w_short, gain, w_conv, cotangent):
    inputs = latent[0]
    pos = frame_pos[0]
    grad_out = cotangent[0]
    frames, rows, cols, c_in = inputs.shape
    width = w_short.shape[1]
    s_val = jnp.dot(inputs.reshape(-1, c_in), w_short, preferred_element_type=jnp.float32).reshape(
        frames, rows, cols, width
    )
    scale = lax.rsqrt(jnp.mean(s_val * s_val, axis=-1, keepdims=True) + EPS)
    normed = s_val * scale
    z_val = normed * gain
    sig = jax.nn.sigmoid(z_val)
    act = (z_val * sig).astype(jnp.bfloat16)
    before = shifted(act, "tm", 1)
    extended = enlarge(jnp.concatenate([before, act], axis=0))
    masks = [(pos >= 2 - k)[:, None, None, None] for k in range(3)]
    output = enlarge(s_val)
    for k in range(3):
        output = output + jnp.where(masks[k], plane_conv(extended[k : k + frames], w_conv[k]), 0.0)
    decoded = output.astype(jnp.bfloat16)[None]
    grad_up = jnp.zeros((frames + 2, 2 * rows, 2 * cols, width), jnp.float32)
    pieces = []
    for k in range(3):
        masked = grad_out * masks[k].astype(jnp.bfloat16)
        grad_up = grad_up.at[k : k + frames].add(adjoint_conv(masked, w_conv[k]))
        pieces.append(patches_of(extended[k : k + frames]) * masks[k].astype(jnp.bfloat16))
    own_grad = grad_up[2:]
    first_one = (pos[0] >= 1).astype(jnp.bfloat16)
    first_two = (pos[0] >= 2).astype(jnp.bfloat16)
    second_two = (pos[1] >= 2).astype(jnp.bfloat16)
    package = jnp.stack(
        [grad_out[0] * first_one, grad_out[0] * first_two, grad_out[1] * second_two]
    )
    arrived = shifted(package, "tm", -1)
    extra_early = adjoint_conv(arrived[1:2], w_conv[0])
    extra_late = adjoint_conv(arrived[0:1], w_conv[1]) + adjoint_conv(arrived[2:3], w_conv[0])
    own_grad = own_grad.at[frames - 2 :].add(jnp.concatenate([extra_early, extra_late], axis=0))
    grad_act = pool_sum(own_grad)
    dz_val = grad_act * sig * (1.0 + z_val * (1.0 - sig))
    gain_term = jnp.sum(dz_val * normed, axis=(0, 1, 2))
    dn_val = dz_val * gain
    ds_val = scale * (
        dn_val - normed * jnp.mean(dn_val * normed, axis=-1, keepdims=True)
    ) + pool_sum(grad_out.astype(jnp.float32))
    ds_flat = ds_val.astype(jnp.bfloat16).reshape(-1, width)
    grad_latent = (
        lax.dot_general(
            ds_flat, w_short, (((1,), (1,)), ((), ())), preferred_element_type=jnp.float32
        )
        .astype(jnp.bfloat16)
        .reshape(inputs.shape)[None]
    )
    short_term = lax.dot_general(
        inputs.reshape(-1, c_in),
        ds_flat,
        (((0,), (0,)), ((), ())),
        preferred_element_type=jnp.float32,
    )
    table = jnp.concatenate(pieces, axis=-1).reshape(-1, 27 * width)
    flat_grad = grad_out.reshape(-1, width)
    full_term = lax.dot_general(
        flat_grad, table, (((0,), (0,)), ((), ())), preferred_element_type=jnp.float32
    )
    partial_rows = lax.psum_scatter(full_term, "tm", scatter_dimension=0, tiled=True)
    partial_rows = lax.psum(partial_rows.astype(jnp.bfloat16), "dp").astype(jnp.float32)
    gathered = lax.all_gather(partial_rows.astype(jnp.bfloat16), "tm", axis=0, tiled=True).astype(
        partial_rows.dtype
    )
    share = width // lax.axis_size("dp")
    grad_conv = lax.dynamic_slice_in_dim(gathered, lax.axis_index("dp") * share, share, 0)
    grad_short, grad_gain = lax.psum((short_term, gain_term), ("tm", "dp"))
    return (decoded, grad_latent, grad_conv, grad_short, grad_gain)


def solution(mesh):
    return jax.shard_map(
        on_device,
        mesh=mesh,
        in_specs=(
            P("dp", "tm", None, None, None),
            P("dp", "tm"),
            P(),
            P(),
            P(),
            P("dp", "tm", None, None, None),
        ),
        out_specs=(
            P("dp", "tm", None, None, None),
            P("dp", "tm", None, None, None),
            P("dp", None),
            P(),
            P(),
        ),
        check_vma=False,
    )
```

profile of v0, /device:TPU:1, one launch (start us, length us, event | category | flops | bytes accessed | tf_op | source)
XLA Modules:
  0.0 1162.0 jit_solution(2514336918715997477)
XLA Ops:
  8.1 0.9 copy.116
  9.0 1.3 fusion.99
  12.4 8.8 collective-permute-start.1
  21.2 1.3 fusion.97
  22.4 1.1 reshape.390
  23.5 1.0 fusion.79
  24.6 1.8 convolution_select_fusion
  26.4 0.2 copy.122
  26.8 1.8 convolution_select_fusion.2
  28.6 0.2 copy.118
  28.9 0.2 reduce_sum.48
  29.2 1.8 convolution_select_fusion.1
  31.1 0.2 copy.120
  31.4 0.1 mul.201
  31.5 0.1 mul.205
  31.7 0.1 mul.209
  31.8 0.3 multiply_reduce_fusion.2
  32.2 1.3 dynamic-slice.28
  34.3 1.7 convolution_select_fusion.6
  36.1 0.4 fusion.3
  36.7 0.4 convolution_select_fusion.8
  37.3 0.1 reshape.321
  37.4 0.2 reduce_sum.46
  37.7 0.7 multiply_reduce_fusion
  38.4 0.7 add_convert_fusion
  39.1 1.9 collective-permute-start
  41.1 0.1 pad_slice_fusion
  41.4 0.1 concatenate.110
  41.7 0.5 concatenate.115
  42.2 1.1 broadcast_multiply_fusion
  43.4 0.1 pad_slice_fusion.16
  43.7 0.1 concatenate.90
  44.0 0.1 pad_slice_fusion.8
  44.3 0.1 concatenate.100
  44.5 0.7 copy.147
  45.2 0.7 copy.148
  45.9 0.7 copy.149
  46.5 0.5 concatenate.95
  47.1 1.1 broadcast_multiply_fusion.2
  48.1 1.4 concatenate.105
  49.5 1.1 broadcast_multiply_fusion.1
  50.6 4.3 concatenate.116
  54.9 2.6 convolution_bitcast_fusion
  57.5 460.9 %all-reduce.9 = bf16[192,5184]{1,0:T(8,128)(2,1)S(1)} all-reduce(f32[192,5184]{1,0:T(8,128)} %convolution_bitcast_fusion), channel_id=2, replica_groups=mesh['tm'=64,'dp'=8] {'tm'}, use_global_device_ids=true, to_apply=%region_4.5.clone | all-reduce | flops 995328 | bytes 5971968
  518.4 68.9 %psum.21 = bf16[3,5184]{1,0:T(4,128)(2,1)} all-reduce(bf16[3,5184]{1,0:T(4,128)(2,1)S(1)} %dynamic-slice_convert_fusion), channel_id=1, replica_groups=mesh['tm'=64,'dp'=8] {'dp'}, use_global_device_ids=true, to_apply=%region_5.6 | all-reduce | flops 15552 | bytes 62208 | tf_op jit(solution)/shard_map/psum | solution.py:112
  587.5 0.1 reshape.319
  587.7 0.1 broadcast.214
  587.8 1.7 fusion
  589.6 0.2 copy.115
  589.8 112.8 %psum.23 = f32[192]{0:T(256)} all-reduce(f32[192]{0:T(256)S(1)} %copy-done.6), channel_id=1, replica_groups=mesh['tm'=64,'dp'=8] {'tm','dp'}, use_global_device_ids=true, to_apply=%region_8.9 | all-reduce | flops 192 | bytes 1536 | tf_op jit(solution)/shard_map/psum | solution.py:118
  702.6 0.8 convolution_convert_fusion
  703.4 0.9 convolution_bitcast_fusion.1
  704.5 0.1 broadcast.211
  704.6 1.7 fusion.1
  706.3 0.2 copy.111
  706.7 0.1 broadcast.207
  706.8 1.7 fusion.2
  708.5 0.2 copy.107
  708.9 0.7 copy.158
  709.6 5.1 all-gather.3.cloned.1.call-done
  714.7 4.9 reshape.424
  719.6 1.8 constant_dynamic-slice_fusion
  721.4 431.4 %all-reduce.8.cloned.1.call-done = f32[384,192]{0,1:T(8,128)} async-done(((f32[384,192]{0,1:T(8,128)}), f32[384,192]{0,1:T(8,128)}) %all-reduce.8.cloned.1.call-update) | async-done | bytes 294928 | tf_op jit(solution)/shard_map/psum | solution.py:118
  1152.9 1.7 copy.206
  (115 shorter events, 2.6 us)
Async XLA Ops:
  8.0 23.8 %copy-start = (bf16[384,192]{0,1:T(8,128)(2,1)S(1)}, bf16[384,192]{0,1:T(8,128)(2,1)}, u32[]{:S(2)}) copy-start(bf16[384,192]{0,1:T(8,128)(2,1)} %param.18) | copy-start | bytes 442372
  8.0 16.6 %copy-start.11 = (pred[16,3]{0,1:T(4,128)(4,1)S(1)}, pred[16,3]{0,1:T(4,128)(4,1)}, u32[]{:S(2)}) copy-start(pred[16,3]{0,1:T(4,128)(4,1)} %constant.196) | copy-start | bytes 148
  8.0 706.6 %all-gather.3.cloned.1.call-start = ((), (), s32[]{:S(2)}) async-start(), calls=%async_computation.1 | async-start | bytes 2728960 | tf_op jit(solution)/shard_map/all_gather | solution.py:113
  12.4 21.7 %collective-permute-start.1 = (bf16[3,8,16,192]{3,1,2,0:T(8,128)(2,1)S(1)}, bf16[3,8,16,192]{3,1,2,0:T(8,128)(2,1)S(1)}, u32[]{:S(2)}, u32[]{:S(2)}) collective-permute-start(bf16[3,8,16,192]{3,1,2,0:T(8,128)(2,1)S(1)} %pad_maximum_fusion), channel_id=1, source_target_pairs={{8,0},{16,8},{24,16},{32,24},{40,32},{48,40},{56,48},{64,56},{72,6... | collective-permute-start | bytes 442376 | tf_op jit(solution)/shard_map/ppermute | solution.py:12
  29.1 2.7 copy-start.3
  29.2 5.1 copy-start.13
  34.1 2.0 copy-start.10
  36.6 1.1 copy-start.5
  39.1 4.2 collective-permute-start
  50.6 4.3 copy-start.1
  57.5 530.2 %copy-start.9 = (pred[2]{0:T(512)(128)(4,1)S(1)}, pred[2]{0:T(512)(128)(4,1)}, u32[]{:S(2)}) copy-start(pred[2]{0:T(512)(128)(4,1)} %get-tuple-element.118) | copy-start | bytes 10
  57.5 530.3 %copy-start.12 = (pred[16,3]{0,1:T(4,128)(4,1)S(1)}, pred[16,3]{0,1:T(4,128)(4,1)}, u32[]{:S(2)}) copy-start(pred[16,3]{0,1:T(4,128)(4,1)} %constant.196) | copy-start | bytes 148
  587.3 565.5 %all-reduce.8.cloned.1.call-start = ((), (), s32[]{:S(2)}) async-start(), calls=%async_computation | async-start | bytes 589824 | tf_op jit(solution)/shard_map/psum | solution.py:118
  587.6 2.2 copy-start.6
  587.6 115.0 %copy-start.2 = (bf16[2,4,8,192]{3,2,1,0:T(8,128)(2,1)S(1)}, bf16[2,4,8,192]{3,2,1,0:T(8,128)(2,1)}, u32[]{:S(2)}) copy-start(bf16[2,4,8,192]{3,2,1,0:T(8,128)(2,1)} %get-tuple-element.111) | copy-start | bytes 73732
  587.7 115.7 %copy-start.4 = (bf16[1,2,4,8,384]{4,3,2,1,0:T(8,128)(2,1)S(1)}, bf16[1,2,4,8,384]{4,3,2,1,0:T(8,128)(2,1)}, u32[]{:S(2)}) copy-start(bf16[1,2,4,8,384]{4,3,2,1,0:T(8,128)(2,1)} %param.16) | copy-start | bytes 147460
  587.8 116.7 %copy-start.8 = (pred[2]{0:T(512)(128)(4,1)S(1)}, pred[2]{0:T(512)(128)(4,1)}, u32[]{:S(2)}) copy-start(pred[2]{0:T(512)(128)(4,1)} %get-tuple-element.119) | copy-start | bytes 10
  704.6 2.1 copy-start.7
Sparse Core Ops, SparseCore 0:
  587.4 127.1 all-gather.2
Sparse Core Ops, SparseCore 1:
  704.5 448.3 all-reduce.7
where the time goes:
time: 1160 us
  blocking collectives  643 us (55%)
  waiting for transfers between devices  437 us (38%)
  local copies, waits for them, and re-layouts  27.2 us (2%)
  between operations  19.1 us (2%)
  matrix products  17.9 us (2%)
    unnamed x1, blocking collectives  461 us
    psum x1, waiting for transfers between devices, on_device(): grad_short, grad_gain = lax.psum((short_term, gain_term), ('tm', 'dp'))  431 us
    psum x1, blocking collectives, on_device(): grad_short, grad_gain = lax.psum((short_term, gain_term), ('tm', 'dp'))  113 us
    psum x1, blocking collectives, on_device(): lax.psum(partial_rows.astype(jnp.bfloat16), 'dp').astype(jnp.float32)  68.9 us
  transfers between devices with their start and end apart: 4, of which 2 were waited for; matrix products, arithmetic and copies ran while one was open for 3% of the time, Pallas kernels for 0%

commit v1 on v0

v1 whole, which is shorter than its diff:
```python
import functools

import jax
import jax.numpy as jnp
import numpy as np
from jax import lax
from jax.experimental import pallas as pl
from jax.experimental.pallas import tpu as pltpu
from jax.sharding import Mesh, PartitionSpec as P

EPS = 1e-06
C_IN = 384
C = 192
CELLS = 32
FINE = 128
TAPS = 27
CONV_ROWS = 256
SHORT_ROWS = 80
MSG = CONV_ROWS + SHORT_ROWS
BF16 = jnp.bfloat16
F32 = jnp.float32


def pool_matrix(frames):
    out = np.zeros((frames, 8, 16, 3, 3, frames, 4, 8), np.float32)
    for t in range(frames):
        for a in range(3):
            for b in range(3):
                for p in range(8):
                    for q in range(16):
                        row, col = p + a - 1, q + b - 1
                        if 0 <= row < 8 and 0 <= col < 16:
                            out[t, p, q, a, b, t, row // 2, col // 2] = 1
    return out.reshape(frames * FINE, 9 * frames * CELLS)


def dot(a, b):
    return jnp.dot(a, b, preferred_element_type=F32)


def features(inputs, w_short, gain):
    s_val = dot(inputs, w_short)
    scale = lax.rsqrt(jnp.mean(s_val * s_val, axis=-1, keepdims=True) + EPS)
    normed = s_val * scale
    z_val = normed * gain
    sig = 1.0 / (1.0 + jnp.exp(-z_val))
    return s_val, scale, normed, z_val, sig, (z_val * sig).astype(BF16)


def grad_kernel(
    core_ref, pos_ref, lat_ref, w_short_ref, gain_ref, cot_ref, next_ref, w_conv_ref, pool_ref,
    keep_ref, send_ref, s_ref, act_ref, ds_ref,
    msg, ct, sems,
):
    lat = lat_ref[...]
    gain = gain_ref[...]
    s_val, scale, normed, z_val, sig, act = features(lat, w_short_ref[...], gain)
    s_ref[...] = s_val
    act_ref[...] = act
    follows = (pos_ref[1] >= 1).astype(F32)

    fine = jnp.concatenate([cot_ref[...], next_ref[...]], axis=0)
    fine_t = jnp.transpose(fine)
    pooled = None
    for ab in range(9):
        part = dot(fine_t, pool_ref[:, ab * 128 : (ab + 1) * 128])
        if ab == 4:
            pooled = jnp.transpose(part)[: 2 * CELLS]
        ct[ab] = part.astype(BF16)

    turned = []
    for k in range(3):
        acc = dot(w_conv_ref[9 * k], ct[0])
        for ab in range(1, 9):
            acc = acc + dot(w_conv_ref[9 * k + ab], ct[ab])
        turned.append(jnp.transpose(acc))
    early = turned[2][:32] + follows * (turned[1][32:64] + turned[0][64:96])
    late = turned[2][32:64] + turned[1][64:96] + turned[0][96:]
    grad_act = jnp.concatenate([early, late], axis=0)
    dz_val = grad_act * sig * (1.0 + z_val * (1.0 - sig))
    gain_term = jnp.sum(dz_val * normed, axis=0, keepdims=True)
    dn_val = dz_val * gain
    ds_val = scale * (dn_val - normed * jnp.mean(dn_val * normed, axis=-1, keepdims=True)) + pooled
    ds_flat = ds_val.astype(BF16)
    ds_ref[...] = ds_flat

    act0 = (act[:CELLS].astype(F32) * follows).astype(BF16)
    act1 = act[CELLS:]
    none = jnp.zeros((CELLS, C), BF16)
    rows = [[none, none, act0, act1], [none, act0, act1, none], [act[:CELLS], act1, none, none]]
    gap = jnp.zeros((4 * CELLS, 64), BF16)
    stacked = [jnp.concatenate(r, axis=0) for r in rows]
    first = [jnp.concatenate([v, gap], axis=1) for v in stacked]
    second = [jnp.concatenate([gap, v], axis=1) for v in stacked]

    def place(tile_pair, index):
        for d in range(8):
            x, zh = d // 2, d % 2
            block = jnp.concatenate([t[24 * d : 24 * d + 24] for t in tile_pair], axis=0).astype(BF16)
            for i in range(3):
                q = 3 * index + i
                c, y, zl = q // 32, (q // 8) % 4, q % 8
                row = zh * 128 + zl * 16
                msg[c, 4 * x + y, row : row + 16] = block[16 * i : 16 * i + 16]

    waiting = []
    index = 0
    for n in range(0, TAPS, 2):
        even = dot(ct[n % 9], first[n // 9])
        waiting.append(even[:, :128])
        if n + 1 < TAPS:
            odd = dot(ct[(n + 1) % 9], second[(n + 1) // 9])
            waiting.append(even[:, 128:] + odd[:, :128])
            waiting.append(odd[:, 128:])
        else:
            waiting.append(even[:, 128:])
        while len(waiting) >= 2:
            place(waiting[:2], index)
            waiting = waiting[2:]
            index += 1
    place([waiting[0], jnp.zeros((C, 128), F32)], index)
    for d in range(8):
        x, zh = d // 2, d % 2
        row = zh * 128 + 7 * 16
        msg[1, 4 * x + 3, row : row + 16] = jnp.zeros((16, 128), BF16)

    short = dot(jnp.transpose(lat), ds_flat)
    tail = jnp.concatenate([short[:192, 128:], short[192:, 128:]], axis=1)
    last = jnp.concatenate(
        [gain_term[:, :128], jnp.concatenate([gain_term[:, 128:], jnp.zeros((1, 64), F32)], axis=1),
         jnp.zeros((14, 128), F32)], axis=0)
    flat = jnp.concatenate([short[:, :128], tail, last, jnp.zeros((48, 128), F32)], axis=0).astype(BF16)
    for i in range(40):
        c, y, z5 = i // 20, (i // 5) % 4, i % 5
        row = CONV_ROWS + 16 * z5
        for x in range(4):
            msg[c, 4 * x + y, row : row + 16] = flat[16 * i : 16 * i + 16]

    core = core_ref[0]
    out = pltpu.make_async_copy(msg.at[1 - core], send_ref, sems.at[0])
    own = pltpu.make_async_copy(msg.at[core], keep_ref, sems.at[1])
    out.start()
    own.start()
    out.wait()
    own.wait()


def forward_kernel(
    pos_ref, before_ref, w_short_ref, gain_ref, s_ref, act_ref, ds_ref, w_conv_ref, spread_ref,
    decoded_ref, grad_latent_ref, z_all,
):
    w_short = w_short_ref[...]
    grad_latent_ref[...] = lax.dot_general(
        ds_ref[...], w_short, (((1,), (1,)), ((), ())), preferred_element_type=F32
    ).astype(BF16)
    prev = features(before_ref[...], w_short, gain_ref[...])[-1].astype(F32)
    act = act_ref[...]
    valid = [[(pos_ref[t] >= 2 - k).astype(F32) for k in range(2)] for t in range(2)]
    taps = [
        jnp.concatenate([prev[:CELLS] * valid[0][0], prev[CELLS:] * valid[1][0]], axis=0).astype(BF16),
        jnp.concatenate([prev[CELLS:] * valid[0][1], act[:CELLS].astype(F32) * valid[1][1]], axis=0).astype(BF16),
        act,
    ]
    for ab in range(9):
        acc = dot(taps[0], w_conv_ref[ab]) + dot(taps[1], w_conv_ref[9 + ab]) + dot(taps[2], w_conv_ref[18 + ab])
        if ab == 4:
            acc = acc + s_ref[...]
        z_all[64 * ab : 64 * ab + 64] = acc.astype(BF16)
    decoded_ref[...] = dot(spread_ref[...], z_all[...]).astype(BF16)


def shape(*dims, dtype=BF16):
    return jax.ShapeDtypeStruct(dims, dtype)


def on_device(latent, frame_pos, w_short, gain, w_conv, cotangent):
    pos = frame_pos[0]
    lat = latent.reshape(2 * CELLS, C_IN)
    cot = cotangent.reshape(2 * FINE, C)
    gain2 = gain.reshape(1, C)
    w27 = w_conv.reshape(TAPS, C, C)
    smem = pl.BlockSpec(memory_space=pltpu.SMEM)
    vmem = pl.BlockSpec(memory_space=pltpu.VMEM)
    any_space = pl.BlockSpec(memory_space=pl.ANY)
    params = pltpu.CompilerParams(vmem_limit_bytes=40 * 1024 * 1024)

    tm = ("zl", "y", "c")
    keep0 = (pos[0] >= 1).astype(BF16)
    keep1 = (pos[1] >= 2).astype(BF16)
    weight = jnp.concatenate([jnp.full((FINE, 1), keep0), jnp.full((FINE, 1), keep1)], axis=0)
    following = lax.ppermute(cot * weight, tm, [(i + 1, i) for i in range(63)])
    before = lax.ppermute(lat, tm, [(i, i + 1) for i in range(63)])

    pool = jnp.asarray(pool_matrix(4), BF16)
    spread = jnp.asarray(pool_matrix(2), BF16)
    core = lax.axis_index("c").astype(jnp.int32).reshape(1)
    keep, send, s_val, act, ds_flat = pl.pallas_call(
        grad_kernel,
        out_shape=[
            shape(16, MSG, 128), shape(16, MSG, 128), shape(2 * CELLS, C, dtype=F32),
            shape(2 * CELLS, C), shape(2 * CELLS, C),
        ],
        in_specs=[smem, smem] + [vmem] * 7,
        out_specs=[any_space, any_space, vmem, vmem, vmem],
        scratch_shapes=[
            pltpu.VMEM((2, 16, MSG, 128), BF16),
            pltpu.VMEM((9, C, 128), BF16),
            pltpu.SemaphoreType.DMA((2,)),
        ],
        compiler_params=params,
        name="grad_kernel",
    )(core, pos, lat, w_short, gain2, cot, following, w27, pool)

    other = lax.ppermute(send, "c", [(0, 1), (1, 0)])
    decoded, grad_latent = pl.pallas_call(
        forward_kernel,
        out_shape=[shape(2 * FINE, C), shape(2 * CELLS, C_IN)],
        in_specs=[smem] + [vmem] * 8,
        out_specs=[vmem, vmem],
        scratch_shapes=[pltpu.VMEM((9 * 2 * CELLS, C), BF16)],
        compiler_params=params,
        name="forward_kernel",
    )(pos, before, w_short, gain2, s_val, act, ds_flat, w27, spread)

    half = (keep.astype(F32) + other.astype(F32)).astype(BF16)
    got = lax.all_to_all(half, ("x", "y"), 0, 0)
    part = jnp.sum(got.astype(F32), axis=0).astype(BF16)
    conv = part[:CONV_ROWS].reshape(2, 8, 16, 128)
    rest = jnp.pad(part[CONV_ROWS:].reshape(5, 16, 128), ((0, 3), (0, 0), (0, 0)))
    both = jnp.concatenate([conv, jnp.broadcast_to(rest, (2, 8, 16, 128))], axis=2).reshape(16, 32, 128)
    got = lax.all_to_all(both, ("zh", "zl"), 0, 0)
    whole = jnp.sum(got.astype(F32), axis=0).astype(BF16)
    got = lax.all_to_all(jnp.broadcast_to(whole, (8, 32, 128)), "zl", 0, 0)
    got = lax.all_to_all(jnp.broadcast_to(got, (8, 8, 32, 128)), ("c", "y"), 0, 0)
    flat = got[:, :, :16].reshape(1024, 128)[:984].reshape(41, 24, 128)
    grad_conv = jnp.transpose(flat, (1, 0, 2)).reshape(24, 41 * 128)[:, : TAPS * C].astype(F32)
    small = got[:, :5, 16:].reshape(640, 128).astype(F32)
    grad_short = jnp.concatenate(
        [small[:384], jnp.concatenate([small[384:576, :64], small[384:576, 64:]], axis=0)], axis=1
    )
    grad_gain = small[576:578].reshape(256)[:C]
    return (
        decoded.reshape(cotangent.shape),
        grad_latent.reshape(latent.shape),
        grad_conv,
        grad_short,
        grad_gain,
    )


def solution(mesh):
    fine = Mesh(mesh.devices.reshape(8, 4, 2, 4, 2), ("zl", "y", "c", "x", "zh"))
    tm, dp = ("zl", "y", "c"), ("x", "zh")
    return jax.shard_map(
        on_device,
        mesh=fine,
        in_specs=(
            P(dp, tm, None, None, None),
            P(dp, tm),
            P(),
            P(),
            P(),
            P(dp, tm, None, None, None),
        ),
        out_specs=(
            P(dp, tm, None, None, None),
            P(dp, tm, None, None, None),
            P(dp, None),
            P(),
            P(),
        ),
        check_vma=False,
    )
```

time: 1160 us -> 119 us (0.10)
  blocking collectives: 643 us -> 65.9 us
  waiting for transfers between devices: 437 us -> 6.44 us
  matrix products: 17.9 us -> 0 us
  between operations: 19.1 us -> 2.17 us
  local copies, waits for them, and re-layouts: 27.2 us -> 12.9 us
  starting transfers between devices: 10.8 us -> 22.7 us
    unnamed x1 -> x0, blocking collectives: 461 us -> none
    psum x1 -> x0, waiting for transfers between devices: 431 us -> none  [on_device(): grad_short, grad_gain = lax.psum((short_term, gain_term), ('tm', 'dp'))]
    psum x2 -> x0, blocking collectives: 182 us -> none  [the longest x1 113 us: on_device(): grad_short, grad_gain = lax.psum((short_term, gain_term), ('tm', 'dp'))]
    all_to_all x0 -> x3, blocking collectives: none -> 65.9 us  [the longest x1 26.8 us: on_device(): got = lax.all_to_all(both, ('zh', 'zl'), 0, 0)]
    conv_general_dilated x9 -> x0, matrix products: 13.2 us -> none  [plane_conv(): lax.conv_general_dilated(inputs, kernel, (1, 1), ((1, 1), (1, 1)), dimens...]
  transfers between devices with their start and end apart: 4 -> 4, of which waited for: 2 -> 3; matrix products, arithmetic and copies ran while one was open for 3% -> 1% of each run, Pallas kernels for 0% -> 2%
where the time goes in v1:
time: 119 us; the launch traced here: 118 us
  blocking collectives  65.9 us (55%)
  starting transfers between devices  22.7 us (19%)
  local copies, waits for them, and re-layouts  12.9 us (11%)
  waiting for transfers between devices  6.44 us (5%)
  Pallas kernels  5.46 us (5%)
  other arithmetic  2.47 us (2%)
  between operations  2.17 us (2%)
    all_to_all x1, blocking collectives, on_device(): got = lax.all_to_all(both, ('zh', 'zl'), 0, 0)  26.8 us
    all_to_all x1, blocking collectives, on_device(): got = lax.all_to_all(half, ('x', 'y'), 0, 0)  25.2 us
    all_to_all x1, blocking collectives, on_device(): got = lax.all_to_all(jnp.broadcast_to(whole, (8, 32, 128)), 'zl', 0, 0)  13.9 us
    ppermute x1, starting transfers between devices, on_device(): following = lax.ppermute(cot * weight, tm, [(i + 1, i) for i in range(63)])  8.79 us
    all_to_all x1, starting transfers between devices, on_device(): lax.all_to_all(jnp.broadcast_to(got, (8, 8, 32, 128)), ('c', 'y'), 0, 0)  8.27 us
    unnamed x24, local copies, waits for them, and re-layouts  7.99 us
    ppermute x1, starting transfers between devices, on_device(): before = lax.ppermute(lat, tm, [(i, i + 1) for i in range(63)])  3.51 us
    ppermute x1, waiting for transfers between devices, on_device(): before = lax.ppermute(lat, tm, [(i, i + 1) for i in range(63)])  3.39 us
  transfers between devices with their start and end apart: 4, of which 3 were waited for; matrix products, arithmetic and copies ran while one was open for 1% of the time, Pallas kernels for 2%

profile of v1, /device:TPU:1, one launch (start us, length us, event | category | flops | bytes accessed | tf_op | source)
XLA Modules:
  0.0 118.0 jit_solution(17717791472473905782)
XLA Ops:
  0.6 1.3 %fusion.1 = (s32[1,1]{1,0:T(1,128)}, s32[1,1]{1,0:T(1,128)}) fusion(s32[1,2]{1,0:T(1,128)} %param.9), kind=kLoop, calls=%fused_computation.9 | loop fusion | bytes 16 | tf_op jit(solution)/shard_map/slice | solution.py:189
  3.3 1.0 broadcast_multiply_fusion
  4.3 8.8 %collective-permute-start.1 = (bf16[256,192]{1,0:T(8,128)(2,1)S(1)}, bf16[256,192]{1,0:T(8,128)(2,1)S(1)}, u32[]{:S(2)}, u32[]{:S(2)}) collective-permute-start(bf16[256,192]{1,0:T(8,128)(2,1)S(1)} %broadcast_multiply_fusion), channel_id=1, source_target_pairs={{8,0},{16,8},{24,16},{32,24},{40,32},{48,40},{56,48},{64,56},{72,6... | collective-permute-start | bytes 294920 | tf_op jit(solution)/shard_map/ppermute | solution.py:191
  13.1 1.0 copy.20.w_short_ref
  14.1 0.0 collective-permute-done.1.next_ref
  14.2 0.0 copy-start
  14.2 1.7 %copy-done = bf16[3,3,3,192,192]{4,3,2,1,0:T(8,128)(2,1)S(1)} copy-done((bf16[3,3,3,192,192]{4,3,2,1,0:T(8,128)(2,1)S(1)}, bf16[3,3,3,192,192]{4,3,2,1,0:T(8,128)(2,1)}, u32[]{:S(2)}) %copy-start) | copy-done | bytes 1990680
  15.9 0.0 copy-start.2
  15.9 1.3 %copy-done.2 = bf16[512,1152]{1,0:T(8,128)(2,1)S(1)} copy-done((bf16[512,1152]{1,0:T(8,128)(2,1)S(1)}, bf16[512,1152]{1,0:T(8,128)(2,1)}, u32[]{:S(2)}) %copy-start.2) | copy-done | bytes 1179672
  17.2 0.0 copy-start.3
  17.2 0.9 copy-done.3
  18.1 0.0 copy-start.5
  18.1 0.8 copy-done.5
  18.9 0.0 copy-start.7
  18.9 0.7 copy-done.7
  19.5 0.0 copy-start.9
  19.5 0.7 copy-done.9
  20.2 3.1 %grad_kernel.1 = (bf16[16,336,128]{2,1,0:T(8,128)(2,1)S(1)}, bf16[16,336,128]{2,1,0:T(8,128)(2,1)S(1)}, f32[64,192]{1,0:T(8,128)S(1)}, bf16[64,192]{1,0:T(8,128)(2,1)S(1)}, bf16[64,192]{1,0:T(8,128)(2,1)S(1)}) custom-call(s32[1]{0:T(128)} %bitcast.3.core_ref, s32[2]{0:T(128)S(1)} %bitcast.33, bf16[64,384]{1,0:T(8,128)(2,1)S(1)} %bitcast.31, ...), custom_call_target="tpu_custom_call" | custom-call | tf_op jit(solution)/shard_map/grad_kernel/pallas_call | solution.py:197
  23.3 2.2 %collective-permute-start.2 = (bf16[16,336,128]{2,1,0:T(8,128)(2,1)S(1)}, bf16[16,336,128]{2,1,0:T(8,128)(2,1)S(1)}, u32[]{:S(2)}, u32[]{:S(2)}) collective-permute-start(bf16[16,336,128]{2,1,0:T(8,128)(2,1)S(1)} %get-tuple-element.18), channel_id=1, source_target_pairs={{0,8},{8,0},{1,9},{9,1},{2,10},{10,2},{3,11},{11,3},{4,12},{12,4},... | collective-permute-start | bytes 4128776 | tf_op jit(solution)/shard_map/ppermute | solution.py:214
  25.5 2.8 %collective-permute-done.2 = bf16[16,336,128]{2,1,0:T(8,128)(2,1)S(1)} collective-permute-done((bf16[16,336,128]{2,1,0:T(8,128)(2,1)S(1)}, bf16[16,336,128]{2,1,0:T(8,128)(2,1)S(1)}, u32[]{:S(2)}, u32[]{:S(2)}) %collective-permute-start.2) | collective-permute-done | bytes 1376288 | tf_op jit(solution)/shard_map/ppermute | solution.py:214
  28.3 0.4 add_convert_fusion
  28.7 25.2 %all_to_all.20 = bf16[16,336,128]{2,1,0:T(8,128)(2,1)S(1)} all-to-all(bf16[16,336,128]{2,1,0:T(8,128)(2,1)S(1)} %add_convert_fusion), channel_id=1, replica_groups=mesh['zl'=8,'y'=4,'c'=2,'x'=4,'zh'=2] {'x','y'}, dimensions={0} | all-to-all | bytes 2752512 | tf_op jit(solution)/shard_map/all_to_all | solution.py:226
  53.9 0.0 copy-start.4
  53.9 0.2 reduce_sum.24
  54.1 0.0 copy-start.6
  54.1 0.0 copy-start.1
  54.1 0.0 copy-start.8
  54.1 0.0 copy-start.10
  54.2 26.8 %all_to_all.21 = bf16[16,32,128]{2,1,0:T(8,128)(2,1)S(1)} all-to-all(bf16[16,32,128]{2,1,0:T(8,128)(2,1)S(1)} %pad_maximum_fusion), channel_id=1, replica_groups=mesh['zl'=8,'y'=4,'c'=2,'x'=4,'zh'=2] {'zh','zl'}, dimensions={0} | all-to-all | bytes 262144 | tf_op jit(solution)/shard_map/all_to_all | solution.py:231
  81.1 13.9 %all_to_all.22 = bf16[8,32,128]{2,1,0:T(8,128)(2,1)S(1)} all-to-all(bf16[8,32,128]{2,1,0:T(8,128)(2,1)S(1)} %broadcast_in_dim.15), channel_id=1, replica_groups=mesh['zl'=8,'y'=4,'c'=2,'x'=4,'zh'=2] {'zl'}, dimensions={0} | all-to-all | bytes 131072 | tf_op jit(solution)/shard_map/all_to_all | solution.py:233
  94.9 0.9 broadcast_in_dim.16
  95.8 8.3 %all-to-all-start.3 = ((bf16[8,8,32,128]{3,2,1,0:T(8,128)(2,1)}), bf16[8,8,32,128]{3,2,1,0:T(8,128)(2,1)}, u32[]{:S(2)}, u32[]{:S(2)}) async-start(bf16[8,8,32,128]{3,2,1,0:T(8,128)(2,1)} %broadcast_in_dim.16), calls=%async_computation.3 | async-start | bytes 1048576 | tf_op jit(solution)/shard_map/all_to_all | solution.py:234
  104.1 0.0 copy-done.6
  104.1 3.5 %collective-permute-start = (bf16[64,384]{1,0:T(8,128)(2,1)S(1)}, bf16[64,384]{1,0:T(8,128)(2,1)S(1)}, u32[]{:S(2)}, u32[]{:S(2)}) collective-permute-start(bf16[64,384]{1,0:T(8,128)(2,1)S(1)} %bitcast.32), channel_id=1, source_target_pairs={{0,8},{8,16},{16,24},{24,32},{32,40},{40,48},{48,56},{56,64},{64,7... | collective-permute-start | bytes 147464 | tf_op jit(solution)/shard_map/ppermute | solution.py:192
  107.6 3.4 %collective-permute-done.before_ref = bf16[64,384]{1,0:T(8,128)(2,1)S(1)} collective-permute-done((bf16[64,384]{1,0:T(8,128)(2,1)S(1)}, bf16[64,384]{1,0:T(8,128)(2,1)S(1)}, u32[]{:S(2)}, u32[]{:S(2)}) %collective-permute-start) | collective-permute-done | bytes 49184 | tf_op jit(solution)/shard_map/ppermute | solution.py:192
  111.0 0.0 copy-done.4
  111.0 0.0 copy-done.1
  111.0 0.0 copy-done.8
  111.0 0.0 copy-done.10
  111.0 2.4 %forward_kernel.1 = (bf16[256,192]{1,0:T(8,128)(2,1)}, bf16[64,384]{1,0:T(8,128)(2,1)}) custom-call(s32[2]{0:T(128)S(1)} %bitcast.34, bf16[64,384]{1,0:T(8,128)(2,1)S(1)} %collective-permute-done.before_ref, bf16[384,192]{1,0:T(8,128)(2,1)S(1)} %copy.20.w_short_ref, f32[1,192]{1,0:T(1,128)S(1)} %bitcast.36, f32[64,192]{1,0:T(8,128)S(1)} %get-tuple-element.12.s_ref, ...), custom_call_target="tpu_custom_call" | custom-call | tf_op jit(solution)/shard_map/forward_kernel/pallas_call | solution.py:215
  113.4 0.2 all-to-all-done.3
  113.6 0.9 slice.59
  114.5 0.6 slice_bitcast_fusion
  115.1 0.1 fusion
  115.2 1.0 slice.56
  116.3 0.9 copy.22
  117.2 0.8 slice_convert_fusion
  (14 shorter events, 0.2 us)
Async XLA Ops:
  4.3 9.9 %collective-permute-start.1 = (bf16[256,192]{1,0:T(8,128)(2,1)S(1)}, bf16[256,192]{1,0:T(8,128)(2,1)S(1)}, u32[]{:S(2)}, u32[]{:S(2)}) collective-permute-start(bf16[256,192]{1,0:T(8,128)(2,1)S(1)} %broadcast_multiply_fusion), channel_id=1, source_target_pairs={{8,0},{16,8},{24,16},{32,24},{40,32},{48,40},{56,48},{64,56},{72,6... | collective-permute-start | bytes 294920 | tf_op jit(solution)/shard_map/ppermute | solution.py:191
  14.2 1.8 %copy-start = (bf16[3,3,3,192,192]{4,3,2,1,0:T(8,128)(2,1)S(1)}, bf16[3,3,3,192,192]{4,3,2,1,0:T(8,128)(2,1)}, u32[]{:S(2)}) copy-start(bf16[3,3,3,192,192]{4,3,2,1,0:T(8,128)(2,1)} %param.12) | copy-start | bytes 5971972
  15.9 1.3 %copy-start.2 = (bf16[512,1152]{1,0:T(8,128)(2,1)S(1)}, bf16[512,1152]{1,0:T(8,128)(2,1)}, u32[]{:S(2)}) copy-start(bf16[512,1152]{1,0:T(8,128)(2,1)} %constant.22.clone.pool_ref) | copy-start | bytes 3538948
  17.2 0.9 copy-start.3
  18.1 0.8 copy-start.5
  18.9 0.7 copy-start.7
  19.5 0.7 copy-start.9
  23.3 5.0 %collective-permute-start.2 = (bf16[16,336,128]{2,1,0:T(8,128)(2,1)S(1)}, bf16[16,336,128]{2,1,0:T(8,128)(2,1)S(1)}, u32[]{:S(2)}, u32[]{:S(2)}) collective-permute-start(bf16[16,336,128]{2,1,0:T(8,128)(2,1)S(1)} %get-tuple-element.18), channel_id=1, source_target_pairs={{0,8},{8,0},{1,9},{9,1},{2,10},{10,2},{3,11},{11,3},{4,12},{12,4},... | collective-permute-start | bytes 4128776 | tf_op jit(solution)/shard_map/ppermute | solution.py:214
  53.9 57.1 %copy-start.4 = (bf16[256,576]{1,0:T(8,128)(2,1)S(1)}, bf16[256,576]{1,0:T(8,128)(2,1)}, u32[]{:S(2)}) copy-start(bf16[256,576]{1,0:T(8,128)(2,1)} %constant.23.clone.spread_ref) | copy-start | bytes 884740
  54.1 50.0 %copy-start.6 = (bf16[1,2,4,8,384]{4,3,2,1,0:T(8,128)(2,1)S(1)}, bf16[1,2,4,8,384]{4,3,2,1,0:T(8,128)(2,1)}, u32[]{:S(2)}) copy-start(bf16[1,2,4,8,384]{4,3,2,1,0:T(8,128)(2,1)} %param.8) | copy-start | bytes 147460
  54.1 56.9 %copy-start.1 = (bf16[3,3,3,192,192]{4,3,2,1,0:T(8,128)(2,1)S(1)}, bf16[3,3,3,192,192]{4,3,2,1,0:T(8,128)(2,1)}, u32[]{:S(2)}) copy-start(bf16[3,3,3,192,192]{4,3,2,1,0:T(8,128)(2,1)} %param.12) | copy-start | bytes 5971972
  54.1 56.9 %copy-start.8 = (s32[1,2]{1,0:T(1,128)S(1)}, s32[1,2]{1,0:T(1,128)}, u32[]{:S(2)}) copy-start(s32[1,2]{1,0:T(1,128)} %param.9) | copy-start | bytes 28
  54.1 56.9 %copy-start.10 = (f32[192]{0:T(256)S(1)}, f32[192]{0:T(256)}, u32[]{:S(2)}) copy-start(f32[192]{0:T(256)} %param.11) | copy-start | bytes 2308
  95.8 17.7 %all-to-all-start.3 = ((bf16[8,8,32,128]{3,2,1,0:T(8,128)(2,1)}), bf16[8,8,32,128]{3,2,1,0:T(8,128)(2,1)}, u32[]{:S(2)}, u32[]{:S(2)}) async-start(bf16[8,8,32,128]{3,2,1,0:T(8,128)(2,1)} %broadcast_in_dim.16), calls=%async_computation.3 | async-start | bytes 1048576 | tf_op jit(solution)/shard_map/all_to_all | solution.py:234
  104.1 6.9 %collective-permute-start = (bf16[64,384]{1,0:T(8,128)(2,1)S(1)}, bf16[64,384]{1,0:T(8,128)(2,1)S(1)}, u32[]{:S(2)}, u32[]{:S(2)}) collective-permute-start(bf16[64,384]{1,0:T(8,128)(2,1)S(1)} %bitcast.32), channel_id=1, source_target_pairs={{0,8},{8,16},{16,24},{24,32},{32,40},{40,48},{48,56},{56,64},{64,7... | collective-permute-start | bytes 147464 | tf_op jit(solution)/shard_map/ppermute | solution.py:192

commit v2 on v1

v2 whole, which is shorter than its diff:
```python
import jax
import jax.numpy as jnp
import numpy as np
from jax import lax
from jax.experimental import pallas as pl
from jax.experimental.pallas import tpu as pltpu
from jax.sharding import Mesh, PartitionSpec as P

EPS = 1e-06
C_IN = 384
C = 192
CELLS = 32
FINE = 128
TAPS = 27
TILES = 41
SHORT_ROWS = 80
SEND_ROWS = 192 + SHORT_ROWS
MSG = 256 + SHORT_ROWS
BF16 = jnp.bfloat16
F32 = jnp.float32


def pool_matrix(frames):
    out = np.zeros((frames, 8, 16, 3, 3, frames, 4, 8), np.float32)
    for t in range(frames):
        for a in range(3):
            for b in range(3):
                for p in range(8):
                    for q in range(16):
                        row, col = p + a - 1, q + b - 1
                        if 0 <= row < 8 and 0 <= col < 16:
                            out[t, p, q, a, b, t, row // 2, col // 2] = 1
    return out.reshape(frames * FINE, 9 * frames * CELLS)


def dot(a, b):
    return jnp.dot(a, b, preferred_element_type=F32)


def dot_nt(a, b):
    return lax.dot_general(a, b, (((1,), (1,)), ((), ())), preferred_element_type=F32)


def features(inputs, w_short_t, gain):
    s_val = dot_nt(inputs, w_short_t)
    scale = lax.rsqrt(jnp.mean(s_val * s_val, axis=-1, keepdims=True) + EPS)
    normed = s_val * scale
    z_val = normed * gain
    sig = 1.0 / (1.0 + jnp.exp(-z_val))
    return s_val, scale, normed, z_val, sig, (z_val * sig).astype(BF16)


def local_kernel(
    next_pos_ref, next_ref, pos_hbm, lat_hbm, w_short_hbm, gain_hbm, cot_hbm, pool_hbm, w_conv_hbm,
    send_ref, s_ref, act_ref, ds_ref,
    pos_ref, lat_ref, w_short_ref, gain_ref, cot_ref, pool_ref, w_conv_ref, turned_ref, ct, sems,
):
    loads = [
        pltpu.make_async_copy(source, target, sems.at[i])
        for i, (source, target) in enumerate([
            (pos_hbm, pos_ref), (lat_hbm, lat_ref), (w_short_hbm, w_short_ref), (gain_hbm, gain_ref),
            (cot_hbm, cot_ref), (pool_hbm, pool_ref), (w_conv_hbm, w_conv_ref),
        ])
    ]
    for load in loads:
        load.start()
    for load in loads[:4]:
        load.wait()
    lat = lat_ref[...]
    gain = gain_ref[...]
    s_val, scale, normed, z_val, sig, act = features(lat, w_short_ref[...], gain)
    s_ref[...] = s_val
    act_ref[...] = act
    follows = (pos_ref[0, 1] >= 1).astype(F32)
    keep0 = (next_pos_ref[0, 0] >= 1).astype(F32)
    keep1 = (next_pos_ref[0, 1] >= 2).astype(F32)

    after = next_ref[...].astype(F32)
    loads[4].wait()
    fine = jnp.concatenate([cot_ref[...].astype(F32), after[:FINE] * keep0, after[FINE:] * keep1], axis=0)
    fine_t = jnp.transpose(fine)
    for tile in range(4):
        turned_ref[tile] = fine_t[:, 128 * tile : 128 * tile + 128]
    for j in range(8):
        parts = []
        for tile in range(4):
            for r in range(3):
                parts.append(turned_ref[tile, pl.ds(8 * r + j, 8, stride=24), :])
        send_ref[j, :96] = jnp.concatenate(parts, axis=0).astype(BF16)
    tail = jnp.concatenate([act[:CELLS, 128:], act[CELLS:, 128:]], axis=1)
    packed = jnp.concatenate([act[:, :128], tail], axis=0)
    for j in range(8):
        send_ref[j, 96:192] = packed

    fine_t = fine_t.astype(BF16)
    loads[5].wait()
    pooled = None
    for ab in range(9):
        part = dot(fine_t, pool_ref[:, ab * 128 : (ab + 1) * 128])
        if ab == 4:
            pooled = jnp.transpose(part)[: 2 * CELLS]
        ct[ab] = part.astype(BF16)

    loads[6].wait()
    turned = []
    for k in range(3):
        acc = dot(w_conv_ref[9 * k], ct[0])
        for ab in range(1, 9):
            acc = acc + dot(w_conv_ref[9 * k + ab], ct[ab])
        turned.append(jnp.transpose(acc))
    early = turned[2][:32] + follows * (turned[1][32:64] + turned[0][64:96])
    late = turned[2][32:64] + turned[1][64:96] + turned[0][96:]
    grad_act = jnp.concatenate([early, late], axis=0)
    dz_val = grad_act * sig * (1.0 + z_val * (1.0 - sig))
    gain_term = jnp.sum(dz_val * normed, axis=0, keepdims=True)
    dn_val = dz_val * gain
    ds_val = scale * (dn_val - normed * jnp.mean(dn_val * normed, axis=-1, keepdims=True)) + pooled
    ds_flat = ds_val.astype(BF16)
    ds_ref[...] = ds_flat

    short_t = dot(jnp.transpose(ds_val).astype(BF16), lat)
    last = jnp.concatenate(
        [gain_term[:, :128], jnp.concatenate([gain_term[:, 128:], jnp.zeros((1, 64), F32)], axis=1),
         jnp.full((1, 128), follows), jnp.zeros((5, 128), F32)], axis=0)
    for j in range(8):
        rows = short_t[24 * j : 24 * j + 24]
        flat = jnp.concatenate([rows[:, :128], rows[:, 128:256], rows[:, 256:], last], axis=0)
        send_ref[j, 192:] = flat.astype(BF16)


def kernel_grad_kernel(got_ref, pool_hbm, out_ref, pool_ref, even_ref, odd_ref, rhs_ref, flat_ref, sem):
    load_pool = pltpu.make_async_copy(pool_hbm, pool_ref, sem)
    load_pool.start()
    none = jnp.zeros((CELLS, C), F32)
    gap = jnp.zeros((4 * CELLS, 64), F32)
    peers = []
    short = jnp.zeros((SHORT_ROWS, 128), F32)
    for p in range(8):
        block = got_ref[p, :96].astype(F32)
        peers.append(jnp.concatenate([block[24 * i : 24 * i + 24] for i in range(4)], axis=1))
        tail = got_ref[p, 160:192].astype(F32)
        act = jnp.concatenate(
            [got_ref[p, 96:160].astype(F32), jnp.concatenate([tail[:, :64], tail[:, 64:]], axis=0)], axis=1)
        extra = got_ref[p, 192:].astype(F32)
        short = short + extra
        act0, act1 = act[:CELLS], act[CELLS:]
        mine = act0 * extra[74:75, :1]
        rows = [[none, none, mine, act1], [none, mine, act1, none], [act0, act1, none, none]]
        for k in range(3):
            value = jnp.concatenate(rows[k], axis=0)
            rhs_ref[2 * k, 128 * p : 128 * p + 128] = jnp.concatenate([value, gap], axis=1).astype(BF16)
            rhs_ref[2 * k + 1, 128 * p : 128 * p + 128] = jnp.concatenate([gap, value], axis=1).astype(BF16)
    fine_t = jnp.concatenate(peers, axis=0).astype(BF16)
    load_pool.wait()
    for ab in range(9):
        part = dot(fine_t, pool_ref[:, ab * 128 : (ab + 1) * 128])
        wide = jnp.concatenate([part[24 * p : 24 * p + 24] for p in range(8)], axis=1)
        target = odd_ref if ab % 2 else even_ref
        target[24 * (ab // 2) : 24 * (ab // 2) + 24] = wide
    flat_ref[...] = jnp.zeros(flat_ref.shape, F32)
    lhs = [even_ref[...].astype(BF16), odd_ref[...].astype(BF16)]
    found = {}
    for k in range(3):
        for parity in range(2):
            value = dot(lhs[parity], rhs_ref[2 * k + (9 * k + parity) % 2])
            for i in range(5 - parity):
                found[9 * k + 2 * i + parity] = value[24 * i : 24 * i + 24]

    def place(tile, value):
        for r in range(3):
            flat_ref[pl.ds(42 * r + tile, 8, stride=128), :] = value[8 * r : 8 * r + 8]

    for n in range(0, TAPS, 2):
        tile = 3 * (n // 2)
        place(tile, found[n][:, :128])
        if n + 1 < TAPS:
            place(tile + 1, found[n][:, 128:] + found[n + 1][:, :128])
            place(tile + 2, found[n + 1][:, 128:])
        else:
            place(tile + 1, found[n][:, 128:])
    short = short.astype(BF16)
    for x in range(4):
        out_ref[x, :256] = flat_ref[256 * x : 256 * x + 256].astype(BF16)
        out_ref[x, 256:] = short


def sum_x_kernel(got_ref, out_ref):
    total = got_ref[0].astype(F32)
    for i in range(1, 4):
        total = total + got_ref[i].astype(F32)
    total = total.astype(BF16)
    for zh in range(2):
        for zl in range(8):
            row = 128 * zh + 16 * zl
            out_ref[2 * zl + zh, :16] = total[row : row + 16]
            rest = total[256 + 16 * zl : 272 + 16 * zl] if zl < 5 else jnp.zeros((16, 128), BF16)
            out_ref[2 * zl + zh, 16:] = rest


def sum_z_kernel(got_ref, out_ref):
    total = got_ref[0].astype(F32)
    for i in range(1, 16):
        total = total + got_ref[i].astype(F32)
    total = total.astype(BF16)
    for i in range(32):
        out_ref[i] = total


def assemble_kernel(got_ref, conv_ref, short_ref, gain_ref, flat_ref):
    for j in range(8):
        for zl in range(8):
            row = 128 * j + 16 * zl
            flat_ref[row : row + 16] = got_ref[8 * j + zl, :16].astype(F32)
        rest = jnp.concatenate([got_ref[8 * j + zl, 16:] for zl in range(5)], axis=0).astype(F32)
        for i in range(3):
            short_ref[24 * j : 24 * j + 24, 128 * i : 128 * i + 128] = rest[24 * i : 24 * i + 24]
        if j == 0:
            gain_ref[...] = jnp.concatenate([rest[72:73], rest[73:74, :64]], axis=1)
    for tile in range(TILES):
        wide = 128 if tile < TILES - 1 else 64
        for r in range(3):
            value = flat_ref[pl.ds(42 * r + tile, 8, stride=128), :]
            conv_ref[8 * r : 8 * r + 8, 128 * tile : 128 * tile + wide] = value[:, :wide]


def forward_kernel(
    before_ref, s_ref, act_ref, ds_ref, pos_hbm, w_short_hbm, gain_hbm, spread_hbm, w_conv_hbm,
    decoded_ref, grad_latent_ref,
    pos_ref, w_short_ref, gain_ref, spread_ref, w_conv_ref, z_all, sems,
):
    loads = [
        pltpu.make_async_copy(source, target, sems.at[i])
        for i, (source, target) in enumerate([
            (pos_hbm, pos_ref), (w_short_hbm, w_short_ref), (gain_hbm, gain_ref), (spread_hbm, spread_ref),
            (w_conv_hbm, w_conv_ref),
        ])
    ]
    for load in loads:
        load.start()
    for load in loads[:3]:
        load.wait()
    w_short = w_short_ref[...]
    grad_latent_ref[...] = dot(ds_ref[...], w_short).astype(BF16)
    prev = features(before_ref[...], w_short, gain_ref[...])[-1].astype(F32)
    act = act_ref[...]
    valid = [[(pos_ref[0, t] >= 2 - k).astype(F32) for k in range(2)] for t in range(2)]
    taps = [
        jnp.concatenate([prev[:CELLS] * valid[0][0], prev[CELLS:] * valid[1][0]], axis=0).astype(BF16),
        jnp.concatenate([prev[CELLS:] * valid[0][1], act[:CELLS].astype(F32) * valid[1][1]], axis=0).astype(BF16),
        act,
    ]
    loads[4].wait()
    for ab in range(9):
        acc = dot(taps[0], w_conv_ref[ab]) + dot(taps[1], w_conv_ref[9 + ab]) + dot(taps[2], w_conv_ref[18 + ab])
        if ab == 4:
            acc = acc + s_ref[...]
        z_all[64 * ab : 64 * ab + 64] = acc.astype(BF16)
    loads[3].wait()
    decoded_ref[...] = dot(spread_ref[...], z_all[...]).astype(BF16)


def shape(*dims, dtype=BF16):
    return jax.ShapeDtypeStruct(dims, dtype)


def in_hbm(value):
    return pltpu.with_memory_space_constraint(value, pltpu.HBM)


def call(kernel, name, outs, in_specs, scratch=()):
    return pl.pallas_call(
        kernel,
        out_shape=outs,
        in_specs=in_specs,
        out_specs=jax.tree.map(lambda _: VMEM, outs),
        scratch_shapes=list(scratch),
        compiler_params=pltpu.CompilerParams(vmem_limit_bytes=40 * 1024 * 1024),
        name=name,
    )


SMEM = pl.BlockSpec(memory_space=pltpu.SMEM)
VMEM = pl.BlockSpec(memory_space=pltpu.VMEM)
HBM = pl.BlockSpec(memory_space=pltpu.HBM)


def on_device(latent, frame_pos, w_short, gain, w_conv, cotangent):
    lat = latent.reshape(2 * CELLS, C_IN)
    cot = cotangent.reshape(2 * FINE, C)
    gain2 = gain.reshape(1, C)
    w27 = w_conv.reshape(TAPS, C, C)
    w_short_t = jnp.transpose(w_short)
    pool = jnp.asarray(pool_matrix(4), BF16)
    spread = jnp.asarray(pool_matrix(2), BF16)

    tm = ("zl", "y", "c")
    back = [(i + 1, i) for i in range(63)]
    following = lax.ppermute(cot, tm, back)
    next_pos = lax.ppermute(frame_pos, tm, back)
    before = lax.ppermute(lat, tm, [(i, i + 1) for i in range(63)])

    send, s_val, act, ds_flat = call(
        local_kernel, "local_kernel",
        [shape(8, SEND_ROWS, 128), shape(2 * CELLS, C, dtype=F32), shape(2 * CELLS, C), shape(2 * CELLS, C)],
        [SMEM, VMEM] + [HBM] * 7,
        [
            pltpu.SMEM((1, 2), jnp.int32), pltpu.VMEM((2 * CELLS, C_IN), BF16), pltpu.VMEM((C, C_IN), BF16),
            pltpu.VMEM((1, C), F32), pltpu.VMEM((2 * FINE, C), BF16), pltpu.VMEM((4 * FINE, 9 * 128), BF16),
            pltpu.VMEM((TAPS, C, C), BF16), pltpu.VMEM((4, C, 128), F32), pltpu.VMEM((9, C, 128), BF16),
            pltpu.SemaphoreType.DMA((7,)),
        ],
    )(next_pos, following, *map(in_hbm, (frame_pos, lat, w_short_t, gain2, cot, pool, w27)))
    got = lax.all_to_all(send, ("c", "y"), 0, 0)
    part = call(
        kernel_grad_kernel, "kernel_grad_kernel", shape(4, MSG, 128), [VMEM, HBM],
        [
            pltpu.VMEM((4 * FINE, 9 * 128), BF16), pltpu.VMEM((120, 1024), F32), pltpu.VMEM((96, 1024), F32),
            pltpu.VMEM((6, 1024, 256), BF16), pltpu.VMEM((1024, 128), F32), pltpu.SemaphoreType.DMA,
        ],
    )(got, in_hbm(pool))
    got = lax.all_to_all(part, "x", 0, 0)
    part = call(sum_x_kernel, "sum_x_kernel", shape(16, 32, 128), [VMEM])(got)
    got = lax.all_to_all(part, ("zl", "zh"), 0, 0)
    part = call(sum_z_kernel, "sum_z_kernel", shape(32, 32, 128), [VMEM])(got)
    got = lax.all_to_all(part, ("y", "zl"), 0, 0)
    got = lax.all_gather(got, "c", axis=0, tiled=True)
    grad_conv, grad_short_t, grad_gain = call(
        assemble_kernel, "assemble_kernel",
        [shape(24, TAPS * C, dtype=F32), shape(C, C_IN, dtype=F32), shape(1, C, dtype=F32)],
        [VMEM], [pltpu.VMEM((1024, 128), F32)],
    )(got)

    decoded, grad_latent = call(
        forward_kernel, "forward_kernel", [shape(2 * FINE, C), shape(2 * CELLS, C_IN)],
        [VMEM] * 4 + [HBM] * 5,
        [
            pltpu.SMEM((1, 2), jnp.int32), pltpu.VMEM((C, C_IN), BF16), pltpu.VMEM((1, C), F32),
            pltpu.VMEM((2 * FINE, 18 * CELLS), BF16), pltpu.VMEM((TAPS, C, C), BF16),
            pltpu.VMEM((9 * 2 * CELLS, C), BF16), pltpu.SemaphoreType.DMA((5,)),
        ],
    )(before, s_val, act, ds_flat, *map(in_hbm, (frame_pos, w_short_t, gain2, spread, w27)))
    return (
        decoded.reshape(cotangent.shape),
        grad_latent.reshape(latent.shape),
        grad_conv,
        jnp.transpose(grad_short_t),
        grad_gain.reshape(C),
    )


def solution(mesh):
    fine = Mesh(mesh.devices.reshape(8, 4, 2, 4, 2), ("zl", "y", "c", "x", "zh"))
    tm, dp = ("zl", "y", "c"), ("x", "zh")
    return jax.shard_map(
        on_device,
        mesh=fine,
        in_specs=(
            P(dp, tm, None, None, None),
            P(dp, tm),
            P(),
            P(),
            P(),
            P(dp, tm, None, None, None),
        ),
        out_specs=(
            P(dp, tm, None, None, None),
            P(dp, tm, None, None, None),
            P(dp, None),
            P(),
            P(),
        ),
        check_vma=False,
    )
```

time: 119 us -> 101 us (0.85)
  local copies, waits for them, and re-layouts: 12.9 us -> 0.01 us
  blocking collectives: 65.9 us -> 53.4 us
  Pallas kernels: 5.46 us -> 12.3 us
  waiting for transfers between devices: 6.44 us -> 12.9 us
  other arithmetic: 2.47 us -> 0 us
  between operations: 2.17 us -> 0.71 us
  starting transfers between devices: 22.7 us -> 21.4 us
    all_to_all x3, blocking collectives: 65.9 us -> 49.7 us  [the longest x1 27.7 us: on_device(): got = lax.all_to_all(part, ('zl', 'zh'), 0, 0)]
    all_to_all x1, waiting for transfers between devices: 0.2 us -> 8.65 us  [on_device(): got = lax.all_to_all(part, ('y', 'zl'), 0, 0)]
    unnamed x24 -> x2, local copies, waits for them, and re-layouts: 7.99 us -> 0.01 us
    pallas_call x2 -> x6, Pallas kernels: 5.46 us -> 12.3 us  [the longest x1 4.34 us: on_device(): call(local_kernel, 'local_kernel', [shape(8, SEND_ROWS, 128), shape(2 * C...]
    all_gather x0 -> x1, blocking collectives: none -> 3.65 us  [on_device(): got = lax.all_gather(got, 'c', axis=0, tiled=True)]
    slice x8 -> x0, local copies, waits for them, and re-layouts: 3.35 us -> none  [the longest x1 1.31 us: on_device(): keep1 = (pos[1] >= 2).astype(BF16)]
    all_to_all x1, starting transfers between devices: 8.27 us -> 5.48 us  [on_device(): got = lax.all_to_all(part, ('y', 'zl'), 0, 0)]
    ppermute x1, waiting for transfers between devices: 3.39 us -> 1.19 us  [on_device(): before = lax.ppermute(lat, tm, [(i, i + 1) for i in range(63)])]
  transfers between devices with their start and end apart: 4 -> 4, of which waited for: 3 -> 3; matrix products, arithmetic and copies ran while one was open for 1% -> 0% of each run, Pallas kernels for 2% -> 4%
where the time goes in v2:
time: 101 us
  blocking collectives  53.4 us (53%)
  starting transfers between devices  21.4 us (21%)
  waiting for transfers between devices  12.9 us (13%)
  Pallas kernels  12.3 us (12%)
    all_to_all x1, blocking collectives, on_device(): got = lax.all_to_all(part, ('zl', 'zh'), 0, 0)  27.7 us
    all_to_all x1, blocking collectives, on_device(): got = lax.all_to_all(send, ('c', 'y'), 0, 0)  11.9 us
    all_to_all x1, blocking collectives, on_device(): got = lax.all_to_all(part, 'x', 0, 0)  10.1 us
    ppermute x1, starting transfers between devices, on_device(): following = lax.ppermute(cot, tm, back)  8.79 us
    all_to_all x1, waiting for transfers between devices, on_device(): got = lax.all_to_all(part, ('y', 'zl'), 0, 0)  8.65 us
    all_to_all x1, starting transfers between devices, on_device(): got = lax.all_to_all(part, ('y', 'zl'), 0, 0)  5.48 us
    ppermute x1, starting transfers between devices, on_device(): before = lax.ppermute(lat, tm, [(i, i + 1) for i in range(63)])  5.22 us
    pallas_call x1, Pallas kernels, on_device(): call(local_kernel, 'local_kernel', [shape(8, SEND_ROWS, 128), shape(2 * C...  4.34 us
  transfers between devices with their start and end apart: 4, of which 3 were waited for; matrix products, arithmetic and copies ran while one was open for 0% of the time, Pallas kernels for 4%

profile of v2, /device:TPU:1, one launch (start us, length us, event | category | flops | bytes accessed | tf_op | source)
XLA Modules:
  0.0 100.7 jit_solution(4273824032218548911)
XLA Ops:
  0.6 8.8 %collective-permute-start.2 = (bf16[256,192]{1,0:T(8,128)(2,1)}, bf16[256,192]{1,0:T(8,128)(2,1)S(1)}, u32[]{:S(2)}, u32[]{:S(2)}) collective-permute-start(bf16[256,192]{1,0:T(8,128)(2,1)} %bitcast.13), channel_id=1, source_target_pairs={{8,0},{16,8},{24,16},{32,24},{40,32},{48,40},{56,48},{64,56},{72,6... | collective-permute-start | bytes 294920 | tf_op jit(solution)/shard_map/ppermute | solution.py:298
  9.4 1.9 %collective-permute-start.1 = (s32[1,2]{1,0:T(1,128)}, s32[1,2]{1,0:T(1,128)S(1)}, u32[]{:S(2)}, u32[]{:S(2)}) collective-permute-start(s32[1,2]{1,0:T(1,128)} %pos_hbm.3), channel_id=1, source_target_pairs={{8,0},{16,8},{24,16},{32,24},{40,32},{48,40},{56,48},{64,56},{72,6... | collective-permute-start | bytes 32 | tf_op jit(solution)/shard_map/ppermute | solution.py:299
  11.4 3.1 %collective-permute-done.1.next_pos_ref = s32[1,2]{1,0:T(1,128)S(1)} collective-permute-done((s32[1,2]{1,0:T(1,128)}, s32[1,2]{1,0:T(1,128)S(1)}, u32[]{:S(2)}, u32[]{:S(2)}) %collective-permute-start.1) | collective-permute-done | bytes 40 | tf_op jit(solution)/shard_map/ppermute | solution.py:299
  14.4 0.0 collective-permute-done.2.next_ref
  14.4 4.3 %local_kernel.1 = (bf16[8,272,128]{2,1,0:T(8,128)(2,1)S(1)}, f32[64,192]{1,0:T(8,128)S(1)}, bf16[64,192]{1,0:T(8,128)(2,1)S(1)}, bf16[64,192]{1,0:T(8,128)(2,1)S(1)}) custom-call(s32[1,2]{1,0:T(1,128)S(1)} %collective-permute-done.1.next_pos_ref, bf16[256,192]{1,0:T(8,128)(2,1)S(1)} %collective-permute-done.2.next_ref, s32[1,2]{1,0:T(1,128)} %pos_hbm.3, ...), custom_call_target="tpu_custom_call" | custom-call | tf_op jit(solution)/shard_map/local_kernel/pallas_call | solution.py:302
  18.8 0.0 copy-start
  18.8 11.9 %all_to_all.20.got_ref = bf16[8,272,128]{2,1,0:T(8,128)(2,1)S(1)} all-to-all(bf16[8,272,128]{2,1,0:T(8,128)(2,1)S(1)} %get-tuple-element.19), channel_id=1, replica_groups=mesh['zl'=8,'y'=4,'c'=2,'x'=4,'zh'=2] {'c','y'}, dimensions={0} | all-to-all | bytes 1114112 | tf_op jit(solution)/shard_map/all_to_all | solution.py:313
  30.7 2.5 %kernel_grad_kernel.1 = bf16[4,336,128]{2,1,0:T(8,128)(2,1)S(1)} custom-call(bf16[8,272,128]{2,1,0:T(8,128)(2,1)S(1)} %all_to_all.20.got_ref, bf16[512,1152]{1,0:T(8,128)(2,1)} %constant.4.clone.pool_hbm), custom_call_target="tpu_custom_call" | custom-call | tf_op jit(solution)/shard_map/kernel_grad_kernel/pallas_call | solution.py:314
  33.2 10.1 %all_to_all.21.got_ref = bf16[4,336,128]{2,1,0:T(8,128)(2,1)S(1)} all-to-all(bf16[4,336,128]{2,1,0:T(8,128)(2,1)S(1)} %kernel_grad_kernel.1), channel_id=1, replica_groups=mesh['zl'=8,'y'=4,'c'=2,'x'=4,'zh'=2] {'x'}, dimensions={0} | all-to-all | bytes 688128 | tf_op jit(solution)/shard_map/all_to_all | solution.py:321
  43.4 27.7 %all_to_all.22.got_ref = bf16[16,32,128]{2,1,0:T(8,128)(2,1)S(1)} all-to-all(bf16[16,32,128]{2,1,0:T(8,128)(2,1)S(1)} %sum_x_kernel.1), channel_id=1, replica_groups=mesh['zl'=8,'y'=4,'c'=2,'x'=4,'zh'=2] {'zl','zh'}, dimensions={0} | all-to-all | bytes 262144 | tf_op jit(solution)/shard_map/all_to_all | solution.py:323
  71.1 0.7 sum_z_kernel.1
  71.8 5.5 %all-to-all-start.3 = ((bf16[32,32,128]{2,1,0:T(8,128)(2,1)}), bf16[32,32,128]{2,1,0:T(8,128)(2,1)S(1)}, u32[]{:S(2)}, u32[]{:S(2)}) async-start(bf16[32,32,128]{2,1,0:T(8,128)(2,1)} %sum_z_kernel.1), calls=%async_computation.3 | async-start | bytes 524288 | tf_op jit(solution)/shard_map/all_to_all | solution.py:325
  77.3 0.0 copy-done
  77.3 5.2 %collective-permute-start = (bf16[64,384]{1,0:T(8,128)(2,1)S(1)}, bf16[64,384]{1,0:T(8,128)(2,1)S(1)}, u32[]{:S(2)}, u32[]{:S(2)}) collective-permute-start(bf16[64,384]{1,0:T(8,128)(2,1)S(1)} %bitcast.16), channel_id=1, source_target_pairs={{0,8},{8,16},{16,24},{24,32},{32,40},{40,48},{48,56},{56,64},{64,7... | collective-permute-start | bytes 147464 | tf_op jit(solution)/shard_map/ppermute | solution.py:300
  82.5 1.2 %collective-permute-done.before_ref = bf16[64,384]{1,0:T(8,128)(2,1)S(1)} collective-permute-done((bf16[64,384]{1,0:T(8,128)(2,1)S(1)}, bf16[64,384]{1,0:T(8,128)(2,1)S(1)}, u32[]{:S(2)}, u32[]{:S(2)}) %collective-permute-start) | collective-permute-done | bytes 49184 | tf_op jit(solution)/shard_map/ppermute | solution.py:300
  83.7 3.6 %forward_kernel.1 = (bf16[256,192]{1,0:T(8,128)(2,1)}, bf16[64,384]{1,0:T(8,128)(2,1)}) custom-call(bf16[64,384]{1,0:T(8,128)(2,1)S(1)} %collective-permute-done.before_ref, f32[64,192]{1,0:T(8,128)S(1)} %get-tuple-element.14.s_ref, bf16[64,192]{1,0:T(8,128)(2,1)S(1)} %get-tuple-element.15.act_ref, bf16[64,192]{1,0:T(8,128)(2,1)S(1)} %get-tuple-element.16.ds_ref, ...), custom_call_target="tpu_custom_call" | custom-call | tf_op jit(solution)/shard_map/forward_kernel/pallas_call | solution.py:333
  87.3 8.6 %all-to-all-done.3 = bf16[32,32,128]{2,1,0:T(8,128)(2,1)S(1)} async-done(((bf16[32,32,128]{2,1,0:T(8,128)(2,1)}), bf16[32,32,128]{2,1,0:T(8,128)(2,1)S(1)}, u32[]{:S(2)}, u32[]{:S(2)}) %all-to-all-start.3) | async-done | bytes 262176 | tf_op jit(solution)/shard_map/all_to_all | solution.py:325
  95.9 3.6 %all_gather.3.got_ref = bf16[64,32,128]{2,1,0:T(8,128)(2,1)S(1)} all-gather(bf16[32,32,128]{2,1,0:T(8,128)(2,1)S(1)} %all-to-all-done.3), channel_id=1, replica_groups=mesh['zl'=8,'y'=4,'c'=2,'x'=4,'zh'=2] {'c'}, dimensions={0}, use_global_device_ids=true | all-gather | bytes 786432 | tf_op jit(solution)/shard_map/all_gather | solution.py:326
  99.6 1.1 %assemble_kernel.1 = (f32[24,5184]{1,0:T(8,128)}, f32[192,384]{1,0:T(8,128)}, f32[1,192]{1,0:T(1,128)}) custom-call(bf16[64,32,128]{2,1,0:T(8,128)(2,1)S(1)} %all_gather.3.got_ref), custom_call_target="tpu_custom_call" | custom-call | tf_op jit(solution)/shard_map/assemble_kernel/pallas_call | solution.py:327
  (1 shorter events, 0.0 us)
Async XLA Ops:
  0.6 13.8 %collective-permute-start.2 = (bf16[256,192]{1,0:T(8,128)(2,1)}, bf16[256,192]{1,0:T(8,128)(2,1)S(1)}, u32[]{:S(2)}, u32[]{:S(2)}) collective-permute-start(bf16[256,192]{1,0:T(8,128)(2,1)} %bitcast.13), channel_id=1, source_target_pairs={{8,0},{16,8},{24,16},{32,24},{40,32},{48,40},{56,48},{64,56},{72,6... | collective-permute-start | bytes 294920 | tf_op jit(solution)/shard_map/ppermute | solution.py:298
  9.4 5.0 %collective-permute-start.1 = (s32[1,2]{1,0:T(1,128)}, s32[1,2]{1,0:T(1,128)S(1)}, u32[]{:S(2)}, u32[]{:S(2)}) collective-permute-start(s32[1,2]{1,0:T(1,128)} %pos_hbm.3), channel_id=1, source_target_pairs={{8,0},{16,8},{24,16},{32,24},{40,32},{48,40},{56,48},{64,56},{72,6... | collective-permute-start | bytes 32 | tf_op jit(solution)/shard_map/ppermute | solution.py:299
  18.8 58.5 %copy-start = (bf16[1,2,4,8,384]{4,3,2,1,0:T(8,128)(2,1)S(1)}, bf16[1,2,4,8,384]{4,3,2,1,0:T(8,128)(2,1)}, u32[]{:S(2)}) copy-start(bf16[1,2,4,8,384]{4,3,2,1,0:T(8,128)(2,1)} %param.8) | copy-start | bytes 147460
  71.8 24.1 %all-to-all-start.3 = ((bf16[32,32,128]{2,1,0:T(8,128)(2,1)}), bf16[32,32,128]{2,1,0:T(8,128)(2,1)S(1)}, u32[]{:S(2)}, u32[]{:S(2)}) async-start(bf16[32,32,128]{2,1,0:T(8,128)(2,1)} %sum_z_kernel.1), calls=%async_computation.3 | async-start | bytes 524288 | tf_op jit(solution)/shard_map/all_to_all | solution.py:325
  77.3 6.4 %collective-permute-start = (bf16[64,384]{1,0:T(8,128)(2,1)S(1)}, bf16[64,384]{1,0:T(8,128)(2,1)S(1)}, u32[]{:S(2)}, u32[]{:S(2)}) collective-permute-start(bf16[64,384]{1,0:T(8,128)(2,1)S(1)} %bitcast.16), channel_id=1, source_target_pairs={{0,8},{8,16},{16,24},{24,32},{32,40},{40,48},{48,56},{56,64},{64,7... | collective-permute-start | bytes 147464 | tf_op jit(solution)/shard_map/ppermute | solution.py:300

commit v3 on v2

--- a/solution.py
+++ b/solution.py
@@ -41,96 +41,121 @@
     return lax.dot_general(a, b, (((1,), (1,)), ((), ())), preferred_element_type=F32)
 
 
-def features(inputs, w_short_t, gain):
-    s_val = dot_nt(inputs, w_short_t)
+def activation(s_val, gain):
     scale = lax.rsqrt(jnp.mean(s_val * s_val, axis=-1, keepdims=True) + EPS)
     normed = s_val * scale
     z_val = normed * gain
-    sig = 1.0 / (1.0 + jnp.exp(-z_val))
-    return s_val, scale, normed, z_val, sig, (z_val * sig).astype(BF16)
-
-
-def local_kernel(
-    next_pos_ref, next_ref, pos_hbm, lat_hbm, w_short_hbm, gain_hbm, cot_hbm, pool_hbm, w_conv_hbm,
-    send_ref, s_ref, act_ref, ds_ref,
-    pos_ref, lat_ref, w_short_ref, gain_ref, cot_ref, pool_ref, w_conv_ref, turned_ref, ct, sems,
-):
-    loads = [
-        pltpu.make_async_copy(source, target, sems.at[i])
-        for i, (source, target) in enumerate([
-            (pos_hbm, pos_ref), (lat_hbm, lat_ref), (w_short_hbm, w_short_ref), (gain_hbm, gain_ref),
-            (cot_hbm, cot_ref), (pool_hbm, pool_ref), (w_conv_hbm, w_conv_ref),
-        ])
-    ]
+    return scale, normed, z_val, 1.0 / (1.0 + jnp.exp(-z_val))
+
+
+def features(inputs, w_short_t, gain):
+    s_val = dot_nt(inputs, w_short_t)
+    _, _, z_val, sig = activation(s_val, gain)
+    return s_val, (z_val * sig).astype(BF16)
+
+
+def start_loads(pairs, sems):
+    loads = [pltpu.make_async_copy(source, target, sems.at[i]) for i, (source, target) in enumerate(pairs)]
     for load in loads:
         load.start()
-    for load in loads[:4]:
+    return loads
+
+
+def slices_for(turned_ref, tiles, j):
+    return jnp.concatenate(
+        [turned_ref[t, pl.ds(8 * r + j, 8, stride=24), :] for t in tiles for r in range(3)], axis=0
+    ).astype(BF16)
+
+
+def ahead_kernel(pos_hbm, cot_hbm, ahead_ref, pos_ref, cot_ref, sems):
+    for load in start_loads([(pos_hbm, pos_ref), (cot_hbm, cot_ref)], sems):
         load.wait()
-    lat = lat_ref[...]
-    gain = gain_ref[...]
-    s_val, scale, normed, z_val, sig, act = features(lat, w_short_ref[...], gain)
+    keep = [(pos_ref[:, t : t + 1] >= t + 1).astype(F32) for t in range(2)]
+    for t in range(2):
+        rows = slice(FINE * t, FINE * t + FINE)
+        ahead_ref[rows] = (cot_ref[rows].astype(F32) * keep[t]).astype(BF16)
+
+
+def own_kernel(
+    lat_hbm, w_short_hbm, gain_hbm, cot_hbm, pos_hbm, pool_hbm, w_conv_hbm,
+    send_ref, s_ref, act_ref, ct_ref, pooled_ref, pool_ref, w_conv_ref, lat_ref, gain_ref, pos_ref,
+    w_short_ref, cot_ref, turned_ref, sems,
+):
+    loads = start_loads([
+        (lat_hbm, lat_ref), (w_short_hbm, w_short_ref), (gain_hbm, gain_ref), (cot_hbm, cot_ref),
+        (pool_hbm, pool_ref), (w_conv_hbm, w_conv_ref), (pos_hbm, pos_ref),
+    ], sems)
+    loads[3].wait()
+    fine_t = jnp.transpose(cot_ref[...].astype(F32))
+    for t in range(2):
+        turned_ref[t] = fine_t[:, 128 * t : 128 * t + 128]
+    for load in loads[:3]:
+        load.wait()
+    s_val, act = features(lat_ref[...], w_short_ref[...], gain_ref[...])
     s_ref[...] = s_val
     act_ref[...] = act
-    follows = (pos_ref[0, 1] >= 1).astype(F32)
-    keep0 = (next_pos_ref[0, 0] >= 1).astype(F32)
-    keep1 = (next_pos_ref[0, 1] >= 2).astype(F32)
-
-    after = next_ref[...].astype(F32)
-    loads[4].wait()
-    fine = jnp.concatenate([cot_ref[...].astype(F32), after[:FINE] * keep0, after[FINE:] * keep1], axis=0)
-    fine_t = jnp.transpose(fine)
-    for tile in range(4):
-        turned_ref[tile] = fine_t[:, 128 * tile : 128 * tile + 128]
-    for j in range(8):
-        parts = []
-        for tile in range(4):
-            for r in range(3):
-                parts.append(turned_ref[tile, pl.ds(8 * r + j, 8, stride=24), :])
-        send_ref[j, :96] = jnp.concatenate(parts, axis=0).astype(BF16)
     tail = jnp.concatenate([act[:CELLS, 128:], act[CELLS:, 128:]], axis=1)
     packed = jnp.concatenate([act[:, :128], tail], axis=0)
+
     for j in range(8):
+        send_ref[j, :48] = slices_for(turned_ref, (0, 1), j)
         send_ref[j, 96:192] = packed
 
     fine_t = fine_t.astype(BF16)
+    loads[4].wait()
+    for ab in range(9):
+        part = dot(fine_t, pool_ref[: 2 * FINE, ab * 128 : (ab + 1) * 128])
+        if ab == 4:
+            pooled_ref[...] = jnp.transpose(part)[: 2 * CELLS]
+        ct_ref[ab] = part.astype(BF16)
     loads[5].wait()
-    pooled = None
+    loads[6].wait()
+
+
+def local_kernel(
+    next_ref, sent_ref, s_ref, ct_ref, pooled_ref, pool_ref, w_conv_ref, lat_ref, gain_ref, pos_ref,
+    send_ref, ds_ref, turned_ref,
+):
+    fine_t = jnp.transpose(next_ref[...].astype(F32))
+    for t in range(2):
+        turned_ref[t] = fine_t[:, 128 * t : 128 * t + 128]
+    for j in range(8):
+        send_ref[j, :48] = sent_ref[j, :48]
+        send_ref[j, 48:96] = slices_for(turned_ref, (0, 1), j)
+        send_ref[j, 96:192] = sent_ref[j, 96:192]
+
+    fine_t = fine_t.astype(BF16)
+    acc = None
     for ab in range(9):
-        part = dot(fine_t, pool_ref[:, ab * 128 : (ab + 1) * 128])
-        if ab == 4:
-            pooled = jnp.transpose(part)[: 2 * CELLS]
-        ct[ab] = part.astype(BF16)
-
-    loads[6].wait()
-    turned = []
-    for k in range(3):
-        acc = dot(w_conv_ref[9 * k], ct[0])
-        for ab in range(1, 9):
-            acc = acc + dot(w_conv_ref[9 * k + ab], ct[ab])
-        turned.append(jnp.transpose(acc))
+        part = dot(fine_t, pool_ref[2 * FINE :, ab * 128 : (ab + 1) * 128]).astype(BF16)
+        pooled = ct_ref[ab] + part
+        taps = jnp.concatenate([w_conv_ref[9 * k + ab] for k in range(3)], axis=0)
+        value = dot(taps, pooled)
+        acc = value if acc is None else acc + value
+    turned = [jnp.transpose(acc[C * k : C * k + C]) for k in range(3)]
+    follows = (pos_ref[:, 1:] >= 1).astype(F32)
+    gain = gain_ref[...]
     early = turned[2][:32] + follows * (turned[1][32:64] + turned[0][64:96])
     late = turned[2][32:64] + turned[1][64:96] + turned[0][96:]
     grad_act = jnp.concatenate([early, late], axis=0)
+    scale, normed, z_val, sig = activation(s_ref[...], gain)
     dz_val = grad_act * sig * (1.0 + z_val * (1.0 - sig))
     gain_term = jnp.sum(dz_val * normed, axis=0, keepdims=True)
     dn_val = dz_val * gain
-    ds_val = scale * (dn_val - normed * jnp.mean(dn_val * normed, axis=-1, keepdims=True)) + pooled
-    ds_flat = ds_val.astype(BF16)
-    ds_ref[...] = ds_flat
-
-    short_t = dot(jnp.transpose(ds_val).astype(BF16), lat)
+    ds_val = scale * (dn_val - normed * jnp.mean(dn_val * normed, axis=-1, keepdims=True)) + pooled_ref[...]
+    ds_ref[...] = ds_val.astype(BF16)
+
+    short_t = dot(jnp.transpose(ds_val).astype(BF16), lat_ref[...])
     last = jnp.concatenate(
         [gain_term[:, :128], jnp.concatenate([gain_term[:, 128:], jnp.zeros((1, 64), F32)], axis=1),
-         jnp.full((1, 128), follows), jnp.zeros((5, 128), F32)], axis=0)
+         jnp.broadcast_to(follows, (1, 128)), jnp.zeros((5, 128), F32)], axis=0)
     for j in range(8):
         rows = short_t[24 * j : 24 * j + 24]
         flat = jnp.concatenate([rows[:, :128], rows[:, 128:256], rows[:, 256:], last], axis=0)
         send_ref[j, 192:] = flat.astype(BF16)
 
 
-def kernel_grad_kernel(got_ref, pool_hbm, out_ref, pool_ref, even_ref, odd_ref, rhs_ref, flat_ref, sem):
-    load_pool = pltpu.make_async_copy(pool_hbm, pool_ref, sem)
-    load_pool.start()
+def kernel_grad_kernel(got_ref, pool_ref, out_ref, even_ref, odd_ref, rhs_ref, flat_ref):
     none = jnp.zeros((CELLS, C), F32)
     gap = jnp.zeros((4 * CELLS, 64), F32)
     peers = []
@@ -151,7 +176,6 @@
             rhs_ref[2 * k, 128 * p : 128 * p + 128] = jnp.concatenate([value, gap], axis=1).astype(BF16)
             rhs_ref[2 * k + 1, 128 * p : 128 * p + 128] = jnp.concatenate([gap, value], axis=1).astype(BF16)
     fine_t = jnp.concatenate(peers, axis=0).astype(BF16)
-    load_pool.wait()
     for ab in range(9):
         part = dot(fine_t, pool_ref[:, ab * 128 : (ab + 1) * 128])
         wide = jnp.concatenate([part[24 * p : 24 * p + 24] for p in range(8)], axis=1)
@@ -184,7 +208,8 @@
         out_ref[x, 256:] = short
 
 
-def sum_x_kernel(got_ref, out_ref):
+def sum_x_kernel(got_ref, lat_ref, out_ref, lat_out_ref):
+    lat_out_ref[...] = lat_ref[...]
     total = got_ref[0].astype(F32)
     for i in range(1, 4):
         total = total + got_ref[i].astype(F32)
@@ -197,7 +222,7 @@
             out_ref[2 * zl + zh, 16:] = rest
 
 
-def sum_z_kernel(got_ref, out_ref):
+def sum_z_kernel(got_ref, turn_ref, out_ref):
     total = got_ref[0].astype(F32)
     for i in range(1, 16):
         total = total + got_ref[i].astype(F32)
@@ -224,19 +249,13 @@
 
 
 def forward_kernel(
-    before_ref, s_ref, act_ref, ds_ref, pos_hbm, w_short_hbm, gain_hbm, spread_hbm, w_conv_hbm,
+    before_ref, s_ref, act_ref, ds_ref, w_conv_ref, pos_hbm, w_short_hbm, gain_hbm, spread_hbm,
     decoded_ref, grad_latent_ref,
-    pos_ref, w_short_ref, gain_ref, spread_ref, w_conv_ref, z_all, sems,
+    pos_ref, w_short_ref, gain_ref, spread_ref, z_all, sems,
 ):
-    loads = [
-        pltpu.make_async_copy(source, target, sems.at[i])
-        for i, (source, target) in enumerate([
-            (pos_hbm, pos_ref), (w_short_hbm, w_short_ref), (gain_hbm, gain_ref), (spread_hbm, spread_ref),
-            (w_conv_hbm, w_conv_ref),
-        ])
-    ]
-    for load in loads:
-        load.start()
+    loads = start_loads([
+        (pos_hbm, pos_ref), (w_short_hbm, w_short_ref), (gain_hbm, gain_ref), (spread_hbm, spread_ref),
+    ], sems)
     for load in loads[:3]:
         load.wait()
     w_short = w_short_ref[...]
@@ -249,7 +268,6 @@
         jnp.concatenate([prev[CELLS:] * valid[0][1], act[:CELLS].astype(F32) * valid[1][1]], axis=0).astype(BF16),
         act,
     ]
-    loads[4].wait()
     for ab in range(9):
         acc = dot(taps[0], w_conv_ref[ab]) + dot(taps[1], w_conv_ref[9 + ab]) + dot(taps[2], w_conv_ref[18 + ab])
         if ab == 4:
@@ -279,9 +297,9 @@
     )
 
 
-SMEM = pl.BlockSpec(memory_space=pltpu.SMEM)
 VMEM = pl.BlockSpec(memory_space=pltpu.VMEM)
 HBM = pl.BlockSpec(memory_space=pltpu.HBM)
+ANY = pl.BlockSpec(memory_space=pl.ANY)
 
 
 def on_device(latent, frame_pos, w_short, gain, w_conv, cotangent):
@@ -294,34 +312,52 @@
     spread = jnp.asarray(pool_matrix(2), BF16)
 
     tm = ("zl", "y", "c")
-    back = [(i + 1, i) for i in range(63)]
-    following = lax.ppermute(cot, tm, back)
-    next_pos = lax.ppermute(frame_pos, tm, back)
-    before = lax.ppermute(lat, tm, [(i, i + 1) for i in range(63)])
-
-    send, s_val, act, ds_flat = call(
-        local_kernel, "local_kernel",
-        [shape(8, SEND_ROWS, 128), shape(2 * CELLS, C, dtype=F32), shape(2 * CELLS, C), shape(2 * CELLS, C)],
-        [SMEM, VMEM] + [HBM] * 7,
+    ahead = call(
+        ahead_kernel, "ahead_kernel", shape(2 * FINE, C), [HBM, HBM],
+        [pltpu.VMEM((1, 2), jnp.int32), pltpu.VMEM((2 * FINE, C), BF16), pltpu.SemaphoreType.DMA((2,))],
+    )(in_hbm(frame_pos), in_hbm(cot))
+    following = lax.ppermute(ahead, tm, [(i + 1, i) for i in range(63)])
+    own, s_val, act, ct, pooled, pool_near, conv_near, lat_near, gain_near, pos_near = call(
+        own_kernel, "own_kernel",
         [
-            pltpu.SMEM((1, 2), jnp.int32), pltpu.VMEM((2 * CELLS, C_IN), BF16), pltpu.VMEM((C, C_IN), BF16),
-            pltpu.VMEM((1, C), F32), pltpu.VMEM((2 * FINE, C), BF16), pltpu.VMEM((4 * FINE, 9 * 128), BF16),
-            pltpu.VMEM((TAPS, C, C), BF16), pltpu.VMEM((4, C, 128), F32), pltpu.VMEM((9, C, 128), BF16),
+            shape(8, SEND_ROWS, 128), shape(2 * CELLS, C, dtype=F32), shape(2 * CELLS, C), shape(9, C, 128),
+            shape(2 * CELLS, C, dtype=F32), shape(4 * FINE, 9 * 128), shape(TAPS, C, C),
+            shape(2 * CELLS, C_IN), shape(1, C, dtype=F32), shape(1, 2, dtype=jnp.int32),
+        ],
+        [HBM] * 7,
+        [
+            pltpu.VMEM((C, C_IN), BF16), pltpu.VMEM((2 * FINE, C), BF16), pltpu.VMEM((2, C, 128), F32),
             pltpu.SemaphoreType.DMA((7,)),
         ],
-    )(next_pos, following, *map(in_hbm, (frame_pos, lat, w_short_t, gain2, cot, pool, w27)))
+    )(*map(in_hbm, (lat, w_short_t, gain2, cot, frame_pos, pool, w27)))
+    send, ds_flat = call(
+        local_kernel, "local_kernel", [shape(8, SEND_ROWS, 128), shape(2 * CELLS, C)],
+        [VMEM] * 10, [pltpu.VMEM((2, C, 128), F32)],
+    )(following, own, s_val, ct, pooled, pool_near, conv_near, lat_near, gain_near, pos_near)
     got = lax.all_to_all(send, ("c", "y"), 0, 0)
     part = call(
-        kernel_grad_kernel, "kernel_grad_kernel", shape(4, MSG, 128), [VMEM, HBM],
+        kernel_grad_kernel, "kernel_grad_kernel", shape(4, MSG, 128), [VMEM, VMEM],
         [
-            pltpu.VMEM((4 * FINE, 9 * 128), BF16), pltpu.VMEM((120, 1024), F32), pltpu.VMEM((96, 1024), F32),
-            pltpu.VMEM((6, 1024, 256), BF16), pltpu.VMEM((1024, 128), F32), pltpu.SemaphoreType.DMA,
+            pltpu.VMEM((120, 1024), F32), pltpu.VMEM((96, 1024), F32),
+            pltpu.VMEM((6, 1024, 256), BF16), pltpu.VMEM((1024, 128), F32),
         ],
-    )(got, in_hbm(pool))
+    )(got, pool_near)
     got = lax.all_to_all(part, "x", 0, 0)
-    part = call(sum_x_kernel, "sum_x_kernel", shape(16, 32, 128), [VMEM])(got)
+    part, lat_late = call(
+        sum_x_kernel, "sum_x_kernel", [shape(16, 32, 128), shape(2 * CELLS, C_IN)], [VMEM, VMEM]
+    )(got, lat_near)
+    before = lax.ppermute(lat_late, tm, [(i, i + 1) for i in range(63)])
+    decoded, grad_latent = call(
+        forward_kernel, "forward_kernel", [shape(2 * FINE, C), shape(2 * CELLS, C_IN)],
+        [VMEM] * 5 + [HBM] * 4,
+        [
+            pltpu.SMEM((1, 2), jnp.int32), pltpu.VMEM((C, C_IN), BF16), pltpu.VMEM((1, C), F32),
+            pltpu.VMEM((2 * FINE, 18 * CELLS), BF16), pltpu.VMEM((9 * 2 * CELLS, C), BF16),
+            pltpu.SemaphoreType.DMA((4,)),
+        ],
+    )(before, s_val, act, ds_flat, conv_near, *map(in_hbm, (frame_pos, w_short_t, gain2, spread)))
     got = lax.all_to_all(part, ("zl", "zh"), 0, 0)
-    part = call(sum_z_kernel, "sum_z_kernel", shape(32, 32, 128), [VMEM])(got)
+    part = call(sum_z_kernel, "sum_z_kernel", shape(32, 32, 128), [VMEM, ANY])(got, in_hbm(grad_latent))
     got = lax.all_to_all(part, ("y", "zl"), 0, 0)
     got = lax.all_gather(got, "c", axis=0, tiled=True)
     grad_conv, grad_short_t, grad_gain = call(
@@ -329,16 +365,6 @@
         [shape(24, TAPS * C, dtype=F32), shape(C, C_IN, dtype=F32), shape(1, C, dtype=F32)],
         [VMEM], [pltpu.VMEM((1024, 128), F32)],
     )(got)
-
-    decoded, grad_latent = call(
-        forward_kernel, "forward_kernel", [shape(2 * FINE, C), shape(2 * CELLS, C_IN)],
-        [VMEM] * 4 + [HBM] * 5,
-        [
-            pltpu.SMEM((1, 2), jnp.int32), pltpu.VMEM((C, C_IN), BF16), pltpu.VMEM((1, C), F32),
-            pltpu.VMEM((2 * FINE, 18 * CELLS), BF16), pltpu.VMEM((TAPS, C, C), BF16),
-            pltpu.VMEM((9 * 2 * CELLS, C), BF16), pltpu.SemaphoreType.DMA((5,)),
-        ],
-    )(before, s_val, act, ds_flat, *map(in_hbm, (frame_pos, w_short_t, gain2, spread, w27)))
     return (
         decoded.reshape(cotangent.shape),
         grad_latent.reshape(latent.shape),

time: 101 us -> 99.1 us (0.981)
  waiting for transfers between devices: 12.9 us -> 6.11 us
  starting transfers between devices: 21.4 us -> 27.7 us
  blocking collectives: 53.4 us -> 52.3 us
    all_to_all x1, starting transfers between devices: 5.48 us -> 14.9 us  [on_device(): got = lax.all_to_all(part, ('zl', 'zh'), 0, 0)]
    all_to_all x1, waiting for transfers between devices: 8.65 us -> 4.95 us  [on_device(): got = lax.all_to_all(part, ('zl', 'zh'), 0, 0)]
    pallas_call x2 -> x4, Pallas kernels: 0.78 us -> 4.14 us  [the longest x1 2.38 us: on_device(): call(own_kernel, 'own_kernel', [shape(8, SEND_ROWS, 128), shape(2 * CELLS...]
    ppermute x3 -> x2, starting transfers between devices: 15.9 us -> 12.8 us  [the longest x1 8.79 us: on_device(): following = lax.ppermute(ahead, tm, [(i + 1, i) for i in range(63)])]
    ppermute x3 -> x2, waiting for transfers between devices: 4.26 us -> 1.16 us  [the longest x1 1.16 us: on_device(): before = lax.ppermute(lat_late, tm, [(i, i + 1) for i in range(63)])]
    all_to_all x1, blocking collectives: 27.7 us -> 25 us  [on_device(): got = lax.all_to_all(part, ('y', 'zl'), 0, 0)]
    pallas_call x1, Pallas kernels: 4.34 us -> 2.53 us  [on_device(): call(local_kernel, 'local_kernel', [shape(8, SEND_ROWS, 128), shape(2 * C...]
    pallas_call x1, Pallas kernels: 2.52 us -> 1.24 us  [on_device(): call(kernel_grad_kernel, 'kernel_grad_kernel', shape(4, MSG, 128), [VMEM,...]
  transfers between devices with their start and end apart: 4 -> 3, of which waited for: 3 -> 2; matrix products, arithmetic and copies ran while one was open for 0% -> 0% of each run, Pallas kernels for 4% -> 5%
where the time goes in v3:
time: 99.1 us; the launch traced here: 98.7 us
  blocking collectives  52.3 us (53%)
  starting transfers between devices  27.7 us (28%)
  Pallas kernels  11.9 us (12%)
  waiting for transfers between devices  6.11 us (6%)
    all_to_all x1, blocking collectives, on_device(): got = lax.all_to_all(part, ('y', 'zl'), 0, 0)  25 us
    all_to_all x1, starting transfers between devices, on_device(): got = lax.all_to_all(part, ('zl', 'zh'), 0, 0)  14.9 us
    all_to_all x1, blocking collectives, on_device(): got = lax.all_to_all(send, ('c', 'y'), 0, 0)  12.4 us
    all_to_all x1, blocking collectives, on_device(): got = lax.all_to_all(part, 'x', 0, 0)  10.8 us
    ppermute x1, starting transfers between devices, on_device(): following = lax.ppermute(ahead, tm, [(i + 1, i) for i in range(63)])  8.79 us
    all_to_all x1, waiting for transfers between devices, on_device(): got = lax.all_to_all(part, ('zl', 'zh'), 0, 0)  4.95 us
    all_gather x1, blocking collectives, on_device(): got = lax.all_gather(got, 'c', axis=0, tiled=True)  4.07 us
    ppermute x1, starting transfers between devices, on_device(): before = lax.ppermute(lat_late, tm, [(i, i + 1) for i in range(63)])  3.98 us
  transfers between devices with their start and end apart: 3, of which 2 were waited for; matrix products, arithmetic and copies ran while one was open for 0% of the time, Pallas kernels for 5%

profile of v3, /device:TPU:1, one launch (start us, length us, event | category | flops | bytes accessed | tf_op | source)
XLA Modules:
  0.0 98.7 jit_solution(9173054366942387380)
XLA Ops:
  0.6 1.0 %ahead_kernel.1 = bf16[256,192]{1,0:T(8,128)(2,1)S(1)} custom-call(s32[1,2]{1,0:T(1,128)} %pos_hbm.5, bf16[256,192]{1,0:T(8,128)(2,1)} %bitcast.12), custom_call_target="tpu_custom_call" | custom-call | tf_op jit(solution)/shard_map/ahead_kernel/pallas_call | solution.py:315
  1.7 8.8 %collective-permute-start = (bf16[256,192]{1,0:T(8,128)(2,1)S(1)}, bf16[256,192]{1,0:T(8,128)(2,1)S(1)}, u32[]{:S(2)}, u32[]{:S(2)}) collective-permute-start(bf16[256,192]{1,0:T(8,128)(2,1)S(1)} %ahead_kernel.1), channel_id=1, source_target_pairs={{8,0},{16,8},{24,16},{32,24},{40,32},{48,40},{56,48},{64,56},{72,6... | collective-permute-start | bytes 294920 | tf_op jit(solution)/shard_map/ppermute | solution.py:319
  10.5 2.4 %own_kernel.1 = (bf16[8,272,128]{2,1,0:T(8,128)(2,1)S(1)}, f32[64,192]{1,0:T(8,128)S(1)}, bf16[64,192]{1,0:T(8,128)(2,1)S(1)}, bf16[9,192,128]{2,1,0:T(8,128)(2,...) custom-call(bf16[64,384]{1,0:T(8,128)(2,1)} %bitcast.14, ...), custom_call_target="tpu_custom_call" | custom-call | tf_op jit(solution)/shard_map/own_kernel/pallas_call | solution.py:320
  12.8 0.0 collective-permute-done.next_ref
  12.9 2.5 %local_kernel.1 = (bf16[8,272,128]{2,1,0:T(8,128)(2,1)S(1)}, bf16[64,192]{1,0:T(8,128)(2,1)S(1)}) custom-call(bf16[256,192]{1,0:T(8,128)(2,1)S(1)} %collective-permute-done.next_ref, bf16[8,272,128]{2,1,0:T(8,128)(2,1)S(1)} %get-tuple-element.24.sent_ref, f32[64,192]{1,0:T(8,128)S(1)} %get-tuple-element.25.s_ref, ...), custom_call_target="tpu_custom_call" | custom-call | tf_op jit(solution)/shard_map/local_kernel/pallas_call | solution.py:333
  15.4 12.4 %all_to_all.20.got_ref = bf16[8,272,128]{2,1,0:T(8,128)(2,1)S(1)} all-to-all(bf16[8,272,128]{2,1,0:T(8,128)(2,1)S(1)} %get-tuple-element.33), channel_id=1, replica_groups=mesh['zl'=8,'y'=4,'c'=2,'x'=4,'zh'=2] {'c','y'}, dimensions={0} | all-to-all | bytes 1114112 | tf_op jit(solution)/shard_map/all_to_all | solution.py:337
  27.8 1.2 %kernel_grad_kernel.1 = bf16[4,336,128]{2,1,0:T(8,128)(2,1)S(1)} custom-call(bf16[8,272,128]{2,1,0:T(8,128)(2,1)S(1)} %all_to_all.20.got_ref, bf16[512,1152]{1,0:T(8,128)(2,1)S(1)} %get-tuple-element.28.pool_ref), custom_call_target="tpu_custom_call" | custom-call | tf_op jit(solution)/shard_map/kernel_grad_kernel/pallas_call | solution.py:338
  29.1 10.8 %all_to_all.21.got_ref = bf16[4,336,128]{2,1,0:T(8,128)(2,1)S(1)} all-to-all(bf16[4,336,128]{2,1,0:T(8,128)(2,1)S(1)} %kernel_grad_kernel.1), channel_id=1, replica_groups=mesh['zl'=8,'y'=4,'c'=2,'x'=4,'zh'=2] {'x'}, dimensions={0} | all-to-all | bytes 688128 | tf_op jit(solution)/shard_map/all_to_all | solution.py:345
  39.8 0.7 sum_x_kernel.1
  40.5 14.9 %all-to-all-start.2 = ((bf16[16,32,128]{2,1,0:T(8,128)(2,1)}), bf16[16,32,128]{2,1,0:T(8,128)(2,1)S(1)}, u32[]{:S(2)}, u32[]{:S(2)}) async-start(bf16[16,32,128]{2,1,0:T(8,128)(2,1)} %get-tuple-element.39), calls=%async_computation.2 | async-start | bytes 262144 | tf_op jit(solution)/shard_map/all_to_all | solution.py:359
  55.4 4.0 %collective-permute-start.1 = (bf16[64,384]{1,0:T(8,128)(2,1)S(1)}, bf16[64,384]{1,0:T(8,128)(2,1)S(1)}, u32[]{:S(2)}, u32[]{:S(2)}) collective-permute-start(bf16[64,384]{1,0:T(8,128)(2,1)S(1)} %get-tuple-element.34), channel_id=1, source_target_pairs={{0,8},{8,16},{16,24},{24,32},{32,40},{40,48},{48,56},{56,64},{64,7... | collective-permute-start | bytes 147464 | tf_op jit(solution)/shard_map/ppermute | solution.py:349
  59.4 1.2 %collective-permute-done.1.before_ref = bf16[64,384]{1,0:T(8,128)(2,1)S(1)} collective-permute-done((bf16[64,384]{1,0:T(8,128)(2,1)S(1)}, bf16[64,384]{1,0:T(8,128)(2,1)S(1)}, u32[]{:S(2)}, u32[]{:S(2)}) %collective-permute-start.1) | collective-permute-done | bytes 49184 | tf_op jit(solution)/shard_map/ppermute | solution.py:349
  60.6 2.9 %forward_kernel.1 = (bf16[256,192]{1,0:T(8,128)(2,1)}, bf16[64,384]{1,0:T(8,128)(2,1)}) custom-call(bf16[64,384]{1,0:T(8,128)(2,1)S(1)} %collective-permute-done.1.before_ref, f32[64,192]{1,0:T(8,128)S(1)} %get-tuple-element.25.s_ref, bf16[64,192]{1,0:T(8,128)(2,1)S(1)} %get-tuple-element.35.act_ref, bf16[64,192]{1,0:T(8,128)(2,1)S(1)} %get-tuple-element.36.ds_ref, ...), custom_call_target="tpu_custom_call" | custom-call | tf_op jit(solution)/shard_map/forward_kernel/pallas_call | solution.py:350
  63.5 4.9 %all-to-all-done.2.got_ref = bf16[16,32,128]{2,1,0:T(8,128)(2,1)S(1)} async-done(((bf16[16,32,128]{2,1,0:T(8,128)(2,1)}), bf16[16,32,128]{2,1,0:T(8,128)(2,1)S(1)}, u32[]{:S(2)}, u32[]{:S(2)}) %all-to-all-start.2) | async-done | bytes 131104 | tf_op jit(solution)/shard_map/all_to_all | solution.py:359
  68.5 25.0 %all_to_all.22 = bf16[32,32,128]{2,1,0:T(8,128)(2,1)S(1)} all-to-all(bf16[32,32,128]{2,1,0:T(8,128)(2,1)S(1)} %sum_z_kernel.1), channel_id=1, replica_groups=mesh['zl'=8,'y'=4,'c'=2,'x'=4,'zh'=2] {'y','zl'}, dimensions={0} | all-to-all | bytes 524288 | tf_op jit(solution)/shard_map/all_to_all | solution.py:361
  93.5 4.1 %all_gather.3.got_ref = bf16[64,32,128]{2,1,0:T(8,128)(2,1)S(1)} all-gather(bf16[32,32,128]{2,1,0:T(8,128)(2,1)S(1)} %all_to_all.22), channel_id=1, replica_groups=mesh['zl'=8,'y'=4,'c'=2,'x'=4,'zh'=2] {'c'}, dimensions={0}, use_global_device_ids=true | all-gather | bytes 786432 | tf_op jit(solution)/shard_map/all_gather | solution.py:362
  97.6 1.1 %assemble_kernel.1 = (f32[24,5184]{1,0:T(8,128)}, f32[192,384]{1,0:T(8,128)}, f32[1,192]{1,0:T(1,128)}) custom-call(bf16[64,32,128]{2,1,0:T(8,128)(2,1)S(1)} %all_gather.3.got_ref), custom_call_target="tpu_custom_call" | custom-call | tf_op jit(solution)/shard_map/assemble_kernel/pallas_call | solution.py:363
  (1 shorter events, 0.0 us)
Async XLA Ops:
  1.7 11.2 %collective-permute-start = (bf16[256,192]{1,0:T(8,128)(2,1)S(1)}, bf16[256,192]{1,0:T(8,128)(2,1)S(1)}, u32[]{:S(2)}, u32[]{:S(2)}) collective-permute-start(bf16[256,192]{1,0:T(8,128)(2,1)S(1)} %ahead_kernel.1), channel_id=1, source_target_pairs={{8,0},{16,8},{24,16},{32,24},{40,32},{48,40},{56,48},{64,56},{72,6... | collective-permute-start | bytes 294920 | tf_op jit(solution)/shard_map/ppermute | solution.py:319
  40.5 27.9 %all-to-all-start.2 = ((bf16[16,32,128]{2,1,0:T(8,128)(2,1)}), bf16[16,32,128]{2,1,0:T(8,128)(2,1)S(1)}, u32[]{:S(2)}, u32[]{:S(2)}) async-start(bf16[16,32,128]{2,1,0:T(8,128)(2,1)} %get-tuple-element.39), calls=%async_computation.2 | async-start | bytes 262144 | tf_op jit(solution)/shard_map/all_to_all | solution.py:359
  55.4 5.1 %collective-permute-start.1 = (bf16[64,384]{1,0:T(8,128)(2,1)S(1)}, bf16[64,384]{1,0:T(8,128)(2,1)S(1)}, u32[]{:S(2)}, u32[]{:S(2)}) collective-permute-start(bf16[64,384]{1,0:T(8,128)(2,1)S(1)} %get-tuple-element.34), channel_id=1, source_target_pairs={{0,8},{8,16},{16,24},{24,32},{32,40},{40,48},{48,56},{56,64},{64,7... | collective-permute-start | bytes 147464 | tf_op jit(solution)/shard_map/ppermute | solution.py:349

commit v4 on v3

--- a/solution.py
+++ b/solution.py
@@ -76,9 +76,13 @@
         ahead_ref[rows] = (cot_ref[rows].astype(F32) * keep[t]).astype(BF16)
 
 
+def two_taps(w_conv_ref, k, ab):
+    return jnp.concatenate([w_conv_ref[9 * k + ab], w_conv_ref[9 * k + 9 + ab]], axis=0)
+
+
 def own_kernel(
     lat_hbm, w_short_hbm, gain_hbm, cot_hbm, pos_hbm, pool_hbm, w_conv_hbm,
-    send_ref, s_ref, act_ref, ct_ref, pooled_ref, pool_ref, w_conv_ref, lat_ref, gain_ref, pos_ref,
+    send_ref, s_ref, act_ref, turned_own_ref, pooled_ref, pool_ref, w_conv_ref, lat_ref, gain_ref, pos_ref,
     w_short_ref, cot_ref, turned_ref, sems,
 ):
     loads = start_loads([
@@ -103,17 +107,21 @@
 
     fine_t = fine_t.astype(BF16)
     loads[4].wait()
+    loads[5].wait()
+    acc = None
     for ab in range(9):
         part = dot(fine_t, pool_ref[: 2 * FINE, ab * 128 : (ab + 1) * 128])
         if ab == 4:
             pooled_ref[...] = jnp.transpose(part)[: 2 * CELLS]
-        ct_ref[ab] = part.astype(BF16)
-    loads[5].wait()
+        value = dot(two_taps(w_conv_ref, 1, ab), part.astype(BF16))
+        acc = value if acc is None else acc + value
+    for i in range(2):
+        turned_own_ref[i] = jnp.transpose(acc[C * i : C * i + C])
     loads[6].wait()
 
 
 def local_kernel(
-    next_ref, sent_ref, s_ref, ct_ref, pooled_ref, pool_ref, w_conv_ref, lat_ref, gain_ref, pos_ref,
+    next_ref, sent_ref, s_ref, turned_own_ref, pooled_ref, pool_ref, w_conv_ref, lat_ref, gain_ref, pos_ref,
     send_ref, ds_ref, turned_ref,
 ):
     fine_t = jnp.transpose(next_ref[...].astype(F32))
@@ -127,16 +135,15 @@
     fine_t = fine_t.astype(BF16)
     acc = None
     for ab in range(9):
-        part = dot(fine_t, pool_ref[2 * FINE :, ab * 128 : (ab + 1) * 128]).astype(BF16)
-        pooled = ct_ref[ab] + part
-        taps = jnp.concatenate([w_conv_ref[9 * k + ab] for k in range(3)], axis=0)
-        value = dot(taps, pooled)
+        part = dot(fine_t, pool_ref[2 * FINE :, ab * 128 : (ab + 1) * 128])
+        value = dot(two_taps(w_conv_ref, 0, ab), part.astype(BF16))
         acc = value if acc is None else acc + value
-    turned = [jnp.transpose(acc[C * k : C * k + C]) for k in range(3)]
+    after = [jnp.transpose(acc[C * i : C * i + C]) for i in range(2)]
+    tap1, tap2 = turned_own_ref[0], turned_own_ref[1]
     follows = (pos_ref[:, 1:] >= 1).astype(F32)
     gain = gain_ref[...]
-    early = turned[2][:32] + follows * (turned[1][32:64] + turned[0][64:96])
-    late = turned[2][32:64] + turned[1][64:96] + turned[0][96:]
+    early = tap2[:32] + follows * (tap1[32:64] + after[0][64:96])
+    late = tap2[32:64] + after[1][64:96] + after[0][96:]
     grad_act = jnp.concatenate([early, late], axis=0)
     scale, normed, z_val, sig = activation(s_ref[...], gain)
     dz_val = grad_act * sig * (1.0 + z_val * (1.0 - sig))
@@ -146,12 +153,15 @@
     ds_ref[...] = ds_val.astype(BF16)
 
     short_t = dot(jnp.transpose(ds_val).astype(BF16), lat_ref[...])
-    last = jnp.concatenate(
-        [gain_term[:, :128], jnp.concatenate([gain_term[:, 128:], jnp.zeros((1, 64), F32)], axis=1),
-         jnp.broadcast_to(follows, (1, 128)), jnp.zeros((5, 128), F32)], axis=0)
+    flag = jnp.broadcast_to(follows, (1, 128))
     for j in range(8):
-        rows = short_t[24 * j : 24 * j + 24]
-        flat = jnp.concatenate([rows[:, :128], rows[:, 128:256], rows[:, 256:], last], axis=0)
+        piece = gain_term[:, 64 * (j % 3) : 64 * (j % 3) + 64]
+        spare = 176 + 8 * (j // 4)
+        flat = jnp.concatenate([
+            short_t[24 * j : 24 * j + 24, :128], short_t[24 * j : 24 * j + 24, 128:256],
+            short_t[22 * j : 22 * j + 22, 256:], short_t[spare : spare + 8, 256:],
+            jnp.concatenate([piece, piece], axis=1), flag,
+        ], axis=0)
         send_ref[j, 192:] = flat.astype(BF16)
 
 
@@ -169,7 +179,7 @@
         extra = got_ref[p, 192:].astype(F32)
         short = short + extra
         act0, act1 = act[:CELLS], act[CELLS:]
-        mine = act0 * extra[74:75, :1]
+        mine = act0 * extra[79:80, :1]
         rows = [[none, none, mine, act1], [none, mine, act1, none], [act0, act1, none, none]]
         for k in range(3):
             value = jnp.concatenate(rows[k], axis=0)
@@ -192,7 +202,7 @@
 
     def place(tile, value):
         for r in range(3):
-            flat_ref[pl.ds(42 * r + tile, 8, stride=128), :] = value[8 * r : 8 * r + 8]
+            flat_ref[pl.ds(40 * r + tile, 8, stride=128), :] = value[8 * r : 8 * r + 8]
 
     for n in range(0, TAPS, 2):
         tile = 3 * (n // 2)
@@ -201,51 +211,56 @@
             place(tile + 1, found[n][:, 128:] + found[n + 1][:, :128])
             place(tile + 2, found[n + 1][:, 128:])
         else:
-            place(tile + 1, found[n][:, 128:])
+            half = found[n][:, 128:192]
+            gain_piece = jnp.broadcast_to(short[78:79, 64:], (8, 64))
+            flat_ref[pl.ds(120, 8, stride=128), :] = jnp.concatenate([half[:8], half[8:16]], axis=1)
+            flat_ref[pl.ds(121, 8, stride=128), :] = jnp.concatenate([half[16:], gain_piece], axis=1)
     short = short.astype(BF16)
     for x in range(4):
         out_ref[x, :256] = flat_ref[256 * x : 256 * x + 256].astype(BF16)
         out_ref[x, 256:] = short
 
 
-def sum_x_kernel(got_ref, lat_ref, out_ref, lat_out_ref):
-    lat_out_ref[...] = lat_ref[...]
+def sum_x_kernel(got_ref, out_ref):
     total = got_ref[0].astype(F32)
     for i in range(1, 4):
         total = total + got_ref[i].astype(F32)
-    total = total.astype(BF16)
     for zh in range(2):
+        chunks = jnp.concatenate([total[128 * zh : 128 * zh + 122], total[256:326]], axis=0)
         for zl in range(8):
-            row = 128 * zh + 16 * zl
-            out_ref[2 * zl + zh, :16] = total[row : row + 16]
-            rest = total[256 + 16 * zl : 272 + 16 * zl] if zl < 5 else jnp.zeros((16, 128), BF16)
-            out_ref[2 * zl + zh, 16:] = rest
-
-
-def sum_z_kernel(got_ref, turn_ref, out_ref):
+            piece = jnp.concatenate([chunks[24 * zl : 24 * zl + 24], total[326:334]], axis=0)
+            out_ref[8 * zh + zl] = piece.astype(BF16)
+
+
+def sum_z_kernel(got_ref, lat_ref, out_ref, spare_ref, lat_out_ref):
+    lat_out_ref[...] = lat_ref[...]
     total = got_ref[0].astype(F32)
     for i in range(1, 16):
         total = total + got_ref[i].astype(F32)
-    total = total.astype(BF16)
+    piece = total[:24].astype(BF16)
     for i in range(32):
-        out_ref[i] = total
-
-
-def assemble_kernel(got_ref, conv_ref, short_ref, gain_ref, flat_ref):
+        out_ref[i] = piece
+    spare_ref[...] = total[24:].astype(BF16)
+
+
+def assemble_kernel(got_ref, spare_ref, conv_ref, short_ref, gain_ref, flat_ref):
     for j in range(8):
         for zl in range(8):
-            row = 128 * j + 16 * zl
-            flat_ref[row : row + 16] = got_ref[8 * j + zl, :16].astype(F32)
-        rest = jnp.concatenate([got_ref[8 * j + zl, 16:] for zl in range(5)], axis=0).astype(F32)
-        for i in range(3):
-            short_ref[24 * j : 24 * j + 24, 128 * i : 128 * i + 128] = rest[24 * i : 24 * i + 24]
-        if j == 0:
-            gain_ref[...] = jnp.concatenate([rest[72:73], rest[73:74, :64]], axis=1)
-    for tile in range(TILES):
-        wide = 128 if tile < TILES - 1 else 64
+            row = 192 * j + 24 * zl
+            flat_ref[row : row + 24] = got_ref[32 * (j // 4) + 4 * zl + j % 4].astype(F32)
+    for tile in range(TILES - 1):
         for r in range(3):
-            value = flat_ref[pl.ds(42 * r + tile, 8, stride=128), :]
-            conv_ref[8 * r : 8 * r + 8, 128 * tile : 128 * tile + wide] = value[:, :wide]
+            value = flat_ref[pl.ds(40 * r + tile, 8, stride=192), :]
+            conv_ref[8 * r : 8 * r + 8, 128 * tile : 128 * tile + 128] = value
+    halves = [flat_ref[pl.ds(120 + i, 8, stride=192), :] for i in range(2)]
+    conv_ref[:, 128 * TILES - 128 :] = jnp.concatenate([halves[0][:, :64], halves[0][:, 64:], halves[1][:, :64]], axis=0)
+    gain_ref[...] = jnp.concatenate([halves[1][m : m + 1, 64:] for m in range(3)], axis=1)
+    for j in range(8):
+        row = 192 * j + 122
+        short_ref[24 * j : 24 * j + 24, :128] = flat_ref[row : row + 24]
+        short_ref[24 * j : 24 * j + 24, 128:256] = flat_ref[row + 24 : row + 48]
+        short_ref[22 * j : 22 * j + 22, 256:] = flat_ref[row + 48 : row + 70]
+    short_ref[176:, 256:] = spare_ref[...].astype(F32)
 
 
 def forward_kernel(
@@ -317,10 +332,10 @@
         [pltpu.VMEM((1, 2), jnp.int32), pltpu.VMEM((2 * FINE, C), BF16), pltpu.SemaphoreType.DMA((2,))],
     )(in_hbm(frame_pos), in_hbm(cot))
     following = lax.ppermute(ahead, tm, [(i + 1, i) for i in range(63)])
-    own, s_val, act, ct, pooled, pool_near, conv_near, lat_near, gain_near, pos_near = call(
+    own, s_val, act, turned_own, pooled, pool_near, conv_near, lat_near, gain_near, pos_near = call(
         own_kernel, "own_kernel",
         [
-            shape(8, SEND_ROWS, 128), shape(2 * CELLS, C, dtype=F32), shape(2 * CELLS, C), shape(9, C, 128),
+            shape(8, SEND_ROWS, 128), shape(2 * CELLS, C, dtype=F32), shape(2 * CELLS, C), shape(2, 128, C, dtype=F32),
             shape(2 * CELLS, C, dtype=F32), shape(4 * FINE, 9 * 128), shape(TAPS, C, C),
             shape(2 * CELLS, C_IN), shape(1, C, dtype=F32), shape(1, 2, dtype=jnp.int32),
         ],
@@ -333,7 +348,7 @@
     send, ds_flat = call(
         local_kernel, "local_kernel", [shape(8, SEND_ROWS, 128), shape(2 * CELLS, C)],
         [VMEM] * 10, [pltpu.VMEM((2, C, 128), F32)],
-    )(following, own, s_val, ct, pooled, pool_near, conv_near, lat_near, gain_near, pos_near)
+    )(following, own, s_val, turned_own, pooled, pool_near, conv_near, lat_near, gain_near, pos_near)
     got = lax.all_to_all(send, ("c", "y"), 0, 0)
     part = call(
         kernel_grad_kernel, "kernel_grad_kernel", shape(4, MSG, 128), [VMEM, VMEM],
@@ -343,8 +358,10 @@
         ],
     )(got, pool_near)
     got = lax.all_to_all(part, "x", 0, 0)
-    part, lat_late = call(
-        sum_x_kernel, "sum_x_kernel", [shape(16, 32, 128), shape(2 * CELLS, C_IN)], [VMEM, VMEM]
+    part = call(sum_x_kernel, "sum_x_kernel", shape(16, 32, 128), [VMEM])(got)
+    got = lax.all_to_all(part, ("zh", "zl"), 0, 0)
+    part, spare, lat_late = call(
+        sum_z_kernel, "sum_z_kernel", [shape(32, 24, 128), shape(8, 128), shape(2 * CELLS, C_IN)], [VMEM, VMEM]
     )(got, lat_near)
     before = lax.ppermute(lat_late, tm, [(i, i + 1) for i in range(63)])
     decoded, grad_latent = call(
@@ -356,15 +373,14 @@
             pltpu.SemaphoreType.DMA((4,)),
         ],
     )(before, s_val, act, ds_flat, conv_near, *map(in_hbm, (frame_pos, w_short_t, gain2, spread)))
-    got = lax.all_to_all(part, ("zl", "zh"), 0, 0)
-    part = call(sum_z_kernel, "sum_z_kernel", shape(32, 32, 128), [VMEM, ANY])(got, in_hbm(grad_latent))
-    got = lax.all_to_all(part, ("y", "zl"), 0, 0)
+    got = lax.all_to_all(part, ("zl", "y"), 0, 0)
     got = lax.all_gather(got, "c", axis=0, tiled=True)
+    spare = lax.all_gather(spare, "c", axis=0, tiled=True)
     grad_conv, grad_short_t, grad_gain = call(
         assemble_kernel, "assemble_kernel",
         [shape(24, TAPS * C, dtype=F32), shape(C, C_IN, dtype=F32), shape(1, C, dtype=F32)],
-        [VMEM], [pltpu.VMEM((1024, 128), F32)],
-    )(got)
+        [VMEM, VMEM], [pltpu.VMEM((1536, 128), F32)],
+    )(got, spare)
     return (
         decoded.reshape(cotangent.shape),
         grad_latent.reshape(latent.shape),

time: 99.1 us -> 93.8 us (0.947)
  starting transfers between devices: 27.7 us -> 20.4 us
  blocking collectives: 52.3 us -> 56.8 us
  waiting for transfers between devices: 6.11 us -> 2.42 us
  Pallas kernels: 11.9 us -> 13.1 us
    all_to_all x1, starting transfers between devices: 14.9 us -> 6.05 us  [on_device(): got = lax.all_to_all(part, ('zl', 'y'), 0, 0)]
    all_gather x1, blocking collectives: 4.07 us -> 6.73 us  [on_device(): got = lax.all_gather(got, 'c', axis=0, tiled=True)]
    all_to_all x1, waiting for transfers between devices: 4.95 us -> 2.42 us  [on_device(): got = lax.all_to_all(part, ('zl', 'y'), 0, 0)]
    all_gather x0 -> x1, blocking collectives: none -> 1.78 us  [on_device(): spare = lax.all_gather(spare, 'c', axis=0, tiled=True)]
    all_to_all x1, blocking collectives: 25 us -> 26.7 us  [on_device(): got = lax.all_to_all(part, ('zh', 'zl'), 0, 0)]
    pallas_call x1, Pallas kernels: 2.38 us -> 4.04 us  [on_device(): call(own_kernel, 'own_kernel', [shape(8, SEND_ROWS, 128), shape(2 * CELLS...]
    ppermute x1, starting transfers between devices: 3.98 us -> 5.59 us  [on_device(): before = lax.ppermute(lat_late, tm, [(i, i + 1) for i in range(63)])]
    all_to_all x1, blocking collectives: 10.8 us -> 9.58 us  [on_device(): got = lax.all_to_all(part, 'x', 0, 0)]
  transfers between devices with their start and end apart: 3 -> 3, of which waited for: 2 -> 1; matrix products, arithmetic and copies ran while one was open for 0% -> 0% of each run, Pallas kernels for 5% -> 7%
where the time goes in v4:
time: 93.8 us; the launch traced here: 93.4 us
  blocking collectives  56.8 us (61%)
  starting transfers between devices  20.4 us (22%)
  Pallas kernels  13.1 us (14%)
  waiting for transfers between devices  2.42 us (3%)
    all_to_all x1, blocking collectives, on_device(): got = lax.all_to_all(part, ('zh', 'zl'), 0, 0)  26.7 us
    all_to_all x1, blocking collectives, on_device(): got = lax.all_to_all(send, ('c', 'y'), 0, 0)  11.9 us
    all_to_all x1, blocking collectives, on_device(): got = lax.all_to_all(part, 'x', 0, 0)  9.58 us
    ppermute x1, starting transfers between devices, on_device(): following = lax.ppermute(ahead, tm, [(i + 1, i) for i in range(63)])  8.79 us
    all_gather x1, blocking collectives, on_device(): got = lax.all_gather(got, 'c', axis=0, tiled=True)  6.73 us
    all_to_all x1, starting transfers between devices, on_device(): got = lax.all_to_all(part, ('zl', 'y'), 0, 0)  6.05 us
    ppermute x1, starting transfers between devices, on_device(): before = lax.ppermute(lat_late, tm, [(i, i + 1) for i in range(63)])  5.59 us
    pallas_call x1, Pallas kernels, on_device(): call(own_kernel, 'own_kernel', [shape(8, SEND_ROWS, 128), shape(2 * CELLS...  4.04 us
  transfers between devices with their start and end apart: 3, of which 1 were waited for; matrix products, arithmetic and copies ran while one was open for 0% of the time, Pallas kernels for 7%

profile of v4, /device:TPU:1, one launch (start us, length us, event | category | flops | bytes accessed | tf_op | source)
XLA Modules:
  0.0 93.4 jit_solution(13895308471232566495)
XLA Ops:
  0.6 1.0 %ahead_kernel.1 = bf16[256,192]{1,0:T(8,128)(2,1)S(1)} custom-call(s32[1,2]{1,0:T(1,128)} %pos_hbm.5, bf16[256,192]{1,0:T(8,128)(2,1)} %bitcast.12), custom_call_target="tpu_custom_call" | custom-call | tf_op jit(solution)/shard_map/ahead_kernel/pallas_call | solution.py:330
  1.7 8.8 %collective-permute-start = (bf16[256,192]{1,0:T(8,128)(2,1)S(1)}, bf16[256,192]{1,0:T(8,128)(2,1)S(1)}, u32[]{:S(2)}, u32[]{:S(2)}) collective-permute-start(bf16[256,192]{1,0:T(8,128)(2,1)S(1)} %ahead_kernel.1), channel_id=1, source_target_pairs={{8,0},{16,8},{24,16},{32,24},{40,32},{48,40},{56,48},{64,56},{72,6... | collective-permute-start | bytes 294920 | tf_op jit(solution)/shard_map/ppermute | solution.py:334
  10.5 4.0 %own_kernel.1 = (bf16[8,272,128]{2,1,0:T(8,128)(2,1)S(1)}, f32[64,192]{1,0:T(8,128)S(1)}, bf16[64,192]{1,0:T(8,128)(2,1)S(1)}, f32[2,128,192]{2,1,0:T(8,128)S(1)...) custom-call(bf16[64,384]{1,0:T(8,128)(2,1)} %bitcast.14, ...), custom_call_target="tpu_custom_call" | custom-call | tf_op jit(solution)/shard_map/own_kernel/pallas_call | solution.py:335
  14.5 0.0 collective-permute-done.next_ref
  14.5 2.0 %local_kernel.1 = (bf16[8,272,128]{2,1,0:T(8,128)(2,1)S(1)}, bf16[64,192]{1,0:T(8,128)(2,1)S(1)}) custom-call(bf16[256,192]{1,0:T(8,128)(2,1)S(1)} %collective-permute-done.next_ref, bf16[8,272,128]{2,1,0:T(8,128)(2,1)S(1)} %get-tuple-element.25.sent_ref, f32[64,192]{1,0:T(8,128)S(1)} %get-tuple-element.26.s_ref, ...), custom_call_target="tpu_custom_call" | custom-call | tf_op jit(solution)/shard_map/local_kernel/pallas_call | solution.py:348
  16.5 11.9 %all_to_all.20.got_ref = bf16[8,272,128]{2,1,0:T(8,128)(2,1)S(1)} all-to-all(bf16[8,272,128]{2,1,0:T(8,128)(2,1)S(1)} %get-tuple-element.34), channel_id=1, replica_groups=mesh['zl'=8,'y'=4,'c'=2,'x'=4,'zh'=2] {'c','y'}, dimensions={0} | all-to-all | bytes 1114112 | tf_op jit(solution)/shard_map/all_to_all | solution.py:352
  28.5 1.2 %kernel_grad_kernel.1 = bf16[4,336,128]{2,1,0:T(8,128)(2,1)S(1)} custom-call(bf16[8,272,128]{2,1,0:T(8,128)(2,1)S(1)} %all_to_all.20.got_ref, bf16[512,1152]{1,0:T(8,128)(2,1)S(1)} %get-tuple-element.29.pool_ref), custom_call_target="tpu_custom_call" | custom-call | tf_op jit(solution)/shard_map/kernel_grad_kernel/pallas_call | solution.py:353
  29.7 9.6 %all_to_all.21.got_ref = bf16[4,336,128]{2,1,0:T(8,128)(2,1)S(1)} all-to-all(bf16[4,336,128]{2,1,0:T(8,128)(2,1)S(1)} %kernel_grad_kernel.1), channel_id=1, replica_groups=mesh['zl'=8,'y'=4,'c'=2,'x'=4,'zh'=2] {'x'}, dimensions={0} | all-to-all | bytes 688128 | tf_op jit(solution)/shard_map/all_to_all | solution.py:360
  39.3 0.1 sum_x_kernel.1
  39.3 26.7 %all_to_all.22.got_ref = bf16[16,32,128]{2,1,0:T(8,128)(2,1)S(1)} all-to-all(bf16[16,32,128]{2,1,0:T(8,128)(2,1)S(1)} %sum_x_kernel.1), channel_id=1, replica_groups=mesh['zl'=8,'y'=4,'c'=2,'x'=4,'zh'=2] {'zh','zl'}, dimensions={0} | all-to-all | bytes 262144 | tf_op jit(solution)/shard_map/all_to_all | solution.py:362
  66.1 0.7 sum_z_kernel.1
  66.8 6.1 %all-to-all-start.3 = ((bf16[32,24,128]{2,1,0:T(8,128)(2,1)}), bf16[32,24,128]{2,1,0:T(8,128)(2,1)S(1)}, u32[]{:S(2)}, u32[]{:S(2)}) async-start(bf16[32,24,128]{2,1,0:T(8,128)(2,1)} %get-tuple-element.40), calls=%async_computation.3 | async-start | bytes 393216 | tf_op jit(solution)/shard_map/all_to_all | solution.py:376
  72.8 5.6 %collective-permute-start.1 = (bf16[64,384]{1,0:T(8,128)(2,1)S(1)}, bf16[64,384]{1,0:T(8,128)(2,1)S(1)}, u32[]{:S(2)}, u32[]{:S(2)}) collective-permute-start(bf16[64,384]{1,0:T(8,128)(2,1)S(1)} %get-tuple-element.35), channel_id=1, source_target_pairs={{0,8},{8,16},{16,24},{24,32},{32,40},{40,48},{48,56},{56,64},{64,7... | collective-permute-start | bytes 147464 | tf_op jit(solution)/shard_map/ppermute | solution.py:366
  78.4 1.8 %all_gather.7.spare_ref = bf16[16,128]{1,0:T(8,128)(2,1)S(1)} all-gather(bf16[8,128]{1,0:T(8,128)(2,1)S(1)} %get-tuple-element.41), channel_id=1, replica_groups=mesh['zl'=8,'y'=4,'c'=2,'x'=4,'zh'=2] {'c'}, dimensions={0}, use_global_device_ids=true | all-gather | bytes 6144 | tf_op jit(solution)/shard_map/all_gather | solution.py:378
  80.2 0.0 collective-permute-done.1.before_ref
  80.2 2.9 %forward_kernel.1 = (bf16[256,192]{1,0:T(8,128)(2,1)}, bf16[64,384]{1,0:T(8,128)(2,1)}) custom-call(bf16[64,384]{1,0:T(8,128)(2,1)S(1)} %collective-permute-done.1.before_ref, f32[64,192]{1,0:T(8,128)S(1)} %get-tuple-element.26.s_ref, bf16[64,192]{1,0:T(8,128)(2,1)S(1)} %get-tuple-element.36.act_ref, bf16[64,192]{1,0:T(8,128)(2,1)S(1)} %get-tuple-element.37.ds_ref, ...), custom_call_target="tpu_custom_call" | custom-call | tf_op jit(solution)/shard_map/forward_kernel/pallas_call | solution.py:367
  83.1 2.4 %all-to-all-done.3 = bf16[32,24,128]{2,1,0:T(8,128)(2,1)S(1)} async-done(((bf16[32,24,128]{2,1,0:T(8,128)(2,1)}), bf16[32,24,128]{2,1,0:T(8,128)(2,1)S(1)}, u32[]{:S(2)}, u32[]{:S(2)}) %all-to-all-start.3) | async-done | bytes 196640 | tf_op jit(solution)/shard_map/all_to_all | solution.py:376
  85.5 6.7 %all_gather.6.got_ref = bf16[64,24,128]{2,1,0:T(8,128)(2,1)S(1)} all-gather(bf16[32,24,128]{2,1,0:T(8,128)(2,1)S(1)} %all-to-all-done.3), channel_id=1, replica_groups=mesh['zl'=8,'y'=4,'c'=2,'x'=4,'zh'=2] {'c'}, dimensions={0}, use_global_device_ids=true | all-gather | bytes 589824 | tf_op jit(solution)/shard_map/all_gather | solution.py:377
  92.3 1.2 %assemble_kernel.1 = (f32[24,5184]{1,0:T(8,128)}, f32[192,384]{1,0:T(8,128)}, f32[1,192]{1,0:T(1,128)}) custom-call(bf16[64,24,128]{2,1,0:T(8,128)(2,1)S(1)} %all_gather.6.got_ref, bf16[16,128]{1,0:T(8,128)(2,1)S(1)} %all_gather.7.spare_ref), custom_call_target="tpu_custom_call" | custom-call | tf_op jit(solution)/shard_map/assemble_kernel/pallas_call | solution.py:379
Async XLA Ops:
  1.7 12.8 %collective-permute-start = (bf16[256,192]{1,0:T(8,128)(2,1)S(1)}, bf16[256,192]{1,0:T(8,128)(2,1)S(1)}, u32[]{:S(2)}, u32[]{:S(2)}) collective-permute-start(bf16[256,192]{1,0:T(8,128)(2,1)S(1)} %ahead_kernel.1), channel_id=1, source_target_pairs={{8,0},{16,8},{24,16},{32,24},{40,32},{48,40},{56,48},{64,56},{72,6... | collective-permute-start | bytes 294920 | tf_op jit(solution)/shard_map/ppermute | solution.py:334
  66.8 18.8 %all-to-all-start.3 = ((bf16[32,24,128]{2,1,0:T(8,128)(2,1)}), bf16[32,24,128]{2,1,0:T(8,128)(2,1)S(1)}, u32[]{:S(2)}, u32[]{:S(2)}) async-start(bf16[32,24,128]{2,1,0:T(8,128)(2,1)} %get-tuple-element.40), calls=%async_computation.3 | async-start | bytes 393216 | tf_op jit(solution)/shard_map/all_to_all | solution.py:376
  72.8 7.4 %collective-permute-start.1 = (bf16[64,384]{1,0:T(8,128)(2,1)S(1)}, bf16[64,384]{1,0:T(8,128)(2,1)S(1)}, u32[]{:S(2)}, u32[]{:S(2)}) collective-permute-start(bf16[64,384]{1,0:T(8,128)(2,1)S(1)} %get-tuple-element.35), channel_id=1, source_target_pairs={{0,8},{8,16},{16,24},{24,32},{32,40},{40,48},{48,56},{56,64},{64,7... | collective-permute-start | bytes 147464 | tf_op jit(solution)/shard_map/ppermute | solution.py:366

commit v5 on v4

--- a/solution.py
+++ b/solution.py
@@ -12,6 +12,8 @@
 CELLS = 32
 FINE = 128
 TAPS = 27
+Z_FIRST = 10
+ZL_ORDER = (4, 3, 5, 2, 6, 1, 7, 0)
 TILES = 41
 SHORT_ROWS = 80
 SEND_ROWS = 192 + SHORT_ROWS
@@ -229,7 +231,7 @@
         chunks = jnp.concatenate([total[128 * zh : 128 * zh + 122], total[256:326]], axis=0)
         for zl in range(8):
             piece = jnp.concatenate([chunks[24 * zl : 24 * zl + 24], total[326:334]], axis=0)
-            out_ref[8 * zh + zl] = piece.astype(BF16)
+            out_ref[(8 * zh + zl - Z_FIRST) % 16] = piece.astype(BF16)
 
 
 def sum_z_kernel(got_ref, lat_ref, out_ref, spare_ref, lat_out_ref):
@@ -247,7 +249,7 @@
     for j in range(8):
         for zl in range(8):
             row = 192 * j + 24 * zl
-            flat_ref[row : row + 24] = got_ref[32 * (j // 4) + 4 * zl + j % 4].astype(F32)
+            flat_ref[row : row + 24] = got_ref[32 * (j // 4) + 4 * ZL_ORDER.index(zl) + j % 4].astype(F32)
     for tile in range(TILES - 1):
         for r in range(3):
             value = flat_ref[pl.ds(40 * r + tile, 8, stride=192), :]
@@ -359,7 +361,7 @@
     )(got, pool_near)
     got = lax.all_to_all(part, "x", 0, 0)
     part = call(sum_x_kernel, "sum_x_kernel", shape(16, 32, 128), [VMEM])(got)
-    got = lax.all_to_all(part, ("zh", "zl"), 0, 0)
+    got = lax.all_to_all(part, ("zh", "zl"), 0, 0, axis_index_groups=[[(Z_FIRST + i) % 16 for i in range(16)]])
     part, spare, lat_late = call(
         sum_z_kernel, "sum_z_kernel", [shape(32, 24, 128), shape(8, 128), shape(2 * CELLS, C_IN)], [VMEM, VMEM]
     )(got, lat_near)
@@ -373,7 +375,7 @@
             pltpu.SemaphoreType.DMA((4,)),
         ],
     )(before, s_val, act, ds_flat, conv_near, *map(in_hbm, (frame_pos, w_short_t, gain2, spread)))
-    got = lax.all_to_all(part, ("zl", "y"), 0, 0)
+    got = lax.all_to_all(part, ("zl", "y"), 0, 0, axis_index_groups=[[4 * zl + y for zl in ZL_ORDER for y in range(4)]])
     got = lax.all_gather(got, "c", axis=0, tiled=True)
     spare = lax.all_gather(spare, "c", axis=0, tiled=True)
     grad_conv, grad_short_t, grad_gain = call(

time: 93.8 us -> 85.8 us (0.915)
  blocking collectives: 56.8 us -> 47.6 us
  starting transfers between devices: 20.4 us -> 23.8 us
  waiting for transfers between devices: 2.42 us -> 0.01 us
    all_to_all x1, blocking collectives: 26.7 us -> 22 us  [on_device(): lax.all_to_all(part, ('zh', 'zl'), 0, 0, axis_index_groups=[[(Z_FIRST + i...]
    all_gather x1, blocking collectives: 6.73 us -> 2.37 us  [on_device(): got = lax.all_gather(got, 'c', axis=0, tiled=True)]
    all_to_all x1, waiting for transfers between devices: 2.42 us -> 0.01 us  [on_device(): lax.all_to_all(part, ('zl', 'y'), 0, 0, axis_index_groups=[[4 * zl + y fo...]
    all_to_all x1, starting transfers between devices: 6.05 us -> 8.03 us  [on_device(): lax.all_to_all(part, ('zl', 'y'), 0, 0, axis_index_groups=[[4 * zl + y fo...]
    ppermute x1, starting transfers between devices: 5.59 us -> 7.01 us  [on_device(): before = lax.ppermute(lat_late, tm, [(i, i + 1) for i in range(63)])]
  transfers between devices with their start and end apart: 3 -> 3, of which waited for: 1 -> 0; matrix products, arithmetic and copies ran while one was open for 0% -> 0% of each run, Pallas kernels for 7% -> 8%
where the time goes in v5:
time: 85.8 us; the launch traced here: 85.3 us
  blocking collectives  47.6 us (55%)
  starting transfers between devices  23.8 us (28%)
  Pallas kernels  13.1 us (15%)
    all_to_all x1, blocking collectives, on_device(): lax.all_to_all(part, ('zh', 'zl'), 0, 0, axis_index_groups=[[(Z_FIRST + i...  22 us
    all_to_all x1, blocking collectives, on_device(): got = lax.all_to_all(send, ('c', 'y'), 0, 0)  11.9 us
    all_to_all x1, blocking collectives, on_device(): got = lax.all_to_all(part, 'x', 0, 0)  9.58 us
    ppermute x1, starting transfers between devices, on_device(): following = lax.ppermute(ahead, tm, [(i + 1, i) for i in range(63)])  8.79 us
    all_to_all x1, starting transfers between devices, on_device(): lax.all_to_all(part, ('zl', 'y'), 0, 0, axis_index_groups=[[4 * zl + y fo...  8.03 us
    ppermute x1, starting transfers between devices, on_device(): before = lax.ppermute(lat_late, tm, [(i, i + 1) for i in range(63)])  7.01 us
    pallas_call x1, Pallas kernels, on_device(): call(own_kernel, 'own_kernel', [shape(8, SEND_ROWS, 128), shape(2 * CELLS...  4.04 us
    pallas_call x1, Pallas kernels, on_device(): call(forward_kernel, 'forward_kernel', [shape(2 * FINE, C), shape(2 * CEL...  2.88 us
  transfers between devices with their start and end apart: 3, of which 0 were waited for; matrix products, arithmetic and copies ran while one was open for 0% of the time, Pallas kernels for 8%

profile of v5, /device:TPU:1, one launch (start us, length us, event | category | flops | bytes accessed | tf_op | source)
XLA Modules:
  0.0 85.3 jit_solution(11430789235267358610)
XLA Ops:
  0.6 1.0 %ahead_kernel.1 = bf16[256,192]{1,0:T(8,128)(2,1)S(1)} custom-call(s32[1,2]{1,0:T(1,128)} %pos_hbm.5, bf16[256,192]{1,0:T(8,128)(2,1)} %bitcast.12), custom_call_target="tpu_custom_call" | custom-call | tf_op jit(solution)/shard_map/ahead_kernel/pallas_call | solution.py:332
  1.7 8.8 %collective-permute-start = (bf16[256,192]{1,0:T(8,128)(2,1)S(1)}, bf16[256,192]{1,0:T(8,128)(2,1)S(1)}, u32[]{:S(2)}, u32[]{:S(2)}) collective-permute-start(bf16[256,192]{1,0:T(8,128)(2,1)S(1)} %ahead_kernel.1), channel_id=1, source_target_pairs={{8,0},{16,8},{24,16},{32,24},{40,32},{48,40},{56,48},{64,56},{72,6... | collective-permute-start | bytes 294920 | tf_op jit(solution)/shard_map/ppermute | solution.py:336
  10.5 4.0 %own_kernel.1 = (bf16[8,272,128]{2,1,0:T(8,128)(2,1)S(1)}, f32[64,192]{1,0:T(8,128)S(1)}, bf16[64,192]{1,0:T(8,128)(2,1)S(1)}, f32[2,128,192]{2,1,0:T(8,128)S(1)...) custom-call(bf16[64,384]{1,0:T(8,128)(2,1)} %bitcast.14, ...), custom_call_target="tpu_custom_call" | custom-call | tf_op jit(solution)/shard_map/own_kernel/pallas_call | solution.py:337
  14.5 0.0 collective-permute-done.next_ref
  14.5 2.0 %local_kernel.1 = (bf16[8,272,128]{2,1,0:T(8,128)(2,1)S(1)}, bf16[64,192]{1,0:T(8,128)(2,1)S(1)}) custom-call(bf16[256,192]{1,0:T(8,128)(2,1)S(1)} %collective-permute-done.next_ref, bf16[8,272,128]{2,1,0:T(8,128)(2,1)S(1)} %get-tuple-element.25.sent_ref, f32[64,192]{1,0:T(8,128)S(1)} %get-tuple-element.26.s_ref, ...), custom_call_target="tpu_custom_call" | custom-call | tf_op jit(solution)/shard_map/local_kernel/pallas_call | solution.py:350
  16.5 11.9 %all_to_all.20.got_ref = bf16[8,272,128]{2,1,0:T(8,128)(2,1)S(1)} all-to-all(bf16[8,272,128]{2,1,0:T(8,128)(2,1)S(1)} %get-tuple-element.34), channel_id=1, replica_groups=mesh['zl'=8,'y'=4,'c'=2,'x'=4,'zh'=2] {'c','y'}, dimensions={0} | all-to-all | bytes 1114112 | tf_op jit(solution)/shard_map/all_to_all | solution.py:354
  28.5 1.2 %kernel_grad_kernel.1 = bf16[4,336,128]{2,1,0:T(8,128)(2,1)S(1)} custom-call(bf16[8,272,128]{2,1,0:T(8,128)(2,1)S(1)} %all_to_all.20.got_ref, bf16[512,1152]{1,0:T(8,128)(2,1)S(1)} %get-tuple-element.29.pool_ref), custom_call_target="tpu_custom_call" | custom-call | tf_op jit(solution)/shard_map/kernel_grad_kernel/pallas_call | solution.py:355
  29.7 9.6 %all_to_all.21.got_ref = bf16[4,336,128]{2,1,0:T(8,128)(2,1)S(1)} all-to-all(bf16[4,336,128]{2,1,0:T(8,128)(2,1)S(1)} %kernel_grad_kernel.1), channel_id=1, replica_groups=mesh['zl'=8,'y'=4,'c'=2,'x'=4,'zh'=2] {'x'}, dimensions={0} | all-to-all | bytes 688128 | tf_op jit(solution)/shard_map/all_to_all | solution.py:362
  39.3 0.1 sum_x_kernel.1
  39.3 22.0 %all_to_all.22.got_ref = bf16[16,32,128]{2,1,0:T(8,128)(2,1)S(1)} all-to-all(bf16[16,32,128]{2,1,0:T(8,128)(2,1)S(1)} %sum_x_kernel.1), channel_id=1, replica_groups={{129,193,257,321,385,449,0,64,128,192,256,320,384,448,1,65},{131,195,25..., dimensions={0} | all-to-all | bytes 262144 | tf_op jit(solution)/shard_map/all_to_all | solution.py:364
  61.3 0.7 sum_z_kernel.1
  62.0 8.0 %all-to-all-start.3 = ((bf16[32,24,128]{2,1,0:T(8,128)(2,1)}), bf16[32,24,128]{2,1,0:T(8,128)(2,1)S(1)}, u32[]{:S(2)}, u32[]{:S(2)}) async-start(bf16[32,24,128]{2,1,0:T(8,128)(2,1)} %get-tuple-element.40), calls=%async_computation.3 | async-start | bytes 393216 | tf_op jit(solution)/shard_map/all_to_all | solution.py:378
  70.1 7.0 %collective-permute-start.1 = (bf16[64,384]{1,0:T(8,128)(2,1)S(1)}, bf16[64,384]{1,0:T(8,128)(2,1)S(1)}, u32[]{:S(2)}, u32[]{:S(2)}) collective-permute-start(bf16[64,384]{1,0:T(8,128)(2,1)S(1)} %get-tuple-element.35), channel_id=1, source_target_pairs={{0,8},{8,16},{16,24},{24,32},{32,40},{40,48},{48,56},{56,64},{64,7... | collective-permute-start | bytes 147464 | tf_op jit(solution)/shard_map/ppermute | solution.py:368
  77.1 1.8 %all_gather.7.spare_ref = bf16[16,128]{1,0:T(8,128)(2,1)S(1)} all-gather(bf16[8,128]{1,0:T(8,128)(2,1)S(1)} %get-tuple-element.41), channel_id=1, replica_groups=mesh['zl'=8,'y'=4,'c'=2,'x'=4,'zh'=2] {'c'}, dimensions={0}, use_global_device_ids=true | all-gather | bytes 6144 | tf_op jit(solution)/shard_map/all_gather | solution.py:380
  78.9 0.0 collective-permute-done.1.before_ref
  78.9 2.9 %forward_kernel.1 = (bf16[256,192]{1,0:T(8,128)(2,1)}, bf16[64,384]{1,0:T(8,128)(2,1)}) custom-call(bf16[64,384]{1,0:T(8,128)(2,1)S(1)} %collective-permute-done.1.before_ref, f32[64,192]{1,0:T(8,128)S(1)} %get-tuple-element.26.s_ref, bf16[64,192]{1,0:T(8,128)(2,1)S(1)} %get-tuple-element.36.act_ref, bf16[64,192]{1,0:T(8,128)(2,1)S(1)} %get-tuple-element.37.ds_ref, ...), custom_call_target="tpu_custom_call" | custom-call | tf_op jit(solution)/shard_map/forward_kernel/pallas_call | solution.py:369
  81.8 0.0 all-to-all-done.3
  81.8 2.4 %all_gather.6.got_ref = bf16[64,24,128]{2,1,0:T(8,128)(2,1)S(1)} all-gather(bf16[32,24,128]{2,1,0:T(8,128)(2,1)S(1)} %all-to-all-done.3), channel_id=1, replica_groups=mesh['zl'=8,'y'=4,'c'=2,'x'=4,'zh'=2] {'c'}, dimensions={0}, use_global_device_ids=true | all-gather | bytes 589824 | tf_op jit(solution)/shard_map/all_gather | solution.py:379
  84.1 1.2 %assemble_kernel.1 = (f32[24,5184]{1,0:T(8,128)}, f32[192,384]{1,0:T(8,128)}, f32[1,192]{1,0:T(1,128)}) custom-call(bf16[64,24,128]{2,1,0:T(8,128)(2,1)S(1)} %all_gather.6.got_ref, bf16[16,128]{1,0:T(8,128)(2,1)S(1)} %all_gather.7.spare_ref), custom_call_target="tpu_custom_call" | custom-call | tf_op jit(solution)/shard_map/assemble_kernel/pallas_call | solution.py:381
Async XLA Ops:
  1.7 12.8 %collective-permute-start = (bf16[256,192]{1,0:T(8,128)(2,1)S(1)}, bf16[256,192]{1,0:T(8,128)(2,1)S(1)}, u32[]{:S(2)}, u32[]{:S(2)}) collective-permute-start(bf16[256,192]{1,0:T(8,128)(2,1)S(1)} %ahead_kernel.1), channel_id=1, source_target_pairs={{8,0},{16,8},{24,16},{32,24},{40,32},{48,40},{56,48},{64,56},{72,6... | collective-permute-start | bytes 294920 | tf_op jit(solution)/shard_map/ppermute | solution.py:336
  62.0 19.7 %all-to-all-start.3 = ((bf16[32,24,128]{2,1,0:T(8,128)(2,1)}), bf16[32,24,128]{2,1,0:T(8,128)(2,1)S(1)}, u32[]{:S(2)}, u32[]{:S(2)}) async-start(bf16[32,24,128]{2,1,0:T(8,128)(2,1)} %get-tuple-element.40), calls=%async_computation.3 | async-start | bytes 393216 | tf_op jit(solution)/shard_map/all_to_all | solution.py:378
  70.1 8.8 %collective-permute-start.1 = (bf16[64,384]{1,0:T(8,128)(2,1)S(1)}, bf16[64,384]{1,0:T(8,128)(2,1)S(1)}, u32[]{:S(2)}, u32[]{:S(2)}) collective-permute-start(bf16[64,384]{1,0:T(8,128)(2,1)S(1)} %get-tuple-element.35), channel_id=1, source_target_pairs={{0,8},{8,16},{16,24},{24,32},{32,40},{40,48},{48,56},{56,64},{64,7... | collective-permute-start | bytes 147464 | tf_op jit(solution)/shard_map/ppermute | solution.py:368

commit v6 on v5

--- a/solution.py
+++ b/solution.py
@@ -83,13 +83,14 @@
 
 
 def own_kernel(
-    lat_hbm, w_short_hbm, gain_hbm, cot_hbm, pos_hbm, pool_hbm, w_conv_hbm,
+    lat_hbm, w_short_hbm, gain_hbm, cot_hbm, pos_hbm, pool_hbm, w_conv_hbm, spread_hbm,
     send_ref, s_ref, act_ref, turned_own_ref, pooled_ref, pool_ref, w_conv_ref, lat_ref, gain_ref, pos_ref,
-    w_short_ref, cot_ref, turned_ref, sems,
+    w_short_ref, spread_ref, cot_ref, turned_ref, sems,
 ):
     loads = start_loads([
         (lat_hbm, lat_ref), (w_short_hbm, w_short_ref), (gain_hbm, gain_ref), (cot_hbm, cot_ref),
         (pool_hbm, pool_ref), (w_conv_hbm, w_conv_ref), (pos_hbm, pos_ref),
+        (spread_hbm, spread_ref),
     ], sems)
     loads[3].wait()
     fine_t = jnp.transpose(cot_ref[...].astype(F32))
@@ -120,6 +121,7 @@
     for i in range(2):
         turned_own_ref[i] = jnp.transpose(acc[C * i : C * i + C])
     loads[6].wait()
+    loads[7].wait()
 
 
 def local_kernel(
@@ -245,11 +247,11 @@
     spare_ref[...] = total[24:].astype(BF16)
 
 
-def assemble_kernel(got_ref, spare_ref, conv_ref, short_ref, gain_ref, flat_ref):
+def assemble_kernel(got_ref, spare_ref, other_ref, core_ref, conv_ref, short_ref, gain_ref, flat_ref):
     for j in range(8):
         for zl in range(8):
             row = 192 * j + 24 * zl
-            flat_ref[row : row + 24] = got_ref[32 * (j // 4) + 4 * ZL_ORDER.index(zl) + j % 4].astype(F32)
+            flat_ref[row : row + 24] = got_ref[32 * (j // 4) + ZL_ORDER.index(zl) + 8 * (j % 4)].astype(F32)
     for tile in range(TILES - 1):
         for r in range(3):
             value = flat_ref[pl.ds(40 * r + tile, 8, stride=192), :]
@@ -262,24 +264,21 @@
         short_ref[24 * j : 24 * j + 24, :128] = flat_ref[row : row + 24]
         short_ref[24 * j : 24 * j + 24, 128:256] = flat_ref[row + 24 : row + 48]
         short_ref[22 * j : 22 * j + 22, 256:] = flat_ref[row + 48 : row + 70]
-    short_ref[176:, 256:] = spare_ref[...].astype(F32)
+    mine, other = spare_ref[...].astype(F32), other_ref[...].astype(F32)
+    low = core_ref[...] == 0
+    short_ref[176:184, 256:] = jnp.where(low, mine, other)
+    short_ref[184:, 256:] = jnp.where(low, other, mine)
 
 
 def forward_kernel(
-    before_ref, s_ref, act_ref, ds_ref, w_conv_ref, pos_hbm, w_short_hbm, gain_hbm, spread_hbm,
-    decoded_ref, grad_latent_ref,
-    pos_ref, w_short_ref, gain_ref, spread_ref, z_all, sems,
+    before_ref, s_ref, act_ref, ds_ref, w_conv_ref, pos_ref, w_short_ref, gain_ref, spread_ref,
+    decoded_ref, grad_latent_ref, z_all,
 ):
-    loads = start_loads([
-        (pos_hbm, pos_ref), (w_short_hbm, w_short_ref), (gain_hbm, gain_ref), (spread_hbm, spread_ref),
-    ], sems)
-    for load in loads[:3]:
-        load.wait()
     w_short = w_short_ref[...]
     grad_latent_ref[...] = dot(ds_ref[...], w_short).astype(BF16)
     prev = features(before_ref[...], w_short, gain_ref[...])[-1].astype(F32)
     act = act_ref[...]
-    valid = [[(pos_ref[0, t] >= 2 - k).astype(F32) for k in range(2)] for t in range(2)]
+    valid = [[(pos_ref[:, t : t + 1] >= 2 - k).astype(F32) for k in range(2)] for t in range(2)]
     taps = [
         jnp.concatenate([prev[:CELLS] * valid[0][0], prev[CELLS:] * valid[1][0]], axis=0).astype(BF16),
         jnp.concatenate([prev[CELLS:] * valid[0][1], act[:CELLS].astype(F32) * valid[1][1]], axis=0).astype(BF16),
@@ -290,7 +289,6 @@
         if ab == 4:
             acc = acc + s_ref[...]
         z_all[64 * ab : 64 * ab + 64] = acc.astype(BF16)
-    loads[3].wait()
     decoded_ref[...] = dot(spread_ref[...], z_all[...]).astype(BF16)
 
 
@@ -334,19 +332,17 @@
         [pltpu.VMEM((1, 2), jnp.int32), pltpu.VMEM((2 * FINE, C), BF16), pltpu.SemaphoreType.DMA((2,))],
     )(in_hbm(frame_pos), in_hbm(cot))
     following = lax.ppermute(ahead, tm, [(i + 1, i) for i in range(63)])
-    own, s_val, act, turned_own, pooled, pool_near, conv_near, lat_near, gain_near, pos_near = call(
+    own, s_val, act, turned_own, pooled, pool_near, conv_near, lat_near, gain_near, pos_near, w_short_near, spread_near = call(
         own_kernel, "own_kernel",
         [
             shape(8, SEND_ROWS, 128), shape(2 * CELLS, C, dtype=F32), shape(2 * CELLS, C), shape(2, 128, C, dtype=F32),
             shape(2 * CELLS, C, dtype=F32), shape(4 * FINE, 9 * 128), shape(TAPS, C, C),
             shape(2 * CELLS, C_IN), shape(1, C, dtype=F32), shape(1, 2, dtype=jnp.int32),
+            shape(C, C_IN), shape(2 * FINE, 18 * CELLS),
         ],
-        [HBM] * 7,
-        [
-            pltpu.VMEM((C, C_IN), BF16), pltpu.VMEM((2 * FINE, C), BF16), pltpu.VMEM((2, C, 128), F32),
-            pltpu.SemaphoreType.DMA((7,)),
-        ],
-    )(*map(in_hbm, (lat, w_short_t, gain2, cot, frame_pos, pool, w27)))
+        [HBM] * 8,
+        [pltpu.VMEM((2 * FINE, C), BF16), pltpu.VMEM((2, C, 128), F32), pltpu.SemaphoreType.DMA((8,))],
+    )(*map(in_hbm, (lat, w_short_t, gain2, cot, frame_pos, pool, w27, spread)))
     send, ds_flat = call(
         local_kernel, "local_kernel", [shape(8, SEND_ROWS, 128), shape(2 * CELLS, C)],
         [VMEM] * 10, [pltpu.VMEM((2, C, 128), F32)],
@@ -368,21 +364,16 @@
     before = lax.ppermute(lat_late, tm, [(i, i + 1) for i in range(63)])
     decoded, grad_latent = call(
         forward_kernel, "forward_kernel", [shape(2 * FINE, C), shape(2 * CELLS, C_IN)],
-        [VMEM] * 5 + [HBM] * 4,
-        [
-            pltpu.SMEM((1, 2), jnp.int32), pltpu.VMEM((C, C_IN), BF16), pltpu.VMEM((1, C), F32),
-            pltpu.VMEM((2 * FINE, 18 * CELLS), BF16), pltpu.VMEM((9 * 2 * CELLS, C), BF16),
-            pltpu.SemaphoreType.DMA((4,)),
-        ],
-    )(before, s_val, act, ds_flat, conv_near, *map(in_hbm, (frame_pos, w_short_t, gain2, spread)))
-    got = lax.all_to_all(part, ("zl", "y"), 0, 0, axis_index_groups=[[4 * zl + y for zl in ZL_ORDER for y in range(4)]])
+        [VMEM] * 9, [pltpu.VMEM((9 * 2 * CELLS, C), BF16)],
+    )(before, s_val, act, ds_flat, conv_near, pos_near, w_short_near, gain_near, spread_near)
+    got = lax.all_to_all(part, ("zl", "y"), 0, 0, axis_index_groups=[[4 * zl + y for y in range(4) for zl in ZL_ORDER]])
     got = lax.all_gather(got, "c", axis=0, tiled=True)
-    spare = lax.all_gather(spare, "c", axis=0, tiled=True)
+    spare_other = lax.ppermute(spare, "c", [(0, 1), (1, 0)])
     grad_conv, grad_short_t, grad_gain = call(
         assemble_kernel, "assemble_kernel",
         [shape(24, TAPS * C, dtype=F32), shape(C, C_IN, dtype=F32), shape(1, C, dtype=F32)],
-        [VMEM, VMEM], [pltpu.VMEM((1536, 128), F32)],
-    )(got, spare)
+        [VMEM] * 4, [pltpu.VMEM((1536, 128), F32)],
+    )(got, spare, spare_other, lax.axis_index("c").astype(jnp.int32).reshape(1, 1))
     return (
         decoded.reshape(cotangent.shape),
         grad_latent.reshape(latent.shape),

time: 85.8 us -> 85.7 us (level)
  starting transfers between devices: 23.8 us -> 25.7 us
  Pallas kernels: 13.1 us -> 12.1 us
  blocking collectives: 47.6 us -> 46.7 us
    ppermute x0 -> x1, starting transfers between devices: none -> 1.92 us  [on_device(): spare_other = lax.ppermute(spare, 'c', [(0, 1), (1, 0)])]
    all_gather x1 -> x0, blocking collectives: 1.78 us -> none  [on_device(): spare = lax.all_gather(spare, 'c', axis=0, tiled=True)]
    pallas_call x1, Pallas kernels: 2.88 us -> 1.92 us  [on_device(): call(forward_kernel, 'forward_kernel', [shape(2 * FINE, C), shape(2 * CEL...]
    all_gather x1, blocking collectives: 2.37 us -> 3.25 us  [on_device(): got = lax.all_gather(got, 'c', axis=0, tiled=True)]
  transfers between devices with their start and end apart: 3 -> 4, of which waited for: 0 -> 0; matrix products, arithmetic and copies ran while one was open for 0% -> 0% of each run, Pallas kernels for 8% -> 7%
where the time goes in v6:
time: 85.7 us; the launch traced here: 85.3 us
  blocking collectives  46.7 us (54%)
  starting transfers between devices  25.7 us (30%)
  Pallas kernels  12.1 us (14%)
    all_to_all x1, blocking collectives, on_device(): lax.all_to_all(part, ('zh', 'zl'), 0, 0, axis_index_groups=[[(Z_FIRST + i...  22 us
    all_to_all x1, blocking collectives, on_device(): got = lax.all_to_all(send, ('c', 'y'), 0, 0)  11.9 us
    all_to_all x1, blocking collectives, on_device(): got = lax.all_to_all(part, 'x', 0, 0)  9.57 us
    ppermute x1, starting transfers between devices, on_device(): following = lax.ppermute(ahead, tm, [(i + 1, i) for i in range(63)])  8.79 us
    all_to_all x1, starting transfers between devices, on_device(): lax.all_to_all(part, ('zl', 'y'), 0, 0, axis_index_groups=[[4 * zl + y fo...  8.01 us
    ppermute x1, starting transfers between devices, on_device(): before = lax.ppermute(lat_late, tm, [(i, i + 1) for i in range(63)])  7.01 us
    pallas_call x1, Pallas kernels, on_device(): call(own_kernel, 'own_kernel', [shape(8, SEND_ROWS, 128), shape(2 * CELLS...  4.05 us
    all_gather x1, blocking collectives, on_device(): got = lax.all_gather(got, 'c', axis=0, tiled=True)  3.25 us
  transfers between devices with their start and end apart: 4, of which 0 were waited for; matrix products, arithmetic and copies ran while one was open for 0% of the time, Pallas kernels for 7%

profile of v6, /device:TPU:1, one launch (start us, length us, event | category | flops | bytes accessed | tf_op | source)
XLA Modules:
  0.0 85.3 jit_solution(12705636589240251303)
XLA Ops:
  0.6 1.0 %ahead_kernel.1 = bf16[256,192]{1,0:T(8,128)(2,1)S(1)} custom-call(s32[1,2]{1,0:T(1,128)} %pos_hbm.3, bf16[256,192]{1,0:T(8,128)(2,1)} %bitcast.11), custom_call_target="tpu_custom_call" | custom-call | tf_op jit(solution)/shard_map/ahead_kernel/pallas_call | solution.py:330
  1.7 8.8 %collective-permute-start = (bf16[256,192]{1,0:T(8,128)(2,1)S(1)}, bf16[256,192]{1,0:T(8,128)(2,1)S(1)}, u32[]{:S(2)}, u32[]{:S(2)}) collective-permute-start(bf16[256,192]{1,0:T(8,128)(2,1)S(1)} %ahead_kernel.1), channel_id=1, source_target_pairs={{8,0},{16,8},{24,16},{32,24},{40,32},{48,40},{56,48},{64,56},{72,6... | collective-permute-start | bytes 294920 | tf_op jit(solution)/shard_map/ppermute | solution.py:334
  10.5 4.1 %own_kernel.1 = (bf16[8,272,128]{2,1,0:T(8,128)(2,1)S(1)}, f32[64,192]{1,0:T(8,128)S(1)}, bf16[64,192]{1,0:T(8,128)(2,1)S(1)}, f32[2,128,192]{2,1,0:T(8,128)S(1)...) custom-call(bf16[64,384]{1,0:T(8,128)(2,1)} %bitcast.14, ...), custom_call_target="tpu_custom_call" | custom-call | tf_op jit(solution)/shard_map/own_kernel/pallas_call | solution.py:335
  14.5 0.0 collective-permute-done.next_ref
  14.5 2.0 %local_kernel.1 = (bf16[8,272,128]{2,1,0:T(8,128)(2,1)S(1)}, bf16[64,192]{1,0:T(8,128)(2,1)S(1)}) custom-call(bf16[256,192]{1,0:T(8,128)(2,1)S(1)} %collective-permute-done.next_ref, bf16[8,272,128]{2,1,0:T(8,128)(2,1)S(1)} %get-tuple-element.27.sent_ref, f32[64,192]{1,0:T(8,128)S(1)} %get-tuple-element.28.s_ref, ...), custom_call_target="tpu_custom_call" | custom-call | tf_op jit(solution)/shard_map/local_kernel/pallas_call | solution.py:346
  16.5 11.9 %all_to_all.20.got_ref = bf16[8,272,128]{2,1,0:T(8,128)(2,1)S(1)} all-to-all(bf16[8,272,128]{2,1,0:T(8,128)(2,1)S(1)} %get-tuple-element.36), channel_id=1, replica_groups=mesh['zl'=8,'y'=4,'c'=2,'x'=4,'zh'=2] {'c','y'}, dimensions={0} | all-to-all | bytes 1114112 | tf_op jit(solution)/shard_map/all_to_all | solution.py:350
  28.5 1.2 %kernel_grad_kernel.1 = bf16[4,336,128]{2,1,0:T(8,128)(2,1)S(1)} custom-call(bf16[8,272,128]{2,1,0:T(8,128)(2,1)S(1)} %all_to_all.20.got_ref, bf16[512,1152]{1,0:T(8,128)(2,1)S(1)} %get-tuple-element.31.pool_ref), custom_call_target="tpu_custom_call" | custom-call | tf_op jit(solution)/shard_map/kernel_grad_kernel/pallas_call | solution.py:351
  29.7 9.6 %all_to_all.21.got_ref = bf16[4,336,128]{2,1,0:T(8,128)(2,1)S(1)} all-to-all(bf16[4,336,128]{2,1,0:T(8,128)(2,1)S(1)} %kernel_grad_kernel.1), channel_id=1, replica_groups=mesh['zl'=8,'y'=4,'c'=2,'x'=4,'zh'=2] {'x'}, dimensions={0} | all-to-all | bytes 688128 | tf_op jit(solution)/shard_map/all_to_all | solution.py:358
  39.3 0.1 sum_x_kernel.1
  39.3 22.0 %all_to_all.22.got_ref = bf16[16,32,128]{2,1,0:T(8,128)(2,1)S(1)} all-to-all(bf16[16,32,128]{2,1,0:T(8,128)(2,1)S(1)} %sum_x_kernel.1), channel_id=1, replica_groups={{129,193,257,321,385,449,0,64,128,192,256,320,384,448,1,65},{131,195,25..., dimensions={0} | all-to-all | bytes 262144 | tf_op jit(solution)/shard_map/all_to_all | solution.py:360
  61.3 0.7 sum_z_kernel.1
  62.0 8.0 %all-to-all-start.3 = ((bf16[32,24,128]{2,1,0:T(8,128)(2,1)}), bf16[32,24,128]{2,1,0:T(8,128)(2,1)}, u32[]{:S(2)}, u32[]{:S(2)}) async-start(bf16[32,24,128]{2,1,0:T(8,128)(2,1)} %get-tuple-element.44), calls=%async_computation.3 | async-start | bytes 393216 | tf_op jit(solution)/shard_map/all_to_all | solution.py:369
  70.0 7.0 %collective-permute-start.1 = (bf16[64,384]{1,0:T(8,128)(2,1)S(1)}, bf16[64,384]{1,0:T(8,128)(2,1)S(1)}, u32[]{:S(2)}, u32[]{:S(2)}) collective-permute-start(bf16[64,384]{1,0:T(8,128)(2,1)S(1)} %get-tuple-element.37), channel_id=1, source_target_pairs={{0,8},{8,16},{16,24},{24,32},{32,40},{40,48},{48,56},{56,64},{64,7... | collective-permute-start | bytes 147464 | tf_op jit(solution)/shard_map/ppermute | solution.py:364
  77.1 1.9 %collective-permute-start.2 = (bf16[8,128]{1,0:T(8,128)(2,1)S(1)}, bf16[8,128]{1,0:T(8,128)(2,1)S(1)}, u32[]{:S(2)}, u32[]{:S(2)}) collective-permute-start(bf16[8,128]{1,0:T(8,128)(2,1)S(1)} %get-tuple-element.45.spare_ref), channel_id=1, source_target_pairs={{0,8},{8,0},{1,9},{9,1},{2,10},{10,2},{3,11},{11,3},{4,12},{12,4},... | collective-permute-start | bytes 6152 | tf_op jit(solution)/shard_map/ppermute | solution.py:371
  79.0 0.0 collective-permute-done.1.before_ref
  79.0 1.9 %forward_kernel.1 = (bf16[256,192]{1,0:T(8,128)(2,1)}, bf16[64,384]{1,0:T(8,128)(2,1)}) custom-call(bf16[64,384]{1,0:T(8,128)(2,1)S(1)} %collective-permute-done.1.before_ref, f32[64,192]{1,0:T(8,128)S(1)} %get-tuple-element.28.s_ref, bf16[64,192]{1,0:T(8,128)(2,1)S(1)} %get-tuple-element.38.act_ref, bf16[64,192]{1,0:T(8,128)(2,1)S(1)} %get-tuple-element.39.ds_ref, ...), custom_call_target="tpu_custom_call" | custom-call | tf_op jit(solution)/shard_map/forward_kernel/pallas_call | solution.py:365
  80.9 0.0 all-to-all-done.3
  80.9 3.3 %all_gather.3.got_ref = bf16[64,24,128]{2,1,0:T(8,128)(2,1)S(1)} all-gather(bf16[32,24,128]{2,1,0:T(8,128)(2,1)} %all-to-all-done.3), channel_id=1, replica_groups=mesh['zl'=8,'y'=4,'c'=2,'x'=4,'zh'=2] {'c'}, dimensions={0}, use_global_device_ids=true | all-gather | bytes 589824 | tf_op jit(solution)/shard_map/all_gather | solution.py:370
  84.2 0.0 collective-permute-done.2.other_ref
  84.2 1.2 %assemble_kernel.1 = (f32[24,5184]{1,0:T(8,128)}, f32[192,384]{1,0:T(8,128)}, f32[1,192]{1,0:T(1,128)}) custom-call(bf16[64,24,128]{2,1,0:T(8,128)(2,1)S(1)} %all_gather.3.got_ref, bf16[8,128]{1,0:T(8,128)(2,1)S(1)} %get-tuple-element.45.spare_ref, bf16[8,128]{1,0:T(8,128)(2,1)S(1)} %collective-permute-done.2.other_ref, s32[1,1]{1,0:T(1,128)} %bitcast.7.core_ref), custom_call_target="tpu_custom_call" | custom-call | tf_op jit(solution)/shard_map/assemble_kernel/pallas_call | solution.py:372
Async XLA Ops:
  1.7 12.9 %collective-permute-start = (bf16[256,192]{1,0:T(8,128)(2,1)S(1)}, bf16[256,192]{1,0:T(8,128)(2,1)S(1)}, u32[]{:S(2)}, u32[]{:S(2)}) collective-permute-start(bf16[256,192]{1,0:T(8,128)(2,1)S(1)} %ahead_kernel.1), channel_id=1, source_target_pairs={{8,0},{16,8},{24,16},{32,24},{40,32},{48,40},{56,48},{64,56},{72,6... | collective-permute-start | bytes 294920 | tf_op jit(solution)/shard_map/ppermute | solution.py:334
  62.0 18.9 %all-to-all-start.3 = ((bf16[32,24,128]{2,1,0:T(8,128)(2,1)}), bf16[32,24,128]{2,1,0:T(8,128)(2,1)}, u32[]{:S(2)}, u32[]{:S(2)}) async-start(bf16[32,24,128]{2,1,0:T(8,128)(2,1)} %get-tuple-element.44), calls=%async_computation.3 | async-start | bytes 393216 | tf_op jit(solution)/shard_map/all_to_all | solution.py:369
  70.0 9.0 %collective-permute-start.1 = (bf16[64,384]{1,0:T(8,128)(2,1)S(1)}, bf16[64,384]{1,0:T(8,128)(2,1)S(1)}, u32[]{:S(2)}, u32[]{:S(2)}) collective-permute-start(bf16[64,384]{1,0:T(8,128)(2,1)S(1)} %get-tuple-element.37), channel_id=1, source_target_pairs={{0,8},{8,16},{16,24},{24,32},{32,40},{40,48},{48,56},{56,64},{64,7... | collective-permute-start | bytes 147464 | tf_op jit(solution)/shard_map/ppermute | solution.py:364
  77.1 7.1 %collective-permute-start.2 = (bf16[8,128]{1,0:T(8,128)(2,1)S(1)}, bf16[8,128]{1,0:T(8,128)(2,1)S(1)}, u32[]{:S(2)}, u32[]{:S(2)}) collective-permute-start(bf16[8,128]{1,0:T(8,128)(2,1)S(1)} %get-tuple-element.45.spare_ref), channel_id=1, source_target_pairs={{0,8},{8,0},{1,9},{9,1},{2,10},{10,2},{3,11},{11,3},{4,12},{12,4},... | collective-permute-start | bytes 6152 | tf_op jit(solution)/shard_map/ppermute | solution.py:371

commit v7 on v6

--- a/solution.py
+++ b/solution.py
@@ -95,7 +95,7 @@
     loads[3].wait()
     fine_t = jnp.transpose(cot_ref[...].astype(F32))
     for t in range(2):
-        turned_ref[t] = fine_t[:, 128 * t : 128 * t + 128]
+        turned_ref[t, :C] = fine_t[:, 128 * t : 128 * t + 128]
     for load in loads[:3]:
         load.wait()
     s_val, act = features(lat_ref[...], w_short_ref[...], gain_ref[...])
@@ -130,7 +130,7 @@
 ):
     fine_t = jnp.transpose(next_ref[...].astype(F32))
     for t in range(2):
-        turned_ref[t] = fine_t[:, 128 * t : 128 * t + 128]
+        turned_ref[t, :C] = fine_t[:, 128 * t : 128 * t + 128]
     for j in range(8):
         send_ref[j, :48] = sent_ref[j, :48]
         send_ref[j, 48:96] = slices_for(turned_ref, (0, 1), j)
@@ -341,18 +341,18 @@
             shape(C, C_IN), shape(2 * FINE, 18 * CELLS),
         ],
         [HBM] * 8,
-        [pltpu.VMEM((2 * FINE, C), BF16), pltpu.VMEM((2, C, 128), F32), pltpu.SemaphoreType.DMA((8,))],
+        [pltpu.VMEM((2 * FINE, C), BF16), pltpu.VMEM((2, C + 24, 128), F32), pltpu.SemaphoreType.DMA((8,))],
     )(*map(in_hbm, (lat, w_short_t, gain2, cot, frame_pos, pool, w27, spread)))
     send, ds_flat = call(
         local_kernel, "local_kernel", [shape(8, SEND_ROWS, 128), shape(2 * CELLS, C)],
-        [VMEM] * 10, [pltpu.VMEM((2, C, 128), F32)],
+        [VMEM] * 10, [pltpu.VMEM((2, C + 24, 128), F32)],
     )(following, own, s_val, turned_own, pooled, pool_near, conv_near, lat_near, gain_near, pos_near)
     got = lax.all_to_all(send, ("c", "y"), 0, 0)
     part = call(
         kernel_grad_kernel, "kernel_grad_kernel", shape(4, MSG, 128), [VMEM, VMEM],
         [
             pltpu.VMEM((120, 1024), F32), pltpu.VMEM((96, 1024), F32),
-            pltpu.VMEM((6, 1024, 256), BF16), pltpu.VMEM((1024, 128), F32),
+            pltpu.VMEM((6, 1024, 256), BF16), pltpu.VMEM((1152, 128), F32),
         ],
     )(got, pool_near)
     got = lax.all_to_all(part, "x", 0, 0)
@@ -372,7 +372,7 @@
     grad_conv, grad_short_t, grad_gain = call(
         assemble_kernel, "assemble_kernel",
         [shape(24, TAPS * C, dtype=F32), shape(C, C_IN, dtype=F32), shape(1, C, dtype=F32)],
-        [VMEM] * 4, [pltpu.VMEM((1536, 128), F32)],
+        [VMEM] * 4, [pltpu.VMEM((1664, 128), F32)],
     )(got, spare, spare_other, lax.axis_index("c").astype(jnp.int32).reshape(1, 1))
     return (
         decoded.reshape(cotangent.shape),

time: 85.7 us -> 85.7 us (level)
  no operation moved by 1% of the time
where the time goes in v7:
time: 85.7 us; the launch traced here: 85.3 us
  blocking collectives  46.7 us (54%)
  starting transfers between devices  25.7 us (30%)
  Pallas kernels  12.1 us (14%)
    all_to_all x1, blocking collectives, on_device(): lax.all_to_all(part, ('zh', 'zl'), 0, 0, axis_index_groups=[[(Z_FIRST + i...  22 us
    all_to_all x1, blocking collectives, on_device(): got = lax.all_to_all(send, ('c', 'y'), 0, 0)  11.9 us
    all_to_all x1, blocking collectives, on_device(): got = lax.all_to_all(part, 'x', 0, 0)  9.57 us
    ppermute x1, starting transfers between devices, on_device(): following = lax.ppermute(ahead, tm, [(i + 1, i) for i in range(63)])  8.79 us
    all_to_all x1, starting transfers between devices, on_device(): lax.all_to_all(part, ('zl', 'y'), 0, 0, axis_index_groups=[[4 * zl + y fo...  8.01 us
    ppermute x1, starting transfers between devices, on_device(): before = lax.ppermute(lat_late, tm, [(i, i + 1) for i in range(63)])  7.01 us
    pallas_call x1, Pallas kernels, on_device(): call(own_kernel, 'own_kernel', [shape(8, SEND_ROWS, 128), shape(2 * CELLS...  4.05 us
    all_gather x1, blocking collectives, on_device(): got = lax.all_gather(got, 'c', axis=0, tiled=True)  3.25 us
  transfers between devices with their start and end apart: 4, of which 0 were waited for; matrix products, arithmetic and copies ran while one was open for 0% of the time, Pallas kernels for 7%

profile of v7, /device:TPU:1, one launch (start us, length us, event | category | flops | bytes accessed | tf_op | source)
XLA Modules:
  0.0 85.3 jit_solution(12447999961073900530)
XLA Ops:
  0.6 1.0 %ahead_kernel.1 = bf16[256,192]{1,0:T(8,128)(2,1)S(1)} custom-call(s32[1,2]{1,0:T(1,128)} %pos_hbm.3, bf16[256,192]{1,0:T(8,128)(2,1)} %bitcast.11), custom_call_target="tpu_custom_call" | custom-call | tf_op jit(solution)/shard_map/ahead_kernel/pallas_call | solution.py:330
  1.7 8.8 %collective-permute-start = (bf16[256,192]{1,0:T(8,128)(2,1)S(1)}, bf16[256,192]{1,0:T(8,128)(2,1)S(1)}, u32[]{:S(2)}, u32[]{:S(2)}) collective-permute-start(bf16[256,192]{1,0:T(8,128)(2,1)S(1)} %ahead_kernel.1), channel_id=1, source_target_pairs={{8,0},{16,8},{24,16},{32,24},{40,32},{48,40},{56,48},{64,56},{72,6... | collective-permute-start | bytes 294920 | tf_op jit(solution)/shard_map/ppermute | solution.py:334
  10.5 4.1 %own_kernel.1 = (bf16[8,272,128]{2,1,0:T(8,128)(2,1)S(1)}, f32[64,192]{1,0:T(8,128)S(1)}, bf16[64,192]{1,0:T(8,128)(2,1)S(1)}, f32[2,128,192]{2,1,0:T(8,128)S(1)...) custom-call(bf16[64,384]{1,0:T(8,128)(2,1)} %bitcast.14, ...), custom_call_target="tpu_custom_call" | custom-call | tf_op jit(solution)/shard_map/own_kernel/pallas_call | solution.py:335
  14.5 0.0 collective-permute-done.next_ref
  14.5 2.0 %local_kernel.1 = (bf16[8,272,128]{2,1,0:T(8,128)(2,1)S(1)}, bf16[64,192]{1,0:T(8,128)(2,1)S(1)}) custom-call(bf16[256,192]{1,0:T(8,128)(2,1)S(1)} %collective-permute-done.next_ref, bf16[8,272,128]{2,1,0:T(8,128)(2,1)S(1)} %get-tuple-element.27.sent_ref, f32[64,192]{1,0:T(8,128)S(1)} %get-tuple-element.28.s_ref, ...), custom_call_target="tpu_custom_call" | custom-call | tf_op jit(solution)/shard_map/local_kernel/pallas_call | solution.py:346
  16.5 11.9 %all_to_all.20.got_ref = bf16[8,272,128]{2,1,0:T(8,128)(2,1)S(1)} all-to-all(bf16[8,272,128]{2,1,0:T(8,128)(2,1)S(1)} %get-tuple-element.36), channel_id=1, replica_groups=mesh['zl'=8,'y'=4,'c'=2,'x'=4,'zh'=2] {'c','y'}, dimensions={0} | all-to-all | bytes 1114112 | tf_op jit(solution)/shard_map/all_to_all | solution.py:350
  28.5 1.2 %kernel_grad_kernel.1 = bf16[4,336,128]{2,1,0:T(8,128)(2,1)S(1)} custom-call(bf16[8,272,128]{2,1,0:T(8,128)(2,1)S(1)} %all_to_all.20.got_ref, bf16[512,1152]{1,0:T(8,128)(2,1)S(1)} %get-tuple-element.31.pool_ref), custom_call_target="tpu_custom_call" | custom-call | tf_op jit(solution)/shard_map/kernel_grad_kernel/pallas_call | solution.py:351
  29.7 9.6 %all_to_all.21.got_ref = bf16[4,336,128]{2,1,0:T(8,128)(2,1)S(1)} all-to-all(bf16[4,336,128]{2,1,0:T(8,128)(2,1)S(1)} %kernel_grad_kernel.1), channel_id=1, replica_groups=mesh['zl'=8,'y'=4,'c'=2,'x'=4,'zh'=2] {'x'}, dimensions={0} | all-to-all | bytes 688128 | tf_op jit(solution)/shard_map/all_to_all | solution.py:358
  39.3 0.1 sum_x_kernel.1
  39.3 22.0 %all_to_all.22.got_ref = bf16[16,32,128]{2,1,0:T(8,128)(2,1)S(1)} all-to-all(bf16[16,32,128]{2,1,0:T(8,128)(2,1)S(1)} %sum_x_kernel.1), channel_id=1, replica_groups={{129,193,257,321,385,449,0,64,128,192,256,320,384,448,1,65},{131,195,25..., dimensions={0} | all-to-all | bytes 262144 | tf_op jit(solution)/shard_map/all_to_all | solution.py:360
  61.3 0.7 sum_z_kernel.1
  62.0 8.0 %all-to-all-start.3 = ((bf16[32,24,128]{2,1,0:T(8,128)(2,1)}), bf16[32,24,128]{2,1,0:T(8,128)(2,1)}, u32[]{:S(2)}, u32[]{:S(2)}) async-start(bf16[32,24,128]{2,1,0:T(8,128)(2,1)} %get-tuple-element.44), calls=%async_computation.3 | async-start | bytes 393216 | tf_op jit(solution)/shard_map/all_to_all | solution.py:369
  70.0 7.0 %collective-permute-start.1 = (bf16[64,384]{1,0:T(8,128)(2,1)S(1)}, bf16[64,384]{1,0:T(8,128)(2,1)S(1)}, u32[]{:S(2)}, u32[]{:S(2)}) collective-permute-start(bf16[64,384]{1,0:T(8,128)(2,1)S(1)} %get-tuple-element.37), channel_id=1, source_target_pairs={{0,8},{8,16},{16,24},{24,32},{32,40},{40,48},{48,56},{56,64},{64,7... | collective-permute-start | bytes 147464 | tf_op jit(solution)/shard_map/ppermute | solution.py:364
  77.1 1.9 %collective-permute-start.2 = (bf16[8,128]{1,0:T(8,128)(2,1)S(1)}, bf16[8,128]{1,0:T(8,128)(2,1)S(1)}, u32[]{:S(2)}, u32[]{:S(2)}) collective-permute-start(bf16[8,128]{1,0:T(8,128)(2,1)S(1)} %get-tuple-element.45.spare_ref), channel_id=1, source_target_pairs={{0,8},{8,0},{1,9},{9,1},{2,10},{10,2},{3,11},{11,3},{4,12},{12,4},... | collective-permute-start | bytes 6152 | tf_op jit(solution)/shard_map/ppermute | solution.py:371
  79.0 0.0 collective-permute-done.1.before_ref
  79.0 1.9 %forward_kernel.1 = (bf16[256,192]{1,0:T(8,128)(2,1)}, bf16[64,384]{1,0:T(8,128)(2,1)}) custom-call(bf16[64,384]{1,0:T(8,128)(2,1)S(1)} %collective-permute-done.1.before_ref, f32[64,192]{1,0:T(8,128)S(1)} %get-tuple-element.28.s_ref, bf16[64,192]{1,0:T(8,128)(2,1)S(1)} %get-tuple-element.38.act_ref, bf16[64,192]{1,0:T(8,128)(2,1)S(1)} %get-tuple-element.39.ds_ref, ...), custom_call_target="tpu_custom_call" | custom-call | tf_op jit(solution)/shard_map/forward_kernel/pallas_call | solution.py:365
  80.9 0.0 all-to-all-done.3
  80.9 3.3 %all_gather.3.got_ref = bf16[64,24,128]{2,1,0:T(8,128)(2,1)S(1)} all-gather(bf16[32,24,128]{2,1,0:T(8,128)(2,1)} %all-to-all-done.3), channel_id=1, replica_groups=mesh['zl'=8,'y'=4,'c'=2,'x'=4,'zh'=2] {'c'}, dimensions={0}, use_global_device_ids=true | all-gather | bytes 589824 | tf_op jit(solution)/shard_map/all_gather | solution.py:370
  84.2 0.0 collective-permute-done.2.other_ref
  84.2 1.2 %assemble_kernel.1 = (f32[24,5184]{1,0:T(8,128)}, f32[192,384]{1,0:T(8,128)}, f32[1,192]{1,0:T(1,128)}) custom-call(bf16[64,24,128]{2,1,0:T(8,128)(2,1)S(1)} %all_gather.3.got_ref, bf16[8,128]{1,0:T(8,128)(2,1)S(1)} %get-tuple-element.45.spare_ref, bf16[8,128]{1,0:T(8,128)(2,1)S(1)} %collective-permute-done.2.other_ref, s32[1,1]{1,0:T(1,128)} %bitcast.7.core_ref), custom_call_target="tpu_custom_call" | custom-call | tf_op jit(solution)/shard_map/assemble_kernel/pallas_call | solution.py:372
Async XLA Ops:
  1.7 12.9 %collective-permute-start = (bf16[256,192]{1,0:T(8,128)(2,1)S(1)}, bf16[256,192]{1,0:T(8,128)(2,1)S(1)}, u32[]{:S(2)}, u32[]{:S(2)}) collective-permute-start(bf16[256,192]{1,0:T(8,128)(2,1)S(1)} %ahead_kernel.1), channel_id=1, source_target_pairs={{8,0},{16,8},{24,16},{32,24},{40,32},{48,40},{56,48},{64,56},{72,6... | collective-permute-start | bytes 294920 | tf_op jit(solution)/shard_map/ppermute | solution.py:334
  62.0 18.9 %all-to-all-start.3 = ((bf16[32,24,128]{2,1,0:T(8,128)(2,1)}), bf16[32,24,128]{2,1,0:T(8,128)(2,1)}, u32[]{:S(2)}, u32[]{:S(2)}) async-start(bf16[32,24,128]{2,1,0:T(8,128)(2,1)} %get-tuple-element.44), calls=%async_computation.3 | async-start | bytes 393216 | tf_op jit(solution)/shard_map/all_to_all | solution.py:369
  70.0 9.0 %collective-permute-start.1 = (bf16[64,384]{1,0:T(8,128)(2,1)S(1)}, bf16[64,384]{1,0:T(8,128)(2,1)S(1)}, u32[]{:S(2)}, u32[]{:S(2)}) collective-permute-start(bf16[64,384]{1,0:T(8,128)(2,1)S(1)} %get-tuple-element.37), channel_id=1, source_target_pairs={{0,8},{8,16},{16,24},{24,32},{32,40},{40,48},{48,56},{56,64},{64,7... | collective-permute-start | bytes 147464 | tf_op jit(solution)/shard_map/ppermute | solution.py:364
  77.1 7.1 %collective-permute-start.2 = (bf16[8,128]{1,0:T(8,128)(2,1)S(1)}, bf16[8,128]{1,0:T(8,128)(2,1)S(1)}, u32[]{:S(2)}, u32[]{:S(2)}) collective-permute-start(bf16[8,128]{1,0:T(8,128)(2,1)S(1)} %get-tuple-element.45.spare_ref), channel_id=1, source_target_pairs={{0,8},{8,0},{1,9},{9,1},{2,10},{10,2},{3,11},{11,3},{4,12},{12,4},... | collective-permute-start | bytes 6152 | tf_op jit(solution)/shard_map/ppermute | solution.py:371

commit v8 on v7

--- a/solution.py
+++ b/solution.py
@@ -76,6 +76,14 @@
     for t in range(2):
         rows = slice(FINE * t, FINE * t + FINE)
         ahead_ref[rows] = (cot_ref[rows].astype(F32) * keep[t]).astype(BF16)
+
+
+def pooled_parts(fine_t, pool_ref, rows):
+    parts = []
+    for start in range(0, 9 * 128, 256):
+        wide = dot(fine_t, pool_ref[rows, start : min(start + 256, 9 * 128)])
+        parts += [wide[:, i : i + 128] for i in range(0, wide.shape[1], 128)]
+    return parts
 
 
 def two_taps(w_conv_ref, k, ab):
@@ -112,8 +120,7 @@
     loads[4].wait()
     loads[5].wait()
     acc = None
-    for ab in range(9):
-        part = dot(fine_t, pool_ref[: 2 * FINE, ab * 128 : (ab + 1) * 128])
+    for ab, part in enumerate(pooled_parts(fine_t, pool_ref, slice(0, 2 * FINE))):
         if ab == 4:
             pooled_ref[...] = jnp.transpose(part)[: 2 * CELLS]
         value = dot(two_taps(w_conv_ref, 1, ab), part.astype(BF16))
@@ -138,8 +145,7 @@
 
     fine_t = fine_t.astype(BF16)
     acc = None
-    for ab in range(9):
-        part = dot(fine_t, pool_ref[2 * FINE :, ab * 128 : (ab + 1) * 128])
+    for ab, part in enumerate(pooled_parts(fine_t, pool_ref, slice(2 * FINE, 4 * FINE))):
         value = dot(two_taps(w_conv_ref, 0, ab), part.astype(BF16))
         acc = value if acc is None else acc + value
     after = [jnp.transpose(acc[C * i : C * i + C]) for i in range(2)]
@@ -190,8 +196,7 @@
             rhs_ref[2 * k, 128 * p : 128 * p + 128] = jnp.concatenate([value, gap], axis=1).astype(BF16)
             rhs_ref[2 * k + 1, 128 * p : 128 * p + 128] = jnp.concatenate([gap, value], axis=1).astype(BF16)
     fine_t = jnp.concatenate(peers, axis=0).astype(BF16)
-    for ab in range(9):
-        part = dot(fine_t, pool_ref[:, ab * 128 : (ab + 1) * 128])
+    for ab, part in enumerate(pooled_parts(fine_t, pool_ref, slice(0, 4 * FINE))):
         wide = jnp.concatenate([part[24 * p : 24 * p + 24] for p in range(8)], axis=1)
         target = odd_ref if ab % 2 else even_ref
         target[24 * (ab // 2) : 24 * (ab // 2) + 24] = wide

time: 85.7 us -> 84.9 us (level)
  Pallas kernels: 12.1 us -> 10.6 us
  transfers between devices with their start and end apart: 4 -> 4, of which waited for: 0 -> 0; matrix products, arithmetic and copies ran while one was open for 0% -> 0% of each run, Pallas kernels for 7% -> 6%
where the time goes in v8:
time: 84.9 us; the launch traced here: 84.5 us
  blocking collectives  47.5 us (56%)
  starting transfers between devices  25.7 us (30%)
  Pallas kernels  10.6 us (12%)
    all_to_all x1, blocking collectives, on_device(): lax.all_to_all(part, ('zh', 'zl'), 0, 0, axis_index_groups=[[(Z_FIRST + i...  22 us
    all_to_all x1, blocking collectives, on_device(): got = lax.all_to_all(send, ('c', 'y'), 0, 0)  11.9 us
    all_to_all x1, blocking collectives, on_device(): got = lax.all_to_all(part, 'x', 0, 0)  10.3 us
    ppermute x1, starting transfers between devices, on_device(): following = lax.ppermute(ahead, tm, [(i + 1, i) for i in range(63)])  8.79 us
    all_to_all x1, starting transfers between devices, on_device(): lax.all_to_all(part, ('zl', 'y'), 0, 0, axis_index_groups=[[4 * zl + y fo...  8.01 us
    ppermute x1, starting transfers between devices, on_device(): before = lax.ppermute(lat_late, tm, [(i, i + 1) for i in range(63)])  7.01 us
    pallas_call x1, Pallas kernels, on_device(): call(own_kernel, 'own_kernel', [shape(8, SEND_ROWS, 128), shape(2 * CELLS...  3.34 us
    all_gather x1, blocking collectives, on_device(): got = lax.all_gather(got, 'c', axis=0, tiled=True)  3.26 us
  transfers between devices with their start and end apart: 4, of which 0 were waited for; matrix products, arithmetic and copies ran while one was open for 0% of the time, Pallas kernels for 6%

profile of v8, /device:TPU:1, one launch (start us, length us, event | category | flops | bytes accessed | tf_op | source)
XLA Modules:
  0.0 84.5 jit_solution(16083792764311260598)
XLA Ops:
  0.6 1.0 %ahead_kernel.1 = bf16[256,192]{1,0:T(8,128)(2,1)S(1)} custom-call(s32[1,2]{1,0:T(1,128)} %pos_hbm.3, bf16[256,192]{1,0:T(8,128)(2,1)} %bitcast.11), custom_call_target="tpu_custom_call" | custom-call | tf_op jit(solution)/shard_map/ahead_kernel/pallas_call | solution.py:335
  1.7 8.8 %collective-permute-start = (bf16[256,192]{1,0:T(8,128)(2,1)S(1)}, bf16[256,192]{1,0:T(8,128)(2,1)S(1)}, u32[]{:S(2)}, u32[]{:S(2)}) collective-permute-start(bf16[256,192]{1,0:T(8,128)(2,1)S(1)} %ahead_kernel.1), channel_id=1, source_target_pairs={{8,0},{16,8},{24,16},{32,24},{40,32},{48,40},{56,48},{64,56},{72,6... | collective-permute-start | bytes 294920 | tf_op jit(solution)/shard_map/ppermute | solution.py:339
  10.5 3.3 %own_kernel.1 = (bf16[8,272,128]{2,1,0:T(8,128)(2,1)S(1)}, f32[64,192]{1,0:T(8,128)S(1)}, bf16[64,192]{1,0:T(8,128)(2,1)S(1)}, f32[2,128,192]{2,1,0:T(8,128)S(1)...) custom-call(bf16[64,384]{1,0:T(8,128)(2,1)} %bitcast.14, ...), custom_call_target="tpu_custom_call" | custom-call | tf_op jit(solution)/shard_map/own_kernel/pallas_call | solution.py:340
  13.8 0.0 collective-permute-done.next_ref
  13.8 1.3 %local_kernel.1 = (bf16[8,272,128]{2,1,0:T(8,128)(2,1)S(1)}, bf16[64,192]{1,0:T(8,128)(2,1)S(1)}) custom-call(bf16[256,192]{1,0:T(8,128)(2,1)S(1)} %collective-permute-done.next_ref, bf16[8,272,128]{2,1,0:T(8,128)(2,1)S(1)} %get-tuple-element.27.sent_ref, f32[64,192]{1,0:T(8,128)S(1)} %get-tuple-element.28.s_ref, ...), custom_call_target="tpu_custom_call" | custom-call | tf_op jit(solution)/shard_map/local_kernel/pallas_call | solution.py:351
  15.2 11.9 %all_to_all.20.got_ref = bf16[8,272,128]{2,1,0:T(8,128)(2,1)S(1)} all-to-all(bf16[8,272,128]{2,1,0:T(8,128)(2,1)S(1)} %get-tuple-element.36), channel_id=1, replica_groups=mesh['zl'=8,'y'=4,'c'=2,'x'=4,'zh'=2] {'c','y'}, dimensions={0} | all-to-all | bytes 1114112 | tf_op jit(solution)/shard_map/all_to_all | solution.py:355
  27.1 1.0 %kernel_grad_kernel.1 = bf16[4,336,128]{2,1,0:T(8,128)(2,1)S(1)} custom-call(bf16[8,272,128]{2,1,0:T(8,128)(2,1)S(1)} %all_to_all.20.got_ref, bf16[512,1152]{1,0:T(8,128)(2,1)S(1)} %get-tuple-element.31.pool_ref), custom_call_target="tpu_custom_call" | custom-call | tf_op jit(solution)/shard_map/kernel_grad_kernel/pallas_call | solution.py:356
  28.1 10.3 %all_to_all.21.got_ref = bf16[4,336,128]{2,1,0:T(8,128)(2,1)S(1)} all-to-all(bf16[4,336,128]{2,1,0:T(8,128)(2,1)S(1)} %kernel_grad_kernel.1), channel_id=1, replica_groups=mesh['zl'=8,'y'=4,'c'=2,'x'=4,'zh'=2] {'x'}, dimensions={0} | all-to-all | bytes 688128 | tf_op jit(solution)/shard_map/all_to_all | solution.py:363
  38.4 0.1 sum_x_kernel.1
  38.5 22.0 %all_to_all.22.got_ref = bf16[16,32,128]{2,1,0:T(8,128)(2,1)S(1)} all-to-all(bf16[16,32,128]{2,1,0:T(8,128)(2,1)S(1)} %sum_x_kernel.1), channel_id=1, replica_groups={{129,193,257,321,385,449,0,64,128,192,256,320,384,448,1,65},{131,195,25..., dimensions={0} | all-to-all | bytes 262144 | tf_op jit(solution)/shard_map/all_to_all | solution.py:365
  60.5 0.7 sum_z_kernel.1
  61.2 8.0 %all-to-all-start.3 = ((bf16[32,24,128]{2,1,0:T(8,128)(2,1)}), bf16[32,24,128]{2,1,0:T(8,128)(2,1)}, u32[]{:S(2)}, u32[]{:S(2)}) async-start(bf16[32,24,128]{2,1,0:T(8,128)(2,1)} %get-tuple-element.44), calls=%async_computation.3 | async-start | bytes 393216 | tf_op jit(solution)/shard_map/all_to_all | solution.py:374
  69.2 7.0 %collective-permute-start.1 = (bf16[64,384]{1,0:T(8,128)(2,1)S(1)}, bf16[64,384]{1,0:T(8,128)(2,1)S(1)}, u32[]{:S(2)}, u32[]{:S(2)}) collective-permute-start(bf16[64,384]{1,0:T(8,128)(2,1)S(1)} %get-tuple-element.37), channel_id=1, source_target_pairs={{0,8},{8,16},{16,24},{24,32},{32,40},{40,48},{48,56},{56,64},{64,7... | collective-permute-start | bytes 147464 | tf_op jit(solution)/shard_map/ppermute | solution.py:369
  76.2 1.9 %collective-permute-start.2 = (bf16[8,128]{1,0:T(8,128)(2,1)S(1)}, bf16[8,128]{1,0:T(8,128)(2,1)S(1)}, u32[]{:S(2)}, u32[]{:S(2)}) collective-permute-start(bf16[8,128]{1,0:T(8,128)(2,1)S(1)} %get-tuple-element.45.spare_ref), channel_id=1, source_target_pairs={{0,8},{8,0},{1,9},{9,1},{2,10},{10,2},{3,11},{11,3},{4,12},{12,4},... | collective-permute-start | bytes 6152 | tf_op jit(solution)/shard_map/ppermute | solution.py:376
  78.1 0.0 collective-permute-done.1.before_ref
  78.2 1.9 %forward_kernel.1 = (bf16[256,192]{1,0:T(8,128)(2,1)}, bf16[64,384]{1,0:T(8,128)(2,1)}) custom-call(bf16[64,384]{1,0:T(8,128)(2,1)S(1)} %collective-permute-done.1.before_ref, f32[64,192]{1,0:T(8,128)S(1)} %get-tuple-element.28.s_ref, bf16[64,192]{1,0:T(8,128)(2,1)S(1)} %get-tuple-element.38.act_ref, bf16[64,192]{1,0:T(8,128)(2,1)S(1)} %get-tuple-element.39.ds_ref, ...), custom_call_target="tpu_custom_call" | custom-call | tf_op jit(solution)/shard_map/forward_kernel/pallas_call | solution.py:370
  80.1 0.0 all-to-all-done.3
  80.1 3.3 %all_gather.3.got_ref = bf16[64,24,128]{2,1,0:T(8,128)(2,1)S(1)} all-gather(bf16[32,24,128]{2,1,0:T(8,128)(2,1)} %all-to-all-done.3), channel_id=1, replica_groups=mesh['zl'=8,'y'=4,'c'=2,'x'=4,'zh'=2] {'c'}, dimensions={0}, use_global_device_ids=true | all-gather | bytes 589824 | tf_op jit(solution)/shard_map/all_gather | solution.py:375
  83.3 0.0 collective-permute-done.2.other_ref
  83.3 1.2 %assemble_kernel.1 = (f32[24,5184]{1,0:T(8,128)}, f32[192,384]{1,0:T(8,128)}, f32[1,192]{1,0:T(1,128)}) custom-call(bf16[64,24,128]{2,1,0:T(8,128)(2,1)S(1)} %all_gather.3.got_ref, bf16[8,128]{1,0:T(8,128)(2,1)S(1)} %get-tuple-element.45.spare_ref, bf16[8,128]{1,0:T(8,128)(2,1)S(1)} %collective-permute-done.2.other_ref, s32[1,1]{1,0:T(1,128)} %bitcast.7.core_ref), custom_call_target="tpu_custom_call" | custom-call | tf_op jit(solution)/shard_map/assemble_kernel/pallas_call | solution.py:377
Async XLA Ops:
  1.7 12.1 %collective-permute-start = (bf16[256,192]{1,0:T(8,128)(2,1)S(1)}, bf16[256,192]{1,0:T(8,128)(2,1)S(1)}, u32[]{:S(2)}, u32[]{:S(2)}) collective-permute-start(bf16[256,192]{1,0:T(8,128)(2,1)S(1)} %ahead_kernel.1), channel_id=1, source_target_pairs={{8,0},{16,8},{24,16},{32,24},{40,32},{48,40},{56,48},{64,56},{72,6... | collective-permute-start | bytes 294920 | tf_op jit(solution)/shard_map/ppermute | solution.py:339
  61.2 18.9 %all-to-all-start.3 = ((bf16[32,24,128]{2,1,0:T(8,128)(2,1)}), bf16[32,24,128]{2,1,0:T(8,128)(2,1)}, u32[]{:S(2)}, u32[]{:S(2)}) async-start(bf16[32,24,128]{2,1,0:T(8,128)(2,1)} %get-tuple-element.44), calls=%async_computation.3 | async-start | bytes 393216 | tf_op jit(solution)/shard_map/all_to_all | solution.py:374
  69.2 9.0 %collective-permute-start.1 = (bf16[64,384]{1,0:T(8,128)(2,1)S(1)}, bf16[64,384]{1,0:T(8,128)(2,1)S(1)}, u32[]{:S(2)}, u32[]{:S(2)}) collective-permute-start(bf16[64,384]{1,0:T(8,128)(2,1)S(1)} %get-tuple-element.37), channel_id=1, source_target_pairs={{0,8},{8,16},{16,24},{24,32},{32,40},{40,48},{48,56},{56,64},{64,7... | collective-permute-start | bytes 147464 | tf_op jit(solution)/shard_map/ppermute | solution.py:369
  76.2 7.1 %collective-permute-start.2 = (bf16[8,128]{1,0:T(8,128)(2,1)S(1)}, bf16[8,128]{1,0:T(8,128)(2,1)S(1)}, u32[]{:S(2)}, u32[]{:S(2)}) collective-permute-start(bf16[8,128]{1,0:T(8,128)(2,1)S(1)} %get-tuple-element.45.spare_ref), channel_id=1, source_target_pairs={{0,8},{8,0},{1,9},{9,1},{2,10},{10,2},{3,11},{11,3},{4,12},{12,4},... | collective-permute-start | bytes 6152 | tf_op jit(solution)/shard_map/ppermute | solution.py:376
